TPU v7x, 32 devices: a whole 2x2x4 slice. The times are simulated.
32 devices in a mesh: blk: 8 (over z, x), dp: 4 (over y, core).
Axes of the slice: x: 2, y: 2, z: 4, core: 2. Of those that a mesh axis runs over, the one named last changes fastest.
Arguments:
- layer_input: bfloat16 [4, 1024, 1024], P('dp', 'blk'), may hold values from -6 to 6
- memory: bfloat16 [4, 512, 1024], P('dp', 'blk'), may hold values from -6 to 6
- cotangent: bfloat16 [4, 1024, 1024], P('dp', 'blk'), may hold values from -6 to 6
- block_order: int32 [8], replicated, may hold values from 0 to 7, each once
- w_query: float32 [1024, 1024], P(('blk', 'dp')), may hold values from -0.1875 to 0.1875
- w_key: float32 [1024, 1024], P(('blk', 'dp')), may hold values from -0.1875 to 0.1875
- w_value: float32 [1024, 1024], P(('blk', 'dp')), may hold values from -0.1875 to 0.1875
- w_output: float32 [1024, 1024], P(('blk', 'dp')), may hold values from -1.5 to 1.5
- w_in: float32 [1024, 4096], P(('blk', 'dp')), may hold values from -0.1875 to 0.1875
- w_out: float32 [4096, 1024], P(('blk', 'dp')), may hold values from -0.09375 to 0.09375
- vectors: float32 [8, 1024], P(None, ('blk', 'dp')), may hold values from -2 to 2, as said below
- b_in: float32 [4096], P(('blk', 'dp')), may hold values from -3 to 3
Outputs:
- layer_out: bfloat16 [4, 1024, 1024], P('dp', 'blk')
- input_grad: float32 [4, 1024, 1024], P('dp', 'blk')
- grad_query: float32 [1024, 1024], P(('blk', 'dp'))
- grad_key: float32 [1024, 1024], P(('blk', 'dp'))
- grad_value: float32 [1024, 1024], P(('blk', 'dp'))
- grad_output: float32 [1024, 1024], P(('blk', 'dp'))
- grad_inner: float32 [1024, 4096], P(('blk', 'dp'))
- grad_outer: float32 [4096, 1024], P(('blk', 'dp'))
- grad_vectors: float32 [8, 1024], P(None, ('blk', 'dp'))
- grad_hidden_bias: float32 [4096], P(('blk', 'dp'))
Inputs may be any that keep to these rules, and one draw needn't show every extreme that they name: Device i of blk holds the positions block_order[i] * 128 to block_order[i] * 128 + 127 of every segment; every block is held once. `vectors`: rows 0 and 5 are gains between 0.5 and 1.5.
All inputs are finite; a program needn't handle non-finite values.
Results may differ from a plain program's by a relative error of at most 0.015.
Values may be sent and summed in bfloat16 or wider, within the bound.
A program may use at most 256 MiB of HBM per device.

v0:
```python
from functools import partial

import jax
import jax.numpy as jnp
from jax import lax
from jax.sharding import PartitionSpec as P

HEADS = 16


masked_value = -1e30


def passed_along(block, axis, distance):
    devices = range(lax.axis_size(axis))
    route = [((i - distance) % len(devices), i) for i in devices]
    return lax.ppermute(block, axis, route)


def layer_norm(values, gain, shift):
    center = values - jnp.mean(values, axis=-1, keepdims=True)
    spread = jnp.mean(center * center, axis=-1, keepdims=True)
    return center * lax.rsqrt(spread + 1e-05) * gain + shift


def contract_rows(left, right):
    return lax.dot_general(
        left, right, (((0,), (0,)), ((), ())), preferred_element_type=jnp.float32
    )


def times_transposed(left, right):
    return lax.dot_general(
        left, right, (((1,), (1,)), ((), ())), preferred_element_type=jnp.float32
    )


def split_heads(matrix, heads):
    return matrix.reshape(matrix.shape[0], heads, matrix.shape[1] // heads)


def score_block(query_heads, key_rows):
    key_heads = split_heads(key_rows, query_heads.shape[1])
    return (
        jnp.einsum("qhd,khd->hqk", query_heads, key_heads, preferred_element_type=jnp.float32)
        * 0.125
    )


def lookup_block(order, device):
    return jnp.sum(jnp.where(jnp.arange(order.shape[0]) == device, order, 0))


def split_piece(piece, rows_dev, mem_rows):
    shards = piece.shape[0] // rows_dev
    blocks = piece.reshape(shards, rows_dev, piece.shape[1])
    memory_part = blocks[:, :mem_rows].reshape(shards * mem_rows, piece.shape[1])
    token_part = blocks[:, mem_rows:].reshape(shards * (rows_dev - mem_rows), piece.shape[1])
    return (shards, memory_part, token_part)


def piece_positions(order, shards, tok_rows):
    shard_ids = jnp.arange(shards)
    hits = shard_ids[:, None] == jnp.arange(order.shape[0])[None, :]
    starts = jnp.sum(jnp.where(hits, order[None, :], 0), axis=1)
    positions = (starts[:, None] * tok_rows + jnp.arange(tok_rows)[None, :]).reshape(
        shards * tok_rows
    )
    return (starts, positions)


def softmax_stats(carry, scores):
    running, total = carry
    top = jnp.maximum(running, jnp.max(scores, axis=2))
    total = total * jnp.exp(running - top) + jnp.sum(jnp.exp(scores - top[:, :, None]), axis=2)
    return (top, total)


def per_device(
    layer_input,
    memory,
    cotangent,
    block_order,
    w_query,
    w_key,
    w_value,
    w_output,
    w_in,
    w_out,
    vectors,
    b_in,
):
    bf16 = jnp.bfloat16
    gathered = (
        lax.all_gather(w_query.astype(bf16), ("blk", "dp"), axis=0, tiled=True),
        lax.all_gather(w_key.astype(bf16), ("blk", "dp"), axis=0, tiled=True),
        lax.all_gather(w_value.astype(bf16), ("blk", "dp"), axis=0, tiled=True),
        lax.all_gather(w_output.astype(bf16), ("blk", "dp"), axis=0, tiled=True),
        lax.all_gather(w_in.astype(bf16), ("blk", "dp"), axis=0, tiled=True),
        lax.all_gather(w_out.astype(bf16), ("blk", "dp"), axis=0, tiled=True),
        lax.all_gather(vectors.astype(bf16), ("blk", "dp"), axis=1, tiled=True),
        lax.all_gather(b_in.astype(bf16), ("blk", "dp"), axis=0, tiled=True),
    )
    (
        query_full,
        key_full,
        value_full,
        output_full,
        inner_full,
        outer_full,
        vector_full,
        inner_low,
    ) = gathered
    params = vector_full.astype(jnp.float32)
    inner_shift = inner_low.astype(jnp.float32)
    heads = HEADS
    tokens = layer_input[0].astype(jnp.float32)
    recalled = memory[0].astype(jnp.float32)
    tok_rows = tokens.shape[0]
    mem_rows = recalled.shape[0]
    rows_dev = tok_rows + mem_rows
    width = tokens.shape[1]
    blocks_total = lax.axis_size("blk")
    here = lax.axis_index("blk")
    own_block = lookup_block(block_order, here)
    query_pos = own_block * tok_rows + jnp.arange(tok_rows)
    both_rows = jnp.concatenate([recalled, tokens], axis=0)
    normed = layer_norm(both_rows, params[0], params[1]).astype(bf16)
    normed_tok = normed[mem_rows:]
    queries = (
        jnp.dot(normed_tok, query_full, preferred_element_type=jnp.float32) + params[2]
    ).astype(bf16)
    keys_all = jnp.dot(normed, key_full, preferred_element_type=jnp.float32).astype(bf16)
    values_all = (
        jnp.dot(normed, value_full, preferred_element_type=jnp.float32) + params[3]
    ).astype(bf16)
    query_heads = split_heads(queries, heads)

    def causal(scores, key_pos):
        return jnp.where(key_pos[None, None, :] <= query_pos[None, :, None], scores, masked_value)

    start_stats = (
        jnp.full((heads, tok_rows), masked_value, jnp.float32),
        jnp.zeros((heads, tok_rows), jnp.float32),
    )
    carry = start_stats
    shards, memory_part, token_part = split_piece(
        lax.all_gather(keys_all, "blk", axis=0, tiled=True), rows_dev, mem_rows
    )
    starts, token_pos = piece_positions(block_order, shards, tok_rows)
    carry = softmax_stats(carry, score_block(query_heads, memory_part))

    def with_tokens(state):
        return softmax_stats(state, causal(score_block(query_heads, token_part), token_pos))

    def without_tokens(state):
        return state

    running, total = lax.cond(jnp.any(starts <= own_block), with_tokens, without_tokens, carry)
    log_total = running + jnp.log(total)

    def value_part(context, part, key_pos):
        scores = score_block(query_heads, part[:, :width])
        if key_pos is not None:
            scores = causal(scores, key_pos)
        weights = jnp.exp(scores - log_total[:, :, None]).astype(bf16)
        return context + jnp.einsum(
            "hqk,khd->qhd",
            weights,
            split_heads(part[:, width:], heads),
            preferred_element_type=jnp.float32,
        )

    key_values = jnp.concatenate([keys_all, values_all], axis=1)
    context = jnp.zeros((tok_rows, heads, width // heads), jnp.float32)
    shards, memory_part, add_token_part = split_piece(
        lax.all_gather(key_values, "blk", axis=0, tiled=True), rows_dev, mem_rows
    )
    starts, add_token_pos = piece_positions(block_order, shards, tok_rows)
    context = value_part(context, memory_part, None)

    def with_tokens(state):
        return value_part(state, add_token_part, add_token_pos)

    def without_tokens(state):
        return state

    context = lax.cond(jnp.any(starts <= own_block), with_tokens, without_tokens, context)
    context_low = context.reshape(tok_rows, width).astype(bf16)
    attended = jnp.dot(context_low, output_full, preferred_element_type=jnp.float32) + params[4]
    middle = tokens + attended
    normed_two = layer_norm(middle, params[5], params[6]).astype(bf16)
    inner = jnp.dot(normed_two, inner_full, preferred_element_type=jnp.float32) + inner_shift
    activated = jax.nn.gelu(inner, approximate=True).astype(bf16)
    result = middle + jnp.dot(activated, outer_full, preferred_element_type=jnp.float32) + params[7]
    output = result.astype(bf16)
    upstream = cotangent[0]
    upstream_full = upstream.astype(jnp.float32)
    grad_outer = contract_rows(activated, upstream)
    grad_outer_bias = jnp.sum(upstream_full, axis=0)
    act_grad = times_transposed(upstream, outer_full)
    _, gelu_back = jax.vjp(partial(jax.nn.gelu, approximate=True), inner)
    inner_grad = gelu_back(act_grad)[0].astype(bf16)
    grad_inner = contract_rows(normed_two, inner_grad)
    grad_inner_bias = jnp.sum(inner_grad.astype(jnp.float32), axis=0)
    normed_two_grad = times_transposed(inner_grad, inner_full)
    _, norm_two_back = jax.vjp(layer_norm, middle, params[5], params[6])
    middle_part, grad_gain_two, grad_shift_two = norm_two_back(normed_two_grad)
    middle_grad = upstream_full + middle_part
    attended_grad = middle_grad.astype(bf16)
    grad_output = contract_rows(context_low, attended_grad)
    grad_output_bias = jnp.sum(attended_grad.astype(jnp.float32), axis=0)
    context_grad = times_transposed(attended_grad, output_full).astype(bf16)
    context_heads = split_heads(context_grad, heads)
    delta = jnp.einsum("qhd,qhd->hq", context_heads.astype(jnp.float32), context)

    def attend_back(queries_grad, part, key_pos):
        count = part.shape[0]
        key_heads = split_heads(part[:, :width], heads)
        value_heads = split_heads(part[:, width:], heads)
        scores = score_block(query_heads, part[:, :width])
        if key_pos is not None:
            scores = causal(scores, key_pos)
        exact = jnp.exp(scores - log_total[:, :, None])
        weight_low = exact.astype(bf16)
        weight_grad = jnp.einsum(
            "qhd,khd->hqk", context_heads, value_heads, preferred_element_type=jnp.float32
        )
        score_grad = (exact * (weight_grad - delta[:, :, None])).astype(bf16)
        queries_grad = (
            queries_grad
            + jnp.einsum("hqk,khd->qhd", score_grad, key_heads, preferred_element_type=jnp.float32)
            * 0.125
        )
        key_grad = (
            jnp.einsum("hqk,qhd->khd", score_grad, query_heads, preferred_element_type=jnp.float32)
            * 0.125
        )
        value_grad = jnp.einsum(
            "hqk,qhd->khd", weight_low, context_heads, preferred_element_type=jnp.float32
        )
        return (
            queries_grad,
            jnp.concatenate(
                [key_grad.reshape(count, width), value_grad.reshape(count, width)], axis=1
            ),
        )

    def visit(queries_grad, travelling, travel_grad, anchor):
        anchor_block = lookup_block(block_order, anchor)
        queries_grad, memory_grad = attend_back(queries_grad, travelling[:mem_rows], None)
        token_pos = anchor_block * tok_rows + jnp.arange(tok_rows)

        def with_tokens(state):
            return attend_back(state, travelling[mem_rows:], token_pos)

        def without_tokens(state):
            return (state, jnp.zeros((tok_rows, 2 * width), jnp.float32))

        queries_grad, token_grad = lax.cond(
            anchor_block <= own_block, with_tokens, without_tokens, queries_grad
        )
        return (queries_grad, travel_grad + jnp.concatenate([memory_grad, token_grad], axis=0))

    def pass_grads(values):
        return passed_along(values.astype(jnp.bfloat16), "blk", 1).astype(values.dtype)

    queries_grad, travel_grad = visit(
        jnp.zeros((tok_rows, heads, width // heads), jnp.float32),
        key_values,
        jnp.zeros((rows_dev, 2 * width), jnp.float32),
        here,
    )

    def turn(step, state):
        queries_grad, travelling, travel_grad = state
        travelling = passed_along(travelling, "blk", 1)
        travel_grad = pass_grads(travel_grad)
        anchor = (here - step) % blocks_total
        queries_grad, travel_grad = visit(queries_grad, travelling, travel_grad, anchor)
        return (queries_grad, travelling, travel_grad)

    queries_grad, travelling, travel_grad = lax.fori_loop(
        1, blocks_total, turn, (queries_grad, key_values, travel_grad)
    )
    travel_grad = pass_grads(travel_grad)
    pair_grad = travel_grad.astype(bf16)
    key_grad = pair_grad[:, :width]
    value_grad = pair_grad[:, width:]
    query_grad = queries_grad.reshape(tok_rows, width).astype(bf16)
    grad_query = contract_rows(normed_tok, query_grad)
    grad_query_bias = jnp.sum(query_grad.astype(jnp.float32), axis=0)
    grad_key = contract_rows(normed, key_grad)
    grad_value = contract_rows(normed, value_grad)
    grad_value_bias = jnp.sum(value_grad.astype(jnp.float32), axis=0)
    normed_grad = times_transposed(key_grad, key_full) + times_transposed(value_grad, value_full)
    query_part = times_transposed(query_grad, query_full)
    normed_grad = normed_grad + jnp.concatenate(
        [jnp.zeros((mem_rows, width), jnp.float32), query_part], axis=0
    )
    _, norm_one_back = jax.vjp(layer_norm, both_rows, params[0], params[1])
    rows_grad, grad_gain_one, grad_shift_one = norm_one_back(normed_grad)
    input_grad = middle_grad + rows_grad[mem_rows:]
    vector_grad = jnp.stack(
        [
            grad_gain_one,
            grad_shift_one,
            grad_query_bias,
            grad_value_bias,
            grad_output_bias,
            grad_gain_two,
            grad_shift_two,
            grad_outer_bias,
        ]
    )
    out_query, out_key, out_value, out_output, out_inner, out_outer, out_vectors, out_bias = (
        lax.psum_scatter(grad_query, ("blk", "dp"), scatter_dimension=0, tiled=True),
        lax.psum_scatter(grad_key, ("blk", "dp"), scatter_dimension=0, tiled=True),
        lax.psum_scatter(grad_value, ("blk", "dp"), scatter_dimension=0, tiled=True),
        lax.psum_scatter(grad_output, ("blk", "dp"), scatter_dimension=0, tiled=True),
        lax.psum_scatter(grad_inner, ("blk", "dp"), scatter_dimension=0, tiled=True),
        lax.psum_scatter(grad_outer, ("blk", "dp"), scatter_dimension=0, tiled=True),
        lax.psum_scatter(vector_grad, ("blk", "dp"), scatter_dimension=1, tiled=True),
        lax.psum_scatter(grad_inner_bias, ("blk", "dp"), scatter_dimension=0, tiled=True),
    )
    return (
        output[None],
        input_grad[None],
        out_query,
        out_key,
        out_value,
        out_output,
        out_inner,
        out_outer,
        out_vectors,
        out_bias,
    )


def solution(mesh):
    return jax.shard_map(
        per_device,
        mesh=mesh,
        in_specs=(
            P("dp", "blk", None),
            P("dp", "blk", None),
            P("dp", "blk", None),
            P(),
            P(("blk", "dp"), None),
            P(("blk", "dp"), None),
            P(("blk", "dp"), None),
            P(("blk", "dp"), None),
            P(("blk", "dp"), None),
            P(("blk", "dp"), None),
            P(None, ("blk", "dp")),
            P(("blk", "dp")),
        ),
        out_specs=(
            P("dp", "blk", None),
            P("dp", "blk", None),
            P(("blk", "dp"), None),
            P(("blk", "dp"), None),
            P(("blk", "dp"), None),
            P(("blk", "dp"), None),
            P(("blk", "dp"), None),
            P(("blk", "dp"), None),
            P(None, ("blk", "dp")),
            P(("blk", "dp")),
        ),
        check_vma=False,
    )
```

profile of v0, /device:TPU:0, one launch (start us, length us, event | category | flops | bytes accessed | tf_op | source)
XLA Modules:
  0.0 1951.2 jit_solution(16729786066048057598)
XLA Ops:
  12.8 43.4 %all-gather = bf16[32,32,8]{1,2,0:T(8,128)(2,1)S(1)} all-gather(bf16[1,32,8]{1,2,0:T(8,128)(2,1)S(1)} %convert_bitcast_fusion), channel_id=1, replica_groups=mesh['blk'=8,'dp'=4] {'blk','dp'}, dimensions={0}, use_global_device_ids=true | all-gather | bytes 16896 | tf_op jit(solution)/shard_map/all_gather | solution.py:101
  59.6 11.1 all-gather.11.cloned.1.call-done
  73.7 55.7 %all-gather.13.cloned.1.call-done = bf16[1024,1024]{1,0:T(8,128)(2,1)} async-done(((bf16[32,1024]{1,0:T(8,128)(2,1)}), bf16[1024,1024]{1,0:T(8,128)(2,1)}) %all-gather.13.cloned.1.call-update) | async-done | bytes 2097168 | tf_op jit(solution)/shard_map/all_gather | solution.py:97
  138.5 39.2 %all-gather.1 = bf16[32,1,128]{2,1,0:T(2,128)(2,1)S(1)} all-gather(bf16[1,1,128]{2,1,0:T(2,128)(2,1)S(1)} %convert_bitcast_fusion.1), channel_id=1, replica_groups=mesh['blk'=8,'dp'=4] {'blk','dp'}, dimensions={0}, use_global_device_ids=true | all-gather | bytes 8448 | tf_op jit(solution)/shard_map/all_gather | solution.py:102
  179.2 9.0 all-gather.17.cloned.1.call-done
  193.9 56.3 %all-gather.19.cloned.1.call-done = bf16[1536,1024]{1,0:T(8,128)(2,1)} async-done(((bf16[192,1024]{1,0:T(8,128)(2,1)}), bf16[1536,1024]{1,0:T(8,128)(2,1)}) %all-gather.19.cloned.1.call-update) | async-done | bytes 3145744 | tf_op jit(solution)/shard_map/all_gather | solution.py:148
  256.2 18.8 conditional.3
  257.9 5.2 copy.126
  268.3 3.2 fusion.2
  279.5 70.4 %all-gather.15.cloned.1.call-done = bf16[1536,2048]{1,0:T(8,128)(2,1)} async-done(((bf16[192,2048]{1,0:T(8,128)(2,1)}), bf16[1536,2048]{1,0:T(8,128)(2,1)}) %all-gather.15.cloned.1.call-update) | async-done | bytes 6291472 | tf_op jit(solution)/shard_map/all_gather | solution.py:177
  354.4 3.0 fusion.47
  357.5 26.8 %conditional.4 = (f32[128,16,64]{0,2,1:T(8,128)S(1)}) conditional(s32[]{:T(128)} %convert_element_type.198, f32[128,16,64]{0,2,1:T(8,128)S(1)} %fusion.47, (s32[8,128]{1,0:T(8,128)S(1)}, s32[128]{0:T(128)S(1)}, bf16[8,192,2048]{2,1,0:T(8,128)(2,1)}, bf16[128,16,64]{0,2,1:T(8,128)(2,1)S(1)}, f32[16,128]{1,0:T(8,128)S(1)}, ...), branch_computations={%region_11.12_spmd, %region_12.13_spmd} | conditional | flops 545521664 | bytes 43528712 | solution.py:188
  357.8 12.9 copy.127
  370.7 4.2 slice.151
  378.5 5.3 fusion.8
  384.4 23.4 %all-gather.21.cloned.1.call-done = bf16[1024,1024]{1,0:T(8,128)(2,1)} async-done(((bf16[32,1024]{1,0:T(8,128)(2,1)}), bf16[1024,1024]{1,0:T(8,128)(2,1)}) %all-gather.21.cloned.1.call-update) | async-done | bytes 2097168 | tf_op jit(solution)/shard_map/all_gather | solution.py:98
  410.2 76.9 %all-gather.23.cloned.1.call-done = bf16[1024,4096]{1,0:T(8,128)(2,1)} async-done(((bf16[32,4096]{1,0:T(8,128)(2,1)}), bf16[1024,4096]{1,0:T(8,128)(2,1)}) %all-gather.23.cloned.1.call-update) | async-done | bytes 8388624 | tf_op jit(solution)/shard_map/all_gather | solution.py:99
  487.1 4.7 convolution_add_fusion
  491.8 74.9 %all-gather.25.cloned.1.call-done = bf16[4096,1024]{1,0:T(8,128)(2,1)} async-done(((bf16[128,1024]{1,0:T(8,128)(2,1)}), bf16[4096,1024]{1,0:T(8,128)(2,1)}) %all-gather.25.cloned.1.call-update) | async-done | bytes 8388624 | tf_op jit(solution)/shard_map/all_gather | solution.py:100
  566.7 7.3 convert_reduce_fusion
  574.0 3.0 multiply_reduce_fusion.4
  585.6 279.0 %while.20 = (s32[]{:T(128)}, f32[128,16,64]{0,2,1:T(8,128)S(1)}, bf16[192,2048]{1,0:T(8,128)(2,1)}, bf16[192,2048]{1,0:T(8,128)(2,1)}, s32[]{:T(128)}, /*index=5...) while((s32[]{:T(128)}, f32[128,16,64]{0,2,1:T(8,128)S(1)}, ...), condition=%wide.region_21.22_spmd.clone, body=%wide.region_17.0_spmd.clone.sunk | while | flops 257245472 | bytes 36114468 | solution.py:283
  590.7 18.4 collective-permute-done
  614.2 11.2 collective-permute-done.1
  630.8 20.3 %collective-permute-done = bf16[192,2048]{1,0:T(8,128)(2,1)S(1)} collective-permute-done((bf16[192,2048]{1,0:T(8,128)(2,1)}, bf16[192,2048]{1,0:T(8,128)(2,1)S(1)}, u32[]{:S(2)}, u32[]{:S(2)}) %collective-permute-start) | collective-permute-done | bytes 786464 | tf_op jit(solution)/shard_map/while/body/eval_jaxpr/ppermute | solution.py:17
  655.1 8.8 conditional.7
  670.7 21.5 %collective-permute-done = bf16[192,2048]{1,0:T(8,128)(2,1)S(1)} collective-permute-done((bf16[192,2048]{1,0:T(8,128)(2,1)}, bf16[192,2048]{1,0:T(8,128)(2,1)S(1)}, u32[]{:S(2)}, u32[]{:S(2)}) %collective-permute-start) | collective-permute-done | bytes 786464 | tf_op jit(solution)/shard_map/while/body/eval_jaxpr/ppermute | solution.py:17
  696.2 8.8 conditional.7
  710.9 21.5 %collective-permute-done = bf16[192,2048]{1,0:T(8,128)(2,1)S(1)} collective-permute-done((bf16[192,2048]{1,0:T(8,128)(2,1)}, bf16[192,2048]{1,0:T(8,128)(2,1)S(1)}, u32[]{:S(2)}, u32[]{:S(2)}) %collective-permute-start) | collective-permute-done | bytes 786464 | tf_op jit(solution)/shard_map/while/body/eval_jaxpr/ppermute | solution.py:17
  737.5 8.4 collective-permute-done.1
  750.2 21.5 %collective-permute-done = bf16[192,2048]{1,0:T(8,128)(2,1)S(1)} collective-permute-done((bf16[192,2048]{1,0:T(8,128)(2,1)}, bf16[192,2048]{1,0:T(8,128)(2,1)S(1)}, u32[]{:S(2)}, u32[]{:S(2)}) %collective-permute-start) | collective-permute-done | bytes 786464 | tf_op jit(solution)/shard_map/while/body/eval_jaxpr/ppermute | solution.py:17
  775.7 8.8 conditional.7
  789.7 21.5 %collective-permute-done = bf16[192,2048]{1,0:T(8,128)(2,1)S(1)} collective-permute-done((bf16[192,2048]{1,0:T(8,128)(2,1)}, bf16[192,2048]{1,0:T(8,128)(2,1)S(1)}, u32[]{:S(2)}, u32[]{:S(2)}) %collective-permute-start) | collective-permute-done | bytes 786464 | tf_op jit(solution)/shard_map/while/body/eval_jaxpr/ppermute | solution.py:17
  815.3 8.8 conditional.7
  829.3 19.0 collective-permute-done
  852.4 8.8 conditional.7
  867.5 12.0 collective-permute-done.2
  898.3 8.2 fusion.90
  908.1 8.1 fusion.74
  916.3 37.0 %all-reduce.1 = f32[4096]{0:T(1024)S(1)} all-reduce(f32[4096]{0:T(1024)S(1)} %get-tuple-element.659), channel_id=9, replica_groups=mesh['blk'=8,'dp'=4] {'blk','dp'}, use_global_device_ids=true, to_apply=%region_40.41.clone | all-reduce | flops 4096 | bytes 32768
  953.9 5.7 fusion.58
  959.6 56.7 %reduce-scatter.22.cloned.1.call-done = f32[32,8]{1,0:T(8,128)} async-done(((f32[1024,8]{1,0:T(8,128)}), f32[32,8]{1,0:T(8,128)}) %reduce-scatter.22.cloned.1.call-update) | async-done | bytes 1040
  1017.6 138.4 %reduce-scatter.16.cloned.1.call-done = f32[32,1024]{1,0:T(8,128)} async-done(((f32[1024,1024]{1,0:T(8,128)}), f32[32,1024]{1,0:T(8,128)}) %reduce-scatter.16.cloned.1.call-update) | async-done | bytes 131088 | tf_op jit(solution)/shard_map/reduce_scatter | solution.py:320
  1155.9 140.0 %reduce-scatter.10.cloned.1.call-done = f32[32,1024]{1,0:T(8,128)} async-done(((f32[1024,1024]{1,0:T(8,128)}), f32[32,1024]{1,0:T(8,128)}) %reduce-scatter.10.cloned.1.call-update) | async-done | bytes 131088 | tf_op jit(solution)/shard_map/reduce_scatter | solution.py:317
  1295.9 139.7 %reduce-scatter.12.cloned.1.call-done = f32[32,1024]{1,0:T(8,128)} async-done(((f32[1024,1024]{1,0:T(8,128)}), f32[32,1024]{1,0:T(8,128)}) %reduce-scatter.12.cloned.1.call-update) | async-done | bytes 131088 | tf_op jit(solution)/shard_map/reduce_scatter | solution.py:318
  1435.6 139.7 %reduce-scatter.14.cloned.1.call-done = f32[32,1024]{1,0:T(8,128)} async-done(((f32[1024,1024]{1,0:T(8,128)}), f32[32,1024]{1,0:T(8,128)}) %reduce-scatter.14.cloned.1.call-update) | async-done | bytes 131088 | tf_op jit(solution)/shard_map/reduce_scatter | solution.py:319
  1575.2 181.8 %reduce-scatter.18.cloned.1.call-done = f32[32,4096]{1,0:T(8,128)} async-done(((f32[1024,4096]{1,0:T(8,128)}), f32[32,4096]{1,0:T(8,128)}) %reduce-scatter.18.cloned.1.call-update) | async-done | bytes 524304 | tf_op jit(solution)/shard_map/reduce_scatter | solution.py:321
  1757.0 187.4 %reduce-scatter.20.cloned.1.call-done = f32[128,1024]{1,0:T(8,128)} async-done(((f32[4096,1024]{1,0:T(8,128)}), f32[128,1024]{1,0:T(8,128)}) %reduce-scatter.20.cloned.1.call-update) | async-done | bytes 524304 | tf_op jit(solution)/shard_map/reduce_scatter | solution.py:322
  (455 shorter events, 194.0 us)
Async XLA Ops:
  7.2 63.5 %all-gather.11.cloned.1.call-start = ((), (), s32[]{:S(2)}) async-start(), calls=%async_computation.7 | async-start | bytes 2162688 | tf_op jit(solution)/shard_map/all_gather | solution.py:96
  8.8 120.6 %all-gather.13.cloned.1.call-start = ((), (), s32[]{:S(2)}) async-start(), calls=%async_computation.8 | async-start | bytes 2162688 | tf_op jit(solution)/shard_map/all_gather | solution.py:97
  10.4 177.7 %all-gather.17.cloned.1.call-start = ((), (), s32[]{:S(2)}) async-start(), calls=%async_computation.10 | async-start | bytes 2162688 | tf_op jit(solution)/shard_map/all_gather | solution.py:95
  12.0 238.1 %all-gather.19.cloned.1.call-start = ((), (), s32[]{:S(2)}) async-start(), calls=%async_computation.11 | async-start | bytes 3538944 | tf_op jit(solution)/shard_map/all_gather | solution.py:148
  58.7 14.9 copy-start.49
  59.6 128.6 %copy-start.6 = (bf16[192,1024]{1,0:T(8,128)(2,1)}, bf16[192,1024]{1,0:T(8,128)(2,1)S(1)}, u32[]{:S(2)}) copy-start(bf16[192,1024]{1,0:T(8,128)(2,1)S(1)} %add_convert_fusion) | copy-start | bytes 1179652
  73.6 58.0 %copy-start.13 = (bf16[192,1024]{1,0:T(8,128)(2,1)S(1)}, bf16[192,1024]{1,0:T(8,128)(2,1)}, u32[]{:S(2)}) copy-start(bf16[192,1024]{1,0:T(8,128)(2,1)} %convolution_convert_fusion) | copy-start | bytes 1179652
  73.6 276.2 %all-gather.15.cloned.1.call-start = ((), (), s32[]{:S(2)}) async-start(), calls=%async_computation.9 | async-start | bytes 7077888 | tf_op jit(solution)/shard_map/all_gather | solution.py:177
  131.6 47.5 %copy-start.31 = (bf16[192,1024]{1,0:T(8,128)(2,1)}, bf16[192,1024]{1,0:T(8,128)(2,1)S(1)}, u32[]{:S(2)}) copy-start(bf16[192,1024]{1,0:T(8,128)(2,1)S(1)} %fusion.46) | copy-start | bytes 1179652
  132.7 275.1 %all-gather.21.cloned.1.call-start = ((), (), s32[]{:S(2)}) async-start(), calls=%async_computation.12 | async-start | bytes 2162688 | tf_op jit(solution)/shard_map/all_gather | solution.py:98
  133.4 353.7 %all-gather.23.cloned.1.call-start = ((), (), s32[]{:S(2)}) async-start(), calls=%async_computation.13 | async-start | bytes 8650752 | tf_op jit(solution)/shard_map/all_gather | solution.py:99
  134.3 432.4 %all-gather.25.cloned.1.call-start = ((), (), s32[]{:S(2)}) async-start(), calls=%async_computation.14 | async-start | bytes 8650752 | tf_op jit(solution)/shard_map/all_gather | solution.py:100
  135.1 881.1 %reduce-scatter.22.cloned.1.call-start = ((), (), s32[]{:S(2)}) async-start(), calls=%async_computation.21 | async-start | bytes 540672
  178.4 77.8 %copy-start.43 = (s32[8,128]{1,0:T(8,128)}, s32[8,128]{1,0:T(8,128)S(1)}, u32[]{:S(2)}) copy-start(s32[8,128]{1,0:T(8,128)S(1)} %iota_add_fusion) | copy-start | bytes 12292
  357.5 50.3 %copy-start.48 = (f32[1,1024]{1,0:T(1,128)S(1)}, f32[1,1024]{1,0:T(1,128)}, u32[]{:S(2)}) copy-start(f32[1,1024]{1,0:T(1,128)} %get-tuple-element.648) | copy-start | bytes 12292
  384.3 23.5 %copy-start.27 = (f32[128,16,64]{0,2,1:T(8,128)}, f32[128,16,64]{0,2,1:T(8,128)S(1)}, u32[]{:S(2)}) copy-start(f32[128,16,64]{0,2,1:T(8,128)S(1)} %get-tuple-element.799) | copy-start | bytes 1572868
  384.3 102.8 %copy-start.40 = (f32[32,1,128]{2,1,0:T(1,128)S(1)}, f32[32,1,128]{2,1,0:T(1,128)}, u32[]{:S(2)}) copy-start(f32[32,1,128]{2,1,0:T(1,128)} %convert_element_type.239) | copy-start | bytes 49156
  384.4 102.7 %copy-start.24 = (bf16[128,16,64]{0,2,1:T(8,128)(2,1)}, bf16[128,16,64]{0,2,1:T(8,128)(2,1)S(1)}, u32[]{:S(2)}) copy-start(bf16[128,16,64]{0,2,1:T(8,128)(2,1)S(1)} %convert_element_type.211) | copy-start | bytes 786436
  409.9 167.2 %copy-start.2 = (f32[128,1024]{1,0:T(8,128)}, f32[128,1024]{1,0:T(8,128)S(1)}, u32[]{:S(2)}) copy-start(f32[128,1024]{1,0:T(8,128)S(1)} %get-tuple-element.656) | copy-start | bytes 1572868
  491.8 82.2 %copy-start.8 = (f32[128,4096]{1,0:T(8,128)}, f32[128,4096]{1,0:T(8,128)S(1)}, u32[]{:S(2)}) copy-start(f32[128,4096]{1,0:T(8,128)S(1)} %convolution_add_fusion) | copy-start | bytes 6291460
  585.7 23.3 %collective-permute-start = (bf16[192,2048]{1,0:T(8,128)(2,1)}, bf16[192,2048]{1,0:T(8,128)(2,1)S(1)}, u32[]{:S(2)}, u32[]{:S(2)}) collective-permute-start(bf16[192,2048]{1,0:T(8,128)(2,1)} %get-tuple-element.768), channel_id=1, source_target_pairs={{28,0},{0,4},{4,8},{8,12},{12,16},{16,20},{20,24},{24,28},{29,1},{... | collective-permute-start | bytes 2359304 | tf_op jit(solution)/shard_map/while/body/eval_jaxpr/ppermute | solution.py:17
  587.2 38.1 %collective-permute-start.1 = (bf16[192,2048]{1,0:T(8,128)(2,1)}, bf16[192,2048]{1,0:T(8,128)(2,1)}, u32[]{:S(2)}, u32[]{:S(2)}) collective-permute-start(bf16[192,2048]{1,0:T(8,128)(2,1)} %get-tuple-element.769), channel_id=1, source_target_pairs={{28,0},{0,4},{4,8},{8,12},{12,16},{16,20},{20,24},{24,28},{29,1},{... | collective-permute-start | bytes 2359304 | tf_op jit(solution)/shard_map/while/body/eval_jaxpr/ppermute | solution.py:17
  627.7 23.4 %collective-permute-start = (bf16[192,2048]{1,0:T(8,128)(2,1)}, bf16[192,2048]{1,0:T(8,128)(2,1)S(1)}, u32[]{:S(2)}, u32[]{:S(2)}) collective-permute-start(bf16[192,2048]{1,0:T(8,128)(2,1)} %get-tuple-element.768), channel_id=1, source_target_pairs={{28,0},{0,4},{4,8},{8,12},{12,16},{16,20},{20,24},{24,28},{29,1},{... | collective-permute-start | bytes 2359304 | tf_op jit(solution)/shard_map/while/body/eval_jaxpr/ppermute | solution.py:17
  627.7 38.7 %collective-permute-start.1 = (bf16[192,2048]{1,0:T(8,128)(2,1)}, bf16[192,2048]{1,0:T(8,128)(2,1)}, u32[]{:S(2)}, u32[]{:S(2)}) collective-permute-start(bf16[192,2048]{1,0:T(8,128)(2,1)} %get-tuple-element.769), channel_id=1, source_target_pairs={{28,0},{0,4},{4,8},{8,12},{12,16},{16,20},{20,24},{24,28},{29,1},{... | collective-permute-start | bytes 2359304 | tf_op jit(solution)/shard_map/while/body/eval_jaxpr/ppermute | solution.py:17
  668.8 23.4 %collective-permute-start = (bf16[192,2048]{1,0:T(8,128)(2,1)}, bf16[192,2048]{1,0:T(8,128)(2,1)S(1)}, u32[]{:S(2)}, u32[]{:S(2)}) collective-permute-start(bf16[192,2048]{1,0:T(8,128)(2,1)} %get-tuple-element.768), channel_id=1, source_target_pairs={{28,0},{0,4},{4,8},{8,12},{12,16},{16,20},{20,24},{24,28},{29,1},{... | collective-permute-start | bytes 2359304 | tf_op jit(solution)/shard_map/while/body/eval_jaxpr/ppermute | solution.py:17
  668.8 37.8 %collective-permute-start.1 = (bf16[192,2048]{1,0:T(8,128)(2,1)}, bf16[192,2048]{1,0:T(8,128)(2,1)}, u32[]{:S(2)}, u32[]{:S(2)}) collective-permute-start(bf16[192,2048]{1,0:T(8,128)(2,1)} %get-tuple-element.769), channel_id=1, source_target_pairs={{28,0},{0,4},{4,8},{8,12},{12,16},{16,20},{20,24},{24,28},{29,1},{... | collective-permute-start | bytes 2359304 | tf_op jit(solution)/shard_map/while/body/eval_jaxpr/ppermute | solution.py:17
  709.0 23.4 %collective-permute-start = (bf16[192,2048]{1,0:T(8,128)(2,1)}, bf16[192,2048]{1,0:T(8,128)(2,1)S(1)}, u32[]{:S(2)}, u32[]{:S(2)}) collective-permute-start(bf16[192,2048]{1,0:T(8,128)(2,1)} %get-tuple-element.768), channel_id=1, source_target_pairs={{28,0},{0,4},{4,8},{8,12},{12,16},{16,20},{20,24},{24,28},{29,1},{... | collective-permute-start | bytes 2359304 | tf_op jit(solution)/shard_map/while/body/eval_jaxpr/ppermute | solution.py:17
  709.0 36.9 %collective-permute-start.1 = (bf16[192,2048]{1,0:T(8,128)(2,1)}, bf16[192,2048]{1,0:T(8,128)(2,1)}, u32[]{:S(2)}, u32[]{:S(2)}) collective-permute-start(bf16[192,2048]{1,0:T(8,128)(2,1)} %get-tuple-element.769), channel_id=1, source_target_pairs={{28,0},{0,4},{4,8},{8,12},{12,16},{16,20},{20,24},{24,28},{29,1},{... | collective-permute-start | bytes 2359304 | tf_op jit(solution)/shard_map/while/body/eval_jaxpr/ppermute | solution.py:17
  748.2 23.4 %collective-permute-start = (bf16[192,2048]{1,0:T(8,128)(2,1)}, bf16[192,2048]{1,0:T(8,128)(2,1)S(1)}, u32[]{:S(2)}, u32[]{:S(2)}) collective-permute-start(bf16[192,2048]{1,0:T(8,128)(2,1)} %get-tuple-element.768), channel_id=1, source_target_pairs={{28,0},{0,4},{4,8},{8,12},{12,16},{16,20},{20,24},{24,28},{29,1},{... | collective-permute-start | bytes 2359304 | tf_op jit(solution)/shard_map/while/body/eval_jaxpr/ppermute | solution.py:17
  748.2 37.2 %collective-permute-start.1 = (bf16[192,2048]{1,0:T(8,128)(2,1)}, bf16[192,2048]{1,0:T(8,128)(2,1)}, u32[]{:S(2)}, u32[]{:S(2)}) collective-permute-start(bf16[192,2048]{1,0:T(8,128)(2,1)} %get-tuple-element.769), channel_id=1, source_target_pairs={{28,0},{0,4},{4,8},{8,12},{12,16},{16,20},{20,24},{24,28},{29,1},{... | collective-permute-start | bytes 2359304 | tf_op jit(solution)/shard_map/while/body/eval_jaxpr/ppermute | solution.py:17
  787.8 23.4 %collective-permute-start = (bf16[192,2048]{1,0:T(8,128)(2,1)}, bf16[192,2048]{1,0:T(8,128)(2,1)S(1)}, u32[]{:S(2)}, u32[]{:S(2)}) collective-permute-start(bf16[192,2048]{1,0:T(8,128)(2,1)} %get-tuple-element.768), channel_id=1, source_target_pairs={{28,0},{0,4},{4,8},{8,12},{12,16},{16,20},{20,24},{24,28},{29,1},{... | collective-permute-start | bytes 2359304 | tf_op jit(solution)/shard_map/while/body/eval_jaxpr/ppermute | solution.py:17
  787.8 37.2 %collective-permute-start.1 = (bf16[192,2048]{1,0:T(8,128)(2,1)}, bf16[192,2048]{1,0:T(8,128)(2,1)}, u32[]{:S(2)}, u32[]{:S(2)}) collective-permute-start(bf16[192,2048]{1,0:T(8,128)(2,1)} %get-tuple-element.769), channel_id=1, source_target_pairs={{28,0},{0,4},{4,8},{8,12},{12,16},{16,20},{20,24},{24,28},{29,1},{... | collective-permute-start | bytes 2359304 | tf_op jit(solution)/shard_map/while/body/eval_jaxpr/ppermute | solution.py:17
  827.4 21.0 %collective-permute-start = (bf16[192,2048]{1,0:T(8,128)(2,1)}, bf16[192,2048]{1,0:T(8,128)(2,1)S(1)}, u32[]{:S(2)}, u32[]{:S(2)}) collective-permute-start(bf16[192,2048]{1,0:T(8,128)(2,1)} %get-tuple-element.768), channel_id=1, source_target_pairs={{28,0},{0,4},{4,8},{8,12},{12,16},{16,20},{20,24},{24,28},{29,1},{... | collective-permute-start | bytes 2359304 | tf_op jit(solution)/shard_map/while/body/eval_jaxpr/ppermute | solution.py:17
  827.4 34.8 %collective-permute-start.1 = (bf16[192,2048]{1,0:T(8,128)(2,1)}, bf16[192,2048]{1,0:T(8,128)(2,1)}, u32[]{:S(2)}, u32[]{:S(2)}) collective-permute-start(bf16[192,2048]{1,0:T(8,128)(2,1)} %get-tuple-element.769), channel_id=1, source_target_pairs={{28,0},{0,4},{4,8},{8,12},{12,16},{16,20},{20,24},{24,28},{29,1},{... | collective-permute-start | bytes 2359304 | tf_op jit(solution)/shard_map/while/body/eval_jaxpr/ppermute | solution.py:17
  864.6 14.9 collective-permute-start.2
  864.9 14.6 copy-start.30
  867.4 12.9 copy-start.5
  867.4 12.9 copy-start.12
  867.5 12.9 copy-start.29
  867.5 12.9 copy-start.42
  867.5 12.9 copy-start.47
  884.8 271.1 %reduce-scatter.16.cloned.1.call-start = ((), (), s32[]{:S(2)}) async-start(), calls=%async_computation.18 | async-start | bytes 4325376 | tf_op jit(solution)/shard_map/reduce_scatter | solution.py:320
  887.5 408.4 %reduce-scatter.10.cloned.1.call-start = ((), (), s32[]{:S(2)}) async-start(), calls=%async_computation.15 | async-start | bytes 4325376 | tf_op jit(solution)/shard_map/reduce_scatter | solution.py:317
  891.2 544.3 %reduce-scatter.12.cloned.1.call-start = ((), (), s32[]{:S(2)}) async-start(), calls=%async_computation.16 | async-start | bytes 4325376 | tf_op jit(solution)/shard_map/reduce_scatter | solution.py:318
  894.1 681.1 %reduce-scatter.14.cloned.1.call-start = ((), (), s32[]{:S(2)}) async-start(), calls=%async_computation.17 | async-start | bytes 4325376 | tf_op jit(solution)/shard_map/reduce_scatter | solution.py:319
  896.9 860.1 %reduce-scatter.18.cloned.1.call-start = ((), (), s32[]{:S(2)}) async-start(), calls=%async_computation.19 | async-start | bytes 17301504 | tf_op jit(solution)/shard_map/reduce_scatter | solution.py:321
  906.6 1037.9 %reduce-scatter.20.cloned.1.call-start = ((), (), s32[]{:S(2)}) async-start(), calls=%async_computation.20 | async-start | bytes 17301504 | tf_op jit(solution)/shard_map/reduce_scatter | solution.py:322
  916.3 37.6 %copy-start.55 = (f32[1,1024]{1,0:T(1,128)S(1)}, f32[1,1024]{1,0:T(1,128)}, u32[]{:S(2)}) copy-start(f32[1,1024]{1,0:T(1,128)} %get-tuple-element.646) | copy-start | bytes 12292
  (47 other events, 150.9 us)
Sparse Core Ops, SparseCore 0:
  11.4 59.1 all-gather.10
  74.1 55.2 all-gather.12
  132.8 55.2 all-gather.16
  190.8 59.3 all-gather.18
  252.2 97.6 all-gather.14
  353.1 54.5 all-gather.20
  410.6 76.4 all-gather.22
  490.5 76.1 all-gather.24
  884.9 131.2 reduce-scatter.21
  1019.0 136.8 reduce-scatter.15
  1158.9 136.9 reduce-scatter.9
  1298.7 136.8 reduce-scatter.11
  1438.5 136.6 reduce-scatter.13
  1578.1 178.8 reduce-scatter.17
  1759.8 184.5 reduce-scatter.19
where the time goes:
time: 1960 us; the launch traced here: 1950 us
  waiting for transfers between devices  1540 us (79%)
  blocking collectives  120 us (6%)
  matrix products  111 us (6%)
  local copies, waits for them, and re-layouts  93.8 us (5%)
  other arithmetic  52.2 us (3%)
    reduce_scatter x1, waiting for transfers between devices, per_device(): lax.psum_scatter(grad_outer, ('blk', 'dp'), scatter_dimension=0, tiled=True)  187 us
    reduce_scatter x1, waiting for transfers between devices, per_device(): lax.psum_scatter(grad_inner, ('blk', 'dp'), scatter_dimension=0, tiled=True)  182 us
    ppermute x15, waiting for transfers between devices, passed_along(): return lax.ppermute(block, axis, route)  177 us
    reduce_scatter x1, waiting for transfers between devices, per_device(): lax.psum_scatter(grad_query, ('blk', 'dp'), scatter_dimension=0, tiled=True)  140 us
    reduce_scatter x1, waiting for transfers between devices, per_device(): lax.psum_scatter(grad_value, ('blk', 'dp'), scatter_dimension=0, tiled=True)  140 us
    reduce_scatter x1, waiting for transfers between devices, per_device(): lax.psum_scatter(grad_key, ('blk', 'dp'), scatter_dimension=0, tiled=True)  140 us
    reduce_scatter x1, waiting for transfers between devices, per_device(): lax.psum_scatter(grad_output, ('blk', 'dp'), scatter_dimension=0, tiled=T...  138 us
    all_gather x1, waiting for transfers between devices, per_device(): lax.all_gather(w_in.astype(bf16), ('blk', 'dp'), axis=0, tiled=True)  76.9 us
  transfers between devices with their start and end apart: 30, of which 27 were waited for; matrix products, arithmetic and copies ran while one was open for 11% of the time, Pallas kernels for 0%

commit v1 on v0

--- a/solution.py
+++ b/solution.py
@@ -1,11 +1,764 @@
-from functools import partial
+import functools
 
 import jax
 import jax.numpy as jnp
 from jax import lax
+from jax.experimental import pallas as pl
+from jax.experimental.pallas import tpu as pltpu
 from jax.sharding import PartitionSpec as P
 
 HEADS = 16
+BF = jnp.bfloat16
+F32 = jnp.float32
+MESH = pl.DeviceIdType.MESH
+EXACT = lax.Precision.HIGHEST
+
+
+def dot(a, b):
+    return lax.dot_general(a, b, (((1,), (0,)), ((), ())), preferred_element_type=F32)
+
+
+def dot_nt(a, b, precision=None):
+    return lax.dot_general(
+        a, b, (((1,), (1,)), ((), ())), preferred_element_type=F32, precision=precision
+    )
+
+
+def dot_tn(a, b):
+    return lax.dot_general(a, b, (((0,), (0,)), ((), ())), preferred_element_type=F32)
+
+
+def flat(value):
+    return value.reshape(-1, value.shape[-1])
+
+
+def col_sum(value):
+    return jnp.sum(value.astype(F32), axis=0, keepdims=True)
+
+
+def norm_parts(rows):
+    center = rows - jnp.mean(rows, axis=-1, keepdims=True)
+    spread = jnp.mean(center * center, axis=-1, keepdims=True)
+    scale = lax.rsqrt(spread + 1e-05)
+    return center * scale, scale
+
+
+def gelu_parts(v):
+    square = v * v
+    t = jnp.tanh(0.7978845608 * v * (1.0 + 0.044715 * square))
+    half = 0.5 * (1.0 + t)
+    slope = half + 0.5 * v * (1.0 - t * t) * (0.7978845608 * (1.0 + 3 * 0.044715 * square))
+    return v * half, slope
+
+
+IN_NAMES = ["x", "mem", "cot", "order", "wq", "wk", "wv", "wo", "win", "wout", "vec", "bias"]
+OUT_NAMES = ["lo", "ig", "gq", "gk", "gv", "go", "gin", "gout", "gvec", "gbin"]
+PLANE = [(1, 1, 1), (1, 1, 0), (1, 0, 1), (1, 0, 0), (0, 1, 1), (0, 1, 0), (0, 0, 1)]
+CLASS = [(1, 1, 0), (1, 0, 0), (0, 1, 0)]
+QUADS = CLASS + [(0, 0, 0)]
+SIB = (0, 0, 1)
+
+
+def scratch_list(T, M, D, FF):
+    R = T + M
+    H = FF // 8
+    Q = D // 4
+    W = D // 8
+    S = 8 * T
+    K = 8 * R
+    return dict(
+        n_all=((8, R, D), BF),
+        xm=((M, D), BF),
+        xt=((T, D), BF),
+        cot_all=((8, T, D), BF),
+        n2_all=((8, T, D), BF),
+        pq=((8, D // 32, 3 * W), BF),
+        pi=((8, D // 32, H), BF),
+        wqkv=((4, 8, D // 32, 3 * W), BF),
+        w_in=((4, 8, D // 32, H), BF),
+        w_out=((4, H // 4, D), BF),
+        w_o=((4, 8, D // 32, D), BF),
+        vg1=((8, 8, W), F32),
+        vg2=((4, 2, 8, W), F32),
+        bslot=((4, 8, H // 4), F32),
+        prm=((8, D), F32),
+        qkv=((8, R, 3 * W), BF),
+        qs=((S, W), BF),
+        kk=((K, W), BF),
+        vv=((K, W), BF),
+        wts=((2, S, K), BF),
+        ctx=((S, W), F32),
+        ctx_send=((8, T, W), BF),
+        ctx_own=((8, T, W), BF),
+        ctx2d=((T, D), BF),
+        mid=((T, D), F32),
+        act=((4, S, H // 4), BF),
+        inner=((S, H), BF),
+        pb_a=((8, T, D), BF),
+        r1_a=((4, T, D), BF),
+        r3_a=((3, T, D), BF),
+        pb_b=((8, T, D), BF),
+        r1_b=((4, T, D), BF),
+        r3_b=((3, T, D), BF),
+        pb_n=((8, T, D), BF),
+        r1_n=((4, T, D), BF),
+        r3_n=((3, T, D), BF),
+        mg=((T, D), F32),
+        attg=((T, D), BF),
+        cg_send=((8, T, W), BF),
+        cg_all=((8, T, W), BF),
+        go_buf=((4, 8, D // 32, D), BF),
+        go_r1=((4, 4, D // 32, D), BF),
+        go_r3=((3, 4, D // 32, D), BF),
+        go_sum=((4, D // 32, D), BF),
+        go_z=((3, D // 32, D), BF),
+        cg_sorted=((S, W), BF),
+        dq=((S, W), F32),
+        dk=((K, W), F32),
+        dv=((K, W), F32),
+        dqkv=((8, R, 3 * W), BF),
+        gout_s=((4, H // 4, D), BF),
+        gout_own=((H // 4, D), F32),
+        gout_r=((3, H // 4, D), BF),
+        gin_s=((4, 8, D // 32, H), BF),
+        gin_own=((Q, H), F32),
+        gin_r=((3, 8, D // 32, H), BF),
+        gin_a=((8, D // 32, H), BF),
+        gin_b=((8, D // 32, H), BF),
+        gqkv_s=((4, 8, D // 32, 3 * W), BF),
+        gqkv_own=((Q, 3 * W), F32),
+        gqkv_r=((3, 8, D // 32, 3 * W), BF),
+        gqkv_a=((8, D // 32, 3 * W), BF),
+        gqkv_b=((8, D // 32, 3 * W), BF),
+        vp=((8, 8, W), F32),
+        vr=((3, 2, 8, W), F32),
+        vs=((2, 8, W), F32),
+        va=((8, 8, W), F32),
+        bp=((4, 8, H // 4), F32),
+        br=((3, 8, H // 4), F32),
+        lo_s=((T, D), BF),
+        ig_s=((T, D), BF),
+    )
+
+
+SEMS = 200
+
+
+class Sender:
+    def __init__(self, ssem, rsem):
+        self.ssem, self.rsem, self.count, self.pending = ssem, rsem, 0, []
+
+    def make(self, src, dst, target):
+        at = self.count
+        self.count += 1
+        return pltpu.make_async_remote_copy(
+            src_ref=src,
+            dst_ref=dst,
+            send_sem=self.ssem.at[at],
+            recv_sem=self.rsem.at[at],
+            device_id=target,
+            device_id_type=MESH,
+        )
+
+    def send(self, src, dst, target):
+        copy = self.make(src, dst, target)
+        copy.start()
+        self.pending.append(copy)
+        return copy
+
+    def drain(self):
+        for copy in self.pending:
+            copy.wait_send()
+
+
+def layer_kernel(T, M, D, FF, *refs):
+    names = IN_NAMES + OUT_NAMES + list(scratch_list(T, M, D, FF))
+    r = dict(zip(names, refs))
+    ssem, rsem = refs[len(names):]
+    g = type("Refs", (), r)
+    R, H, Q, W, S = T + M, FF // 8, D // 4, D // 8, 8 * T
+    H4, D32 = H // 4, D // 32
+    MK = 8 * M
+    tx = Sender(ssem, rsem)
+
+    b, d = lax.axis_index("blk"), lax.axis_index("dp")
+    z, x, y, c = b // 2, b % 2, d // 2, d % 2
+    p = 4 * x + 2 * y + c
+
+    def dev(z, x, y, c):
+        return (2 * z + x, 2 * y + c)
+
+    def near(rel):
+        return dev(z, (x + rel[0]) % 2, (y + rel[1]) % 2, (c + rel[2]) % 2)
+
+    def slot(rel):
+        return 4 * ((x + rel[0]) % 2) + 2 * ((y + rel[1]) % 2) + (c + rel[2]) % 2
+
+    def along(dz):
+        return dev((z + dz) % 4, x, y, c)
+
+    home_z = y + c * (3 - 2 * y)
+    home_y, home_c = (z + z // 2) % 2, z // 2
+    partner = dev(home_z, x, home_y, home_c)
+    partner_slot = 4 * x + 2 * home_y + home_c
+    stays = home_z == z
+    moves = jnp.logical_not(stays)
+
+    barrier = pltpu.get_barrier_semaphore()
+    for rel in PLANE:
+        pl.semaphore_signal(barrier, inc=1, device_id=near(rel), device_id_type=MESH)
+    for dz in (1, 2, 3):
+        pl.semaphore_signal(barrier, inc=1, device_id=along(dz), device_id_type=MESH)
+
+    @pl.when(moves)
+    def _():
+        pl.semaphore_signal(barrier, inc=1, device_id=partner, device_id_type=MESH)
+
+    for q in range(8):
+        for i, w in enumerate((g.wq, g.wk, g.wv)):
+            g.pq[q, :, i * W : (i + 1) * W] = w[:, q * W : (q + 1) * W].astype(BF)
+        for k in range(4):
+            at = (8 * k + q) * H4
+            g.pi[q, :, k * H4 : (k + 1) * H4] = g.win[:, at : at + H4].astype(BF)
+    g.w_out[z] = g.wout[...].astype(BF)
+    g.w_o[z, p] = g.wo[...].astype(BF)
+    g.wqkv[z, p] = g.pq[p]
+    g.w_in[z, p] = g.pi[p]
+    g.vg1[p] = g.vec[...]
+    g.bslot[z] = g.bias[...]
+
+    @pl.when(moves)
+    def _():
+        pl.semaphore_wait(barrier, 11)
+
+    @pl.when(stays)
+    def _():
+        pl.semaphore_wait(barrier, 10)
+
+    def swap(src, dst_there, dst_here):
+        copy = tx.make(src, dst_there, partner)
+
+        @pl.when(moves)
+        def _():
+            copy.start()
+
+        @pl.when(stays)
+        def _():
+            dst_here[...] = src[...]
+
+        return copy
+
+    def swap_wait(copy):
+        @pl.when(moves)
+        def _():
+            copy.wait_recv()
+
+    def gather_start(ref):
+        at = ref(p)
+        return [tx.send(at, at, near(rel)) for rel in CLASS + [SIB]]
+
+    def gather_finish(ref, copies):
+        forwards = [copies[3]]
+        for rel, copy in zip(CLASS, copies):
+            copy.wait_recv()
+            at = ref(slot(rel))
+            forwards.append(tx.send(at, at, near(SIB)))
+        for copy in forwards:
+            copy.wait_recv()
+
+    def scatter_pair(buf, first, order):
+        rel = QUADS[order]
+        return tx.send(buf(slot((rel[0], rel[1], 1))), first.at[order], near(SIB))
+
+    def scatter_add(buf, first, third, order, copy):
+        rel = QUADS[order]
+        copy.wait_recv()
+        own = buf(slot(rel))
+        own[...] = (own[...].astype(F32) + first[order].astype(F32)).astype(BF)
+        if order < 3:
+            return tx.send(own, third.at[order], near(rel))
+        return None
+
+    def scatter_total(buf, third, copies):
+        for copy in copies:
+            copy.wait_recv()
+        total = buf(p)[...].astype(F32)
+        for k in range(3):
+            total = total + third[k].astype(F32)
+        return total
+
+    swap_x = swap(g.x, g.xt, g.xt)
+    swap_m = swap(g.mem, g.xm, g.xm)
+    vec_copies = [tx.send(g.vg1.at[p], g.vg1.at[p], near(rel)) for rel in PLANE]
+    qkv_copies = [
+        tx.send(g.pq.at[slot(rel)], g.wqkv.at[z, p], near(rel)) for rel in PLANE
+    ]
+    for copy in vec_copies:
+        copy.wait_recv()
+    for k in range(2):
+        total = g.vg1[4 * k]
+        for i in range(1, 4):
+            total = total + g.vg1[4 * k + i]
+        g.vg2[z, k] = total
+    vec_copies = [tx.send(g.vg2.at[z], g.vg2.at[z], along(dz)) for dz in (1, 2, 3)]
+    bias_copies = [tx.send(g.bslot.at[z], g.bslot.at[z], along(dz)) for dz in (1, 2, 3)]
+    for copy in qkv_copies:
+        copy.wait_recv()
+    qkv_copies = [tx.send(g.wqkv.at[z], g.wqkv.at[z], along(dz)) for dz in (1, 2, 3)]
+    swap_c = swap(g.cot, g.cot_all.at[partner_slot], g.cot_all.at[p])
+    wo_copies = [tx.send(g.w_o.at[z, p], g.w_o.at[z, p], along(dz)) for dz in (1, 2, 3)]
+    for copy in vec_copies + bias_copies:
+        copy.wait_recv()
+    for k in range(8):
+        g.prm[:, k * W : (k + 1) * W] = g.vg2[k // 2, k % 2]
+    prm = g.prm
+
+    swap_wait(swap_m)
+    swap_wait(swap_x)
+    for src, at, count in ((g.xm, 0, M), (g.xt, M, T)):
+
+        def norm_rows(i, _, src=src, at=at):
+            rows = pl.ds(pl.multiple_of(i * 32, 32), 32)
+            hat, _unused = norm_parts(src[rows, :].astype(F32))
+            out = (hat * prm[0:1] + prm[1:2]).astype(BF)
+            g.n_all[p, pl.ds(pl.multiple_of(at + i * 32, 32), 32), :] = out
+            return 0
+
+        lax.fori_loop(0, count // 32, norm_rows, 0)
+    n_at = lambda q: g.n_all.at[q]
+    n_copies = gather_start(n_at)
+    win_copies = [tx.send(g.pi.at[slot(rel)], g.w_in.at[z, p], near(rel)) for rel in PLANE]
+    gather_finish(n_at, n_copies)
+    for copy in qkv_copies:
+        copy.wait_recv()
+    wout_copies = [tx.send(g.w_out.at[z], g.w_out.at[z], along(dz)) for dz in (1, 2, 3)]
+    for copy in win_copies:
+        copy.wait_recv()
+    win_copies = [tx.send(g.w_in.at[z], g.w_in.at[z], along(dz)) for dz in (1, 2, 3)]
+    for copy in wo_copies:
+        copy.wait_recv()
+    wo_at = lambda q: g.w_o.at[:, q]
+    wo_copies = gather_start(wo_at)
+    swap_wait(swap_c)
+    cot_at = lambda q: g.cot_all.at[q]
+    cot_copies = gather_start(cot_at)
+
+    wqkv = flat(g.wqkv[...].reshape(32, D32, 3 * W))
+    own_vec = g.vg2[p // 2, p % 2]
+    qkv_bias = jnp.concatenate(
+        [own_vec[2:3], jnp.zeros((1, W), F32), own_vec[3:4]], axis=1
+    )
+
+    def project(i, _):
+        rows = flat(g.n_all[pl.ds(2 * i, 2)])
+        out = dot(rows, wqkv) + qkv_bias
+        g.qkv[pl.ds(2 * i, 2)] = out.astype(BF).reshape(2, R, 3 * W)
+        return 0
+
+    lax.fori_loop(0, 4, project, 0)
+
+    place = [
+        g.order[2 * (qy + qc * (3 - 2 * qy)) + qx]
+        for qx in (0, 1)
+        for qy in (0, 1)
+        for qc in (0, 1)
+    ]
+
+    def pick(blocks, wanted):
+        out = blocks[0]
+        for block, (left, right) in zip(blocks[1:], wanted[1:]):
+            out = jnp.where(jnp.full(out.shape, left, jnp.int32) == right, block, out)
+        return out
+
+    def to_sorted(load, store):
+        def step(i, _):
+            at = pl.multiple_of(i * 16, 16)
+            blocks = [load(q, at).astype(F32) for q in range(8)]
+            for j in range(8):
+                store(j, at, pick(blocks, [(place[q], j) for q in range(8)]))
+            return 0
+
+        lax.fori_loop(0, T // 16, step, 0)
+
+    def from_sorted(load, store):
+        def step(i, _):
+            at = pl.multiple_of(i * 16, 16)
+            blocks = [load(j, at).astype(F32) for j in range(8)]
+            for q in range(8):
+                store(q, at, pick(blocks, [(place[q], j) for j in range(8)]))
+            return 0
+
+        lax.fori_loop(0, T // 16, step, 0)
+
+    def store_qkv(j, at, rows):
+        g.qs[pl.ds(j * T + at, 16), :] = (rows[:, :W] * 0.125).astype(BF)
+        g.kk[pl.ds(MK + j * T + at, 16), :] = rows[:, W : 2 * W].astype(BF)
+        g.vv[pl.ds(MK + j * T + at, 16), :] = rows[:, 2 * W :].astype(BF)
+
+    to_sorted(lambda q, at: g.qkv[q, pl.ds(M + at, 16), :], store_qkv)
+    for j in range(8):
+        g.kk[j * M : (j + 1) * M, :] = g.qkv[j, :M, W : 2 * W]
+        g.vv[j * M : (j + 1) * M, :] = g.qkv[j, :M, 2 * W :]
+
+    B = 2 * T
+    lane = lax.broadcasted_iota(jnp.int32, (B, W), 1)
+    head_lanes = [lane < W // 2, lane >= W // 2]
+    below = lax.broadcasted_iota(jnp.int32, (B, B), 1) <= lax.broadcasted_iota(
+        jnp.int32, (B, B), 0
+    )
+
+    def only(value, h):
+        return jnp.where(head_lanes[h], value, jnp.zeros_like(value))
+
+    for i in range(S // B):
+        rows = slice(i * B, (i + 1) * B)
+        past = MK + i * B
+        end = past + B
+        q_rows = g.qs[rows, :]
+        parts = []
+        for h in range(2):
+            qh = only(q_rows, h)
+            s0 = dot_nt(qh, g.kk[:past, :])
+            s1 = dot_nt(qh, g.kk[past:end, :])
+            s1 = jnp.where(below, s1, -1e30)
+            top = jnp.maximum(
+                jnp.max(s0, axis=1, keepdims=True), jnp.max(s1, axis=1, keepdims=True)
+            )
+            e0 = jnp.exp(s0 - top)
+            e1 = jnp.exp(s1 - top)
+            total = jnp.sum(e0, axis=1, keepdims=True) + jnp.sum(e1, axis=1, keepdims=True)
+            scale = 1.0 / total
+            w0 = (e0 * scale).astype(BF)
+            w1 = (e1 * scale).astype(BF)
+            g.wts[h, rows, :past] = w0
+            g.wts[h, rows, past:end] = w1
+            parts.append(dot(w0, g.vv[:past, :]) + dot(w1, g.vv[past:end, :]))
+        g.ctx[rows, :] = jnp.where(head_lanes[0], parts[0], parts[1])
+
+    def store_ctx(q, at, rows):
+        g.ctx_send[q, pl.ds(at, 16), :] = rows.astype(BF)
+
+    from_sorted(lambda j, at: g.ctx[pl.ds(j * T + at, 16), :], store_ctx)
+    ctx_copies = [tx.send(g.ctx_send.at[slot(rel)], g.ctx_own.at[p], near(rel)) for rel in PLANE]
+    g.ctx_own[p] = g.ctx_send[p]
+    gather_finish(wo_at, wo_copies)
+    gather_finish(cot_at, cot_copies)
+    for copy in ctx_copies:
+        copy.wait_recv()
+    for q in range(8):
+        g.ctx2d[:, q * W : (q + 1) * W] = g.ctx_own[q]
+    w_o = lambda: flat(g.w_o[...].reshape(32, D32, D))
+    g.mid[...] = dot(g.ctx2d[...], w_o()) + g.xt[...].astype(F32) + prm[4:5]
+
+    def norm_mid(i, _):
+        rows = pl.ds(pl.multiple_of(i * 32, 32), 32)
+        hat, _unused = norm_parts(g.mid[rows, :])
+        g.n2_all[p, rows, :] = (hat * prm[5:6] + prm[6:7]).astype(BF)
+        return 0
+
+    lax.fori_loop(0, T // 32, norm_mid, 0)
+    n2_at = lambda q: g.n2_all.at[q]
+    n2_copies = gather_start(n2_at)
+    gather_finish(n2_at, n2_copies)
+    for copy in wout_copies + win_copies:
+        copy.wait_recv()
+
+    hidden_bias = jnp.concatenate([g.bslot[k, 0:1, :] for k in range(4)], axis=1)
+    pb_a = lambda q: g.pb_a.at[q]
+    pb_b = lambda q: g.pb_b.at[q]
+    sib_a, sib_b, class_a, class_b = [], [], [], []
+    for order in range(4):
+        rel = QUADS[order]
+        pair = 4 * ((x + rel[0]) % 2) + 2 * ((y + rel[1]) % 2)
+        w_in = flat(g.w_in[...].reshape(32, D32, H))
+        w_out = flat(g.w_out[...])
+        inner = dot(flat(g.n2_all[pl.ds(pair, 2)]), w_in) + hidden_bias
+        act, slope = gelu_parts(inner)
+        act = act.astype(BF)
+        act_grad = dot_nt(flat(g.cot_all[pl.ds(pair, 2)]), w_out)
+        inner_grad = (act_grad * slope).astype(BF)
+        at = pl.ds(pl.multiple_of(pair * T, 2 * T), 2 * T)
+        g.inner[at, :] = inner_grad
+        for k in range(4):
+            g.act[k, at, :] = act[:, k * H4 : (k + 1) * H4]
+        g.pb_b[pl.ds(pair, 2)] = dot_nt(inner_grad, w_in).astype(BF).reshape(2, T, D)
+        sib_b.append(scatter_pair(pb_b, g.r1_b, order))
+        g.pb_a[pl.ds(pair, 2)] = dot(act, w_out).astype(BF).reshape(2, T, D)
+        if order:
+            class_b.append(scatter_add(pb_b, g.r1_b, g.r3_b, order - 1, sib_b[order - 1]))
+    scatter_add(pb_b, g.r1_b, g.r3_b, 3, sib_b[3])
+    for order in range(4):
+        sib_a.append(scatter_pair(pb_a, g.r1_a, order))
+    for order in range(4):
+        class_a.append(scatter_add(pb_a, g.r1_a, g.r3_a, order, sib_a[order]))
+
+    gout_copies, gin_copies, gb_copies = [], [], []
+    cot = lambda: flat(g.cot_all[...])
+    inner_sum = col_sum(g.inner[...])
+    for k in range(4):
+        g.bp[k] = jnp.broadcast_to(inner_sum[:, k * H4 : (k + 1) * H4], (8, H4))
+    for dz in (1, 2, 3, 0):
+        to = (z + dz) % 4
+        grad = dot_tn(g.act[to], cot())
+        if dz:
+            g.gout_s[to] = grad.astype(BF)
+            gout_copies.append(tx.send(g.gout_s.at[to], g.gout_r.at[dz - 1], along(dz)))
+            gb_copies.append(tx.send(g.bp.at[to], g.br.at[dz - 1], along(dz)))
+        else:
+            g.gout_own[...] = grad
+    for dz in (1, 2, 3, 0):
+        to = (z + dz) % 4
+        cols = pl.ds(pl.multiple_of(to * Q, Q), Q)
+        grad = dot_tn(flat(g.n2_all[:, :, cols]), g.inner[...])
+        if dz:
+            g.gin_s[to] = grad.astype(BF).reshape(8, D32, H)
+            gin_copies.append(tx.send(g.gin_s.at[to], g.gin_r.at[dz - 1], along(dz)))
+        else:
+            g.gin_own[...] = grad
+
+    g.mg[...] = scatter_total(pb_b, g.r3_b, class_b[:3])
+
+    def norm_two_back(i, sums):
+        rows = pl.ds(pl.multiple_of(i * 32, 32), 32)
+        up = g.mg[rows, :]
+        hat, scale = norm_parts(g.mid[rows, :])
+        pull = up * prm[5:6]
+        mean = jnp.mean(pull, axis=-1, keepdims=True)
+        along_hat = jnp.mean(pull * hat, axis=-1, keepdims=True)
+        cot_rows = g.cot_all[p, rows, :].astype(F32)
+        out = cot_rows + scale * (pull - mean - hat * along_hat)
+        low = out.astype(BF)
+        g.mg[rows, :] = out
+        g.attg[rows, :] = low
+        return (
+            sums[0] + col_sum(up * hat),
+            sums[1] + col_sum(up),
+            sums[2] + col_sum(low),
+            sums[3] + col_sum(cot_rows),
+        )
+
+    zero_row = jnp.zeros((1, D), F32)
+    gain_two, shift_two, bias_o, bias_out = lax.fori_loop(
+        0, T // 32, norm_two_back, (zero_row, zero_row, zero_row, zero_row)
+    )
+    attg = g.attg[...]
+    cg = dot_nt(attg, w_o()).astype(BF)
+    for q in range(8):
+        g.cg_send[q] = cg[:, q * W : (q + 1) * W]
+    cg_copies = [tx.send(g.cg_send.at[slot(rel)], g.cg_all.at[p], near(rel)) for rel in PLANE]
+    g.cg_all[p] = g.cg_send[p]
+
+    go_at = lambda q: g.go_buf.at[:, q]
+    for k in range(4):
+        grad = dot_tn(g.ctx2d[:, k * Q : (k + 1) * Q], attg)
+        g.go_buf[k] = grad.astype(BF).reshape(8, D32, D)
+    sib_o = [scatter_pair(go_at, g.go_r1, order) for order in range(4)]
+    class_o = [scatter_add(go_at, g.go_r1, g.go_r3, order, sib_o[order]) for order in range(4)]
+
+    for copy in cg_copies:
+        copy.wait_recv()
+
+    def store_cg(j, at, rows):
+        g.cg_sorted[pl.ds(j * T + at, 16), :] = rows.astype(BF)
+
+    to_sorted(lambda q, at: g.cg_all[q, pl.ds(at, 16), :], store_cg)
+    g.dk[...] = jnp.zeros_like(g.dk)
+    g.dv[...] = jnp.zeros_like(g.dv)
+    for i in range(S // B):
+        rows = slice(i * B, (i + 1) * B)
+        end = MK + (i + 1) * B
+        cg_rows = g.cg_sorted[rows, :]
+        q_rows = g.qs[rows, :]
+        product = cg_rows.astype(F32) * g.ctx[rows, :]
+        parts = []
+        for h in range(2):
+            qh, ch = only(q_rows, h), only(cg_rows, h)
+            delta = jnp.sum(only(product, h), axis=1, keepdims=True)
+            w = g.wts[h, rows, :end]
+            pull = dot_nt(ch, g.vv[:end, :])
+            ds = (w.astype(F32) * (pull - delta)).astype(BF)
+            parts.append(dot(ds, g.kk[:end, :]))
+            g.dk[:end, :] += dot_tn(ds, qh)
+            g.dv[:end, :] += dot_tn(w, ch)
+        g.dq[rows, :] = jnp.where(head_lanes[0], parts[0], parts[1]) * 0.125
+
+    def load_grads(j, at):
+        keys = pl.ds(MK + j * T + at, 16)
+        return jnp.concatenate(
+            [g.dq[pl.ds(j * T + at, 16), :], g.dk[keys, :], g.dv[keys, :]], axis=1
+        )
+
+    def store_grads(q, at, rows):
+        g.dqkv[q, pl.ds(M + at, 16), :] = rows.astype(BF)
+
+    from_sorted(load_grads, store_grads)
+    for q in range(8):
+        mt = slice(q * M, (q + 1) * M)
+        g.dqkv[q, :M, :W] = jnp.zeros((M, W), BF)
+        g.dqkv[q, :M, W : 2 * W] = g.dk[mt, :].astype(BF)
+        g.dqkv[q, :M, 2 * W :] = g.dv[mt, :].astype(BF)
+
+    lo = scatter_total(pb_a, g.r3_a, class_a[:3]) + g.mid[...] + prm[7:8]
+    g.lo_s[...] = lo.astype(BF)
+    swap_lo = swap(g.lo_s, g.lo, g.lo)
+    go_total = scatter_total(go_at, g.go_r3, class_o[:3])
+    g.go_sum[...] = go_total.astype(BF)
+    go_copies = [
+        tx.send(g.go_sum.at[(z + dz) % 4], g.go_z.at[dz - 1], along(dz)) for dz in (1, 2, 3)
+    ]
+
+    sib_n, class_n = [], []
+    for order in range(4):
+        rel = QUADS[order]
+        pair = 4 * ((x + rel[0]) % 2) + 2 * ((y + rel[1]) % 2)
+        rows = flat(g.dqkv[pl.ds(pair, 2), M:, :])
+        w = flat(g.wqkv[...].reshape(32, D32, 3 * W))
+        g.pb_n[pl.ds(pair, 2)] = dot_nt(rows, w).astype(BF).reshape(2, T, D)
+        sib_n.append(scatter_pair(lambda q: g.pb_n.at[q], g.r1_n, order))
+        if order:
+            class_n.append(
+                scatter_add(lambda q: g.pb_n.at[q], g.r1_n, g.r3_n, order - 1, sib_n[order - 1])
+            )
+    scatter_add(lambda q: g.pb_n.at[q], g.r1_n, g.r3_n, 3, sib_n[3])
+
+    g.vp[...] = jnp.zeros_like(g.vp)
+    qkv_sum = jnp.zeros((1, 3 * W), F32)
+    for q in range(8):
+        qkv_sum = qkv_sum + col_sum(g.dqkv[q])
+    qkv_sum8 = jnp.broadcast_to(qkv_sum, (8, 3 * W))
+    ones = jnp.ones((8, 3 * W), F32)
+    gqkv_copies = []
+    for dz in (1, 2, 3, 0):
+        to = (z + dz) % 4
+        cols = pl.ds(pl.multiple_of(to * Q, Q), Q)
+        grad = dot_tn(flat(g.n_all[:, :, cols]), flat(g.dqkv[...]))
+        if dz:
+            g.gqkv_s[to] = grad.astype(BF).reshape(8, D32, 3 * W)
+            gqkv_copies.append(tx.send(g.gqkv_s.at[to], g.gqkv_r.at[dz - 1], along(dz)))
+        else:
+            g.gqkv_own[...] = grad
+        w = flat(g.wqkv[to]).astype(F32)
+        gains = dot_nt(ones, grad * w, EXACT)
+        shifts = dot_nt(qkv_sum8, w, EXACT)
+        for k in range(2):
+            at = slice(k * W, (k + 1) * W)
+            shift = shifts[0:1, at]
+            vec = g.vg2[to, k]
+            g.vp[2 * to + k, 0:1, :] = (gains[0:1, at] - vec[1:2] * shift) / vec[0:1]
+            g.vp[2 * to + k, 1:2, :] = shift
+    g.vp[p, 2:3, :] = qkv_sum[:, :W]
+    g.vp[p, 3:4, :] = qkv_sum[:, 2 * W :]
+    for k in range(8):
+        at = slice(k * W, (k + 1) * W)
+        g.vp[k, 4:5, :] = bias_o[:, at]
+        g.vp[k, 5:6, :] = gain_two[:, at]
+        g.vp[k, 6:7, :] = shift_two[:, at]
+        g.vp[k, 7:8, :] = bias_out[:, at]
+    vec_copies = [
+        tx.send(g.vp.at[pl.ds(2 * ((z + dz) % 4), 2)], g.vr.at[dz - 1], along(dz))
+        for dz in (1, 2, 3)
+    ]
+
+    for copy in gout_copies + gb_copies + gin_copies + go_copies:
+        copy.wait_recv()
+    g.gout[...] = g.gout_own[...] + sum(g.gout_r[k].astype(F32) for k in range(3))
+    g.gbin[...] = g.bp[z] + g.br[0] + g.br[1] + g.br[2]
+    total = g.gin_own[...] + sum(flat(g.gin_r[k]).astype(F32) for k in range(3))
+    g.gin_a[...] = total.astype(BF).reshape(8, D32, H)
+    gin_copies = [tx.send(g.gin_a.at[slot(rel)], g.gin_b.at[p], near(rel)) for rel in PLANE]
+    g.gin_b[p] = g.gin_a[p]
+    g.go[...] = g.go_sum[z].astype(F32) + sum(g.go_z[k].astype(F32) for k in range(3))
+
+    g.mid[...] = scatter_total(lambda q: g.pb_n.at[q], g.r3_n, class_n[:3])
+
+    def norm_one_back(i, _):
+        rows = pl.ds(pl.multiple_of(i * 32, 32), 32)
+        hat, scale = norm_parts(g.xt[rows, :].astype(F32))
+        pull = g.mid[rows, :] * prm[0:1]
+        mean = jnp.mean(pull, axis=-1, keepdims=True)
+        along_hat = jnp.mean(pull * hat, axis=-1, keepdims=True)
+        out = g.mg[rows, :] + scale * (pull - mean - hat * along_hat)
+        g.ig_s[rows, :] = out.astype(BF)
+        return 0
+
+    lax.fori_loop(0, T // 32, norm_one_back, 0)
+    swap_ig = swap(g.ig_s, g.ig, g.ig)
+
+    for copy in gqkv_copies + vec_copies:
+        copy.wait_recv()
+    total = g.gqkv_own[...] + sum(flat(g.gqkv_r[k]).astype(F32) for k in range(3))
+    g.gqkv_a[...] = total.astype(BF).reshape(8, D32, 3 * W)
+    gqkv_copies = [tx.send(g.gqkv_a.at[slot(rel)], g.gqkv_b.at[p], near(rel)) for rel in PLANE]
+    g.gqkv_b[p] = g.gqkv_a[p]
+    g.vs[...] = g.vp[pl.ds(2 * z, 2)] + g.vr[0] + g.vr[1] + g.vr[2]
+    vec_copies = [tx.send(g.vs.at[(x + rel[0]) % 2], g.va.at[p], near(rel)) for rel in PLANE]
+    g.va[p] = g.vs[x]
+
+    for copy in gin_copies:
+        copy.wait_recv()
+    for q in range(8):
+        for k in range(4):
+            at = (8 * k + q) * H4
+            g.gin[:, at : at + H4] = g.gin_b[q, :, k * H4 : (k + 1) * H4].astype(F32)
+    for copy in gqkv_copies + vec_copies:
+        copy.wait_recv()
+    for q in range(8):
+        for i, out in enumerate((g.gq, g.gk, g.gv)):
+            out[:, q * W : (q + 1) * W] = g.gqkv_b[q, :, i * W : (i + 1) * W].astype(F32)
+    total = g.va[0]
+    for q in range(1, 8):
+        total = total + g.va[q]
+    g.gvec[...] = total
+
+    for copy in (swap_lo, swap_ig):
+        swap_wait(copy)
+    tx.drain()
+
+    @pl.when(moves)
+    def _():
+        for copy in (swap_x, swap_m, swap_c, swap_lo, swap_ig):
+            copy.wait_send()
+
+
+def run_layer(layer_input, memory, cotangent, block_order, w_query, w_key, w_value, w_output, w_in, w_out, vectors, b_in):
+    T, D = layer_input.shape[1:]
+    M = memory.shape[1]
+    FF = w_in.shape[1]
+    W = D // 8
+    share = vectors.shape[1]
+    low = vectors.astype(BF).astype(F32)
+    lanes = lax.broadcasted_iota(jnp.int32, (8, W), 1) // share
+    mine = lanes == lax.axis_index("dp")
+    vec = jnp.where(mine, jnp.tile(low, (1, W // share)), 0.0)
+    bias = jnp.broadcast_to(b_in.astype(BF).astype(F32)[None], (8, b_in.shape[0]))
+    shapes = scratch_list(T, M, D, FF)
+    vmem = pl.BlockSpec(memory_space=pltpu.VMEM)
+    smem = pl.BlockSpec(memory_space=pltpu.SMEM)
+    outs = pl.pallas_call(
+        functools.partial(layer_kernel, T, M, D, FF),
+        out_shape=(
+            jax.ShapeDtypeStruct((T, D), BF),
+            jax.ShapeDtypeStruct((T, D), BF),
+            jax.ShapeDtypeStruct(w_query.shape, F32),
+            jax.ShapeDtypeStruct(w_key.shape, F32),
+            jax.ShapeDtypeStruct(w_value.shape, F32),
+            jax.ShapeDtypeStruct(w_output.shape, F32),
+            jax.ShapeDtypeStruct(w_in.shape, F32),
+            jax.ShapeDtypeStruct(w_out.shape, F32),
+            jax.ShapeDtypeStruct((8, W), F32),
+            jax.ShapeDtypeStruct((8, b_in.shape[0]), F32),
+        ),
+        in_specs=[vmem, vmem, vmem, smem] + [vmem] * 8,
+        out_specs=[vmem] * 10,
+        scratch_shapes=[pltpu.VMEM(shape, kind) for shape, kind in shapes.values()]
+        + [pltpu.SemaphoreType.DMA((SEMS,)), pltpu.SemaphoreType.DMA((SEMS,))],
+        compiler_params=pltpu.CompilerParams(
+            collective_id=0, has_side_effects=True, vmem_limit_bytes=63 * 2**20
+        ),
+    )(layer_input[0], memory[0], cotangent[0], block_order, w_query, w_key, w_value, w_output, w_in, w_out, vec, bias)
+    lo, ig, gq, gk, gv, go, gin, gout, gvec, gbin = outs
+    gvec = lax.dynamic_slice(gvec, (0, lax.axis_index("dp") * share), (8, share))
+    return (lo[None], ig.astype(F32)[None], gq, gk, gv, go, gin, gout, gvec, gbin[0])
 
 
 masked_value = -1e30
@@ -199,7 +952,7 @@
     grad_outer = contract_rows(activated, upstream)
     grad_outer_bias = jnp.sum(upstream_full, axis=0)
     act_grad = times_transposed(upstream, outer_full)
-    _, gelu_back = jax.vjp(partial(jax.nn.gelu, approximate=True), inner)
+    _, gelu_back = jax.vjp(functools.partial(jax.nn.gelu, approximate=True), inner)
     inner_grad = gelu_back(act_grad)[0].astype(bf16)
     grad_inner = contract_rows(normed_two, inner_grad)
     grad_inner_bias = jnp.sum(inner_grad.astype(jnp.float32), axis=0)
@@ -338,34 +1091,15 @@
 
 
 def solution(mesh):
+    rows = P("dp", "blk", None)
+    shard = P(("blk", "dp"), None)
+    in_specs = (rows, rows, rows, P()) + (shard,) * 6 + (P(None, ("blk", "dp")), P(("blk", "dp")))
+    out_specs = (rows, rows) + (shard,) * 6 + (P(None, ("blk", "dp")), P(("blk", "dp")))
+    planes = mesh.shape["blk"] == 8 and mesh.shape["dp"] == 4
     return jax.shard_map(
-        per_device,
+        run_layer if planes else per_device,
         mesh=mesh,
-        in_specs=(
-            P("dp", "blk", None),
-            P("dp", "blk", None),
-            P("dp", "blk", None),
-            P(),
-            P(("blk", "dp"), None),
-            P(("blk", "dp"), None),
-            P(("blk", "dp"), None),
-            P(("blk", "dp"), None),
-            P(("blk", "dp"), None),
-            P(("blk", "dp"), None),
-            P(None, ("blk", "dp")),
-            P(("blk", "dp")),
-        ),
-        out_specs=(
-            P("dp", "blk", None),
-            P("dp", "blk", None),
-            P(("blk", "dp"), None),
-            P(("blk", "dp"), None),
-            P(("blk", "dp"), None),
-            P(("blk", "dp"), None),
-            P(("blk", "dp"), None),
-            P(("blk", "dp"), None),
-            P(None, ("blk", "dp")),
-            P(("blk", "dp")),
-        ),
+        in_specs=in_specs,
+        out_specs=out_specs,
         check_vma=False,
     )

time: 1960 us -> 211 us (0.11)
  waiting for transfers between devices: 1540 us -> 0 us
  Pallas kernels: 0 us -> 198 us
  blocking collectives: 120 us -> 0 us
  matrix products: 111 us -> 0 us
  local copies, waits for them, and re-layouts: 93.8 us -> 9.22 us
  other arithmetic: 52.2 us -> 2.45 us
    reduce_scatter x6 -> x0, waiting for transfers between devices: 927 us -> none  [the longest x1 187 us: per_device(): lax.psum_scatter(grad_outer, ('blk', 'dp'), scatter_dimension=0, tiled=True)]
    all_gather x8 -> x0, waiting for transfers between devices: 378 us -> none  [the longest x1 76.9 us: per_device(): lax.all_gather(w_in.astype(bf16), ('blk', 'dp'), axis=0, tiled=True)]
    pallas_call x0 -> x1, Pallas kernels: none -> 198 us  [run_layer(): pl.pallas_call(functools.partial(layer_kernel, T, M, D, FF), out_shape=(j...]
    ppermute x15 -> x0, waiting for transfers between devices: 177 us -> none  [passed_along(): return lax.ppermute(block, axis, route)]
    dot_general x92 -> x0, matrix products: 111 us -> none  [the longest x6 27.2 us: contract_rows(): lax.dot_general(left, right, (((0,), (0,)), ((), ())), preferred_element_...]
    all_gather x2 -> x0, blocking collectives: 82.6 us -> none  [the longest x1 43.4 us: per_device(): lax.all_gather(vectors.astype(bf16), ('blk', 'dp'), axis=1, tiled=True)]
    unnamed x16 -> x0, waiting for transfers between devices: 56.9 us -> none
    unnamed x1 -> x0, blocking collectives: 37 us -> none
  transfers between devices with their start and end apart: 30 -> 0, of which waited for: 27 -> 0; matrix products, arithmetic and copies ran while one was open for 11% -> 0% of each run, Pallas kernels for 0% -> 0%
where the time goes in v1:
time: 211 us; the launch traced here: 210 us
  Pallas kernels  198 us (94%)
  local copies, waits for them, and re-layouts  9.22 us (4%)
  other arithmetic  2.45 us (1%)
    pallas_call x1, Pallas kernels, run_layer(): pl.pallas_call(functools.partial(layer_kernel, T, M, D, FF), out_shape=(j...  198 us
    unnamed x27, local copies, waits for them, and re-layouts  6.68 us

profile of v1, /device:TPU:0, one launch (start us, length us, event | category | flops | bytes accessed | tf_op | source)
XLA Modules:
  0.0 210.3 jit_solution(10795728906635165403)
XLA Ops:
  0.6 0.0 copy-start.9
  0.7 0.6 copy-done.9
  1.3 0.0 copy-start.7
  1.3 0.6 broadcast_in_dim.20.refs_11_
  1.9 0.1 copy-done.7
  2.0 0.1 tile.10
  2.1 0.6 fusion.refs_10_
  2.7 198.0 %shard_map.195 = (bf16[128,1024]{1,0:T(8,128)(2,1)}, bf16[128,1024]{1,0:T(8,128)(2,1)}, f32[32,1024]{1,0:T(8,128)}, f32[32,1024]{1,0:T(8,128)}, f32[32,1024]{1,0...) custom-call(bf16[128,1024]{1,0:T(8,128)(2,1)} %bitcast.9, ...), custom_call_target="tpu_custom_call" | custom-call | tf_op jit(solution)/shard_map/pallas_call | solution.py:737
  200.7 0.0 copy-start.8
  200.7 1.2 slice_bitcast_fusion
  201.9 0.0 copy-done.8
  201.9 0.7 constant_dynamic-slice_fusion
  202.6 0.0 copy-start.2
  202.6 1.8 bitcast_convert_fusion
  204.4 0.0 copy-done.2
  204.4 0.0 copy-start.6
  204.4 0.0 copy-start.5
  204.4 0.0 copy-start.4
  204.4 0.7 copy.29
  205.1 0.3 copy-done.6
  205.4 0.0 copy-start.1
  205.4 0.7 copy.30
  206.1 0.0 copy-done.5
  206.1 0.7 copy.31
  206.7 0.0 copy-done.4
  206.7 0.0 copy-start.3
  206.7 0.7 copy.32
  207.4 0.3 copy-done.3
  207.7 0.7 copy.33
  208.3 0.0 copy-done.1
  208.3 0.0 copy-start
  208.3 0.8 copy.34
  209.1 0.4 copy-done
  209.6 0.8 copy.35
  (5 shorter events, 0.0 us)
Async XLA Ops:
  0.6 0.7 copy-start.9
  1.3 0.7 copy-start.7
  200.7 1.2 copy-start.8
  202.6 1.8 copy-start.2
  204.4 1.0 copy-start.6
  204.4 1.7 copy-start.5
  204.4 2.3 %copy-start.4 = (f32[32,1024]{1,0:T(8,128)S(1)}, f32[32,1024]{1,0:T(8,128)}, u32[]{:S(2)}) copy-start(f32[32,1024]{1,0:T(8,128)} %get-tuple-element.46) | copy-start | bytes 393220
  205.4 2.9 %copy-start.1 = (f32[32,4096]{1,0:T(8,128)S(1)}, f32[32,4096]{1,0:T(8,128)}, u32[]{:S(2)}) copy-start(f32[32,4096]{1,0:T(8,128)} %get-tuple-element.48) | copy-start | bytes 1572868
  206.7 1.0 copy-start.3
  208.3 1.2 copy-start

commit v2 on v1

--- a/solution.py
+++ b/solution.py
@@ -53,34 +53,41 @@
 
 IN_NAMES = ["x", "mem", "cot", "order", "wq", "wk", "wv", "wo", "win", "wout", "vec", "bias"]
 OUT_NAMES = ["lo", "ig", "gq", "gk", "gv", "go", "gin", "gout", "gvec", "gbin"]
-PLANE = [(1, 1, 1), (1, 1, 0), (1, 0, 1), (1, 0, 0), (0, 1, 1), (0, 1, 0), (0, 0, 1)]
-CLASS = [(1, 1, 0), (1, 0, 0), (0, 1, 0)]
-QUADS = CLASS + [(0, 0, 0)]
-SIB = (0, 0, 1)
+TEAM = [(1, 1, 1), (1, 1, 0), (1, 0, 1), (1, 0, 0), (0, 1, 1), (0, 1, 0), (0, 0, 1)]
+FAR = [(1, 0), (0, 1), (1, 1)]
+QUADS = [(1, 1, 0), (0, 1, 0), (1, 0, 0), (0, 0, 0)]
+SIB, XN, ZN = (0, 0, 1), (0, 1, 0), (1, 0, 0)
 
 
 def scratch_list(T, M, D, FF):
     R = T + M
     H = FF // 8
-    Q = D // 4
+    H4 = H // 4
     W = D // 8
+    B = D // 32
     S = 8 * T
     K = 8 * R
+    grid = (2, 4, 2, 2, B)
     return dict(
+        f_qkv=((3, B, D), F32),
+        f_o=((B, D), F32),
+        f_in=((B, FF), F32),
+        f_out=((H4, D), F32),
         n_all=((8, R, D), BF),
         xm=((M, D), BF),
         xt=((T, D), BF),
         cot_all=((8, T, D), BF),
         n2_all=((8, T, D), BF),
-        pq=((8, D // 32, 3 * W), BF),
-        pi=((8, D // 32, H), BF),
-        wqkv=((4, 8, D // 32, 3 * W), BF),
-        w_in=((4, 8, D // 32, H), BF),
-        w_out=((4, H // 4, D), BF),
-        w_o=((4, 8, D // 32, D), BF),
+        pq=((8, B, 3 * W), BF),
+        pi=((8, B, H), BF),
+        wqkv=(grid + (3 * W,), BF),
+        w_in=(grid + (H,), BF),
+        w_out=((2, 2, H4, D), BF),
+        w_o=(grid + (D,), BF),
         vg1=((8, 8, W), F32),
-        vg2=((4, 2, 8, W), F32),
-        bslot=((4, 8, H // 4), F32),
+        vg2=((4, 4, 8, W), F32),
+        pg=((8, 8, W), F32),
+        bslot=((4, 8, H4), F32),
         prm=((8, D), F32),
         qkv=((8, R, 3 * W), BF),
         qs=((S, W), BF),
@@ -92,56 +99,65 @@
         ctx_own=((8, T, W), BF),
         ctx2d=((T, D), BF),
         mid=((T, D), F32),
-        act=((4, S, H // 4), BF),
+        act=((4, S, H4), BF),
         inner=((S, H), BF),
         pb_a=((8, T, D), BF),
         r1_a=((4, T, D), BF),
-        r3_a=((3, T, D), BF),
+        rx_a=((2, T, D), BF),
+        rz_a=((T, D), BF),
         pb_b=((8, T, D), BF),
         r1_b=((4, T, D), BF),
-        r3_b=((3, T, D), BF),
+        rx_b=((2, T, D), BF),
+        rz_b=((T, D), BF),
         pb_n=((8, T, D), BF),
         r1_n=((4, T, D), BF),
-        r3_n=((3, T, D), BF),
+        rx_n=((2, T, D), BF),
+        rz_n=((T, D), BF),
         mg=((T, D), F32),
         attg=((T, D), BF),
         cg_send=((8, T, W), BF),
         cg_all=((8, T, W), BF),
-        go_buf=((4, 8, D // 32, D), BF),
-        go_r1=((4, 4, D // 32, D), BF),
-        go_r3=((3, 4, D // 32, D), BF),
-        go_sum=((4, D // 32, D), BF),
-        go_z=((3, D // 32, D), BF),
+        pb_o=(grid + (D,), BF),
+        r1_o=((4, 2, 2, B, D), BF),
+        rx_o=((2, 2, 2, B, D), BF),
+        rz_o=((2, 2, B, D), BF),
+        go_s=((2, 2, B, D), BF),
+        go_a=((2, B, D), BF),
+        go_b=((B, D), BF),
+        go_c=((B, D), BF),
         cg_sorted=((S, W), BF),
         dq=((S, W), F32),
         dk=((K, W), F32),
         dv=((K, W), F32),
         dqkv=((8, R, 3 * W), BF),
-        gout_s=((4, H // 4, D), BF),
-        gout_own=((H // 4, D), F32),
-        gout_r=((3, H // 4, D), BF),
-        gin_s=((4, 8, D // 32, H), BF),
-        gin_own=((Q, H), F32),
-        gin_r=((3, 8, D // 32, H), BF),
-        gin_a=((8, D // 32, H), BF),
-        gin_b=((8, D // 32, H), BF),
-        gqkv_s=((4, 8, D // 32, 3 * W), BF),
-        gqkv_own=((Q, 3 * W), F32),
-        gqkv_r=((3, 8, D // 32, 3 * W), BF),
-        gqkv_a=((8, D // 32, 3 * W), BF),
-        gqkv_b=((8, D // 32, 3 * W), BF),
+        gout_s=((2, 2, H4, D), BF),
+        gout_a=((2, H4, D), BF),
+        gout_b=((H4, D), BF),
+        gout_c=((H4, D), BF),
+        gin_s=(grid + (H,), BF),
+        gin_a=((2, 4, 2, B, H), BF),
+        gin_b=((4, 2, B, H), BF),
+        gin_c=((4, 2, B, H), BF),
+        gin_d=((8, B, H), BF),
+        gin_e=((8, B, H), BF),
+        gqkv_s=(grid + (3 * W,), BF),
+        gqkv_a=((2, 4, 2, B, 3 * W), BF),
+        gqkv_b=((4, 2, B, 3 * W), BF),
+        gqkv_c=((4, 2, B, 3 * W), BF),
+        gqkv_d=((8, B, 3 * W), BF),
+        gqkv_e=((8, B, 3 * W), BF),
         vp=((8, 8, W), F32),
-        vr=((3, 2, 8, W), F32),
-        vs=((2, 8, W), F32),
+        vr=((3, 4, 8, W), F32),
+        vs=((4, 8, W), F32),
         va=((8, 8, W), F32),
-        bp=((4, 8, H // 4), F32),
-        br=((3, 8, H // 4), F32),
+        bp=((4, 8, H4), F32),
+        br=((3, 8, H4), F32),
         lo_s=((T, D), BF),
         ig_s=((T, D), BF),
     )
 
 
-SEMS = 200
+SEMS = 320
 
 
 class Sender:
@@ -160,6 +176,13 @@
             device_id_type=MESH,
         )
 
+    def local(self, src, dst):
+        at = self.count
+        self.count += 1
+        copy = pltpu.make_async_copy(src, dst, self.rsem.at[at])
+        copy.start()
+        return copy
+
     def send(self, src, dst, target):
         copy = self.make(src, dst, target)
         copy.start()
@@ -171,62 +194,137 @@
             copy.wait_send()
 
 
-def layer_kernel(T, M, D, FF, *refs):
+class TeamGather:
+    def __init__(self, tx, near, slot, ref):
+        self.tx, self.near, self.slot, self.ref = tx, near, slot, ref
+        self.sib, self.zn, self.xn, self.diag = [], {}, {}, {}
+
+    def pass_on(self, rel, half, to):
+        at = self.ref(self.slot(rel), half)
+        return self.tx.send(at, at, self.near(to))
+
+    def start(self, half):
+        own = (0, 0, 0)
+        self.zn[half] = self.pass_on(own, half, ZN)
+        self.xn[half] = self.pass_on(own, half, XN)
+        self.sib.append(self.pass_on(own, half, SIB))
+
+    def forward(self, half):
+        self.zn[half].wait_recv()
+        self.diag[half] = self.pass_on(ZN, half, XN)
+        self.sib.append(self.pass_on(ZN, half, SIB))
+
+    def finish(self):
+        for half in (0, 1):
+            self.xn[half].wait_recv()
+            self.sib.append(self.pass_on(XN, half, SIB))
+        for half in (0, 1):
+            self.diag[half].wait_recv()
+            self.sib.append(self.pass_on((1, 1, 0), half, SIB))
+        for copy in self.sib:
+            copy.wait_recv()
+
+
+class TeamScatter:
+    def __init__(self, tx, near, slot, buf, first, cross, last, halves):
+        self.tx, self.near, self.slot, self.buf = tx, near, slot, buf
+        self.first, self.cross, self.last, self.halves = first, cross, last, halves
+        self.sib, self.turned, self.ended = {}, [], []
+
+    def push(self, order):
+        rel = QUADS[order]
+        src = self.buf(self.slot((rel[0], rel[1], 1)))
+        self.sib[order] = self.tx.send(src, self.first.at[order], self.near(SIB))
+
+    def add(self, order):
+        self.sib[order].wait_recv()
+        own = self.buf(self.slot(QUADS[order]))
+        for half in self.halves:
+            part, more = own.at[half], self.first.at[order].at[half]
+            part[...] = (part[...].astype(F32) + more[...].astype(F32)).astype(BF)
+            if order == 0:
+                self.turned.append(self.tx.send(part, self.cross.at[0].at[half], self.near(XN)))
+            if order == 1:
+                self.ended.append(self.tx.send(part, self.cross.at[1].at[half], self.near(XN)))
+
+    def turn(self):
+        own = self.buf(self.slot(ZN))
+        for half, copy in zip(self.halves, self.turned):
+            copy.wait_recv()
+            part, more = own.at[half], self.cross.at[0].at[half]
+            part[...] = (part[...].astype(F32) + more[...].astype(F32)).astype(BF)
+            self.ended.append(self.tx.send(part, self.last.at[half], self.near(ZN)))
+
+    def total(self, own):
+        for copy in self.ended:
+            copy.wait_recv()
+        return (
+            self.buf(own)[...].astype(F32)
+            + self.cross[1].astype(F32)
+            + self.last[...].astype(F32)
+        )
+
+
+def layer_kernel(T, M, D, FF, share, *refs):
     names = IN_NAMES + OUT_NAMES + list(scratch_list(T, M, D, FF))
-    r = dict(zip(names, refs))
-    ssem, rsem = refs[len(names):]
-    g = type("Refs", (), r)
+    ssem, rsem = refs[len(names) :]
+    g = type("Refs", (), dict(zip(names, refs)))
     R, H, Q, W, S = T + M, FF // 8, D // 4, D // 8, 8 * T
-    H4, D32 = H // 4, D // 32
+    H4, B = H // 4, D // 32
     MK = 8 * M
     tx = Sender(ssem, rsem)
 
     b, d = lax.axis_index("blk"), lax.axis_index("dp")
     z, x, y, c = b // 2, b % 2, d // 2, d % 2
-    p = 4 * x + 2 * y + c
-
-    def dev(z, x, y, c):
-        return (2 * z + x, 2 * y + c)
+    zh, zl = z // 2, z % 2
+    zx = 2 * zl + x
+    p = 2 * zx + c
+    e = 2 * zh + y
+
+    def dev(zh, zl, x, y, c):
+        return (4 * zh + 2 * zl + x, 2 * y + c)
 
     def near(rel):
-        return dev(z, (x + rel[0]) % 2, (y + rel[1]) % 2, (c + rel[2]) % 2)
+        return dev(zh, (zl + rel[0]) % 2, (x + rel[1]) % 2, y, (c + rel[2]) % 2)
 
     def slot(rel):
-        return 4 * ((x + rel[0]) % 2) + 2 * ((y + rel[1]) % 2) + (c + rel[2]) % 2
-
-    def along(dz):
-        return dev((z + dz) % 4, x, y, c)
-
-    home_z = y + c * (3 - 2 * y)
-    home_y, home_c = (z + z // 2) % 2, z // 2
-    partner = dev(home_z, x, home_y, home_c)
-    partner_slot = 4 * x + 2 * home_y + home_c
-    stays = home_z == z
+        return 4 * ((zl + rel[0]) % 2) + 2 * ((x + rel[1]) % 2) + (c + rel[2]) % 2
+
+    def far(rel):
+        return dev((zh + rel[0]) % 2, zl, x, (y + rel[1]) % 2, c)
+
+    partner = dev(c, zl, x, y, zh)
+    partner_slot = 2 * zx + zh
+    stays = c == zh
     moves = jnp.logical_not(stays)
 
     barrier = pltpu.get_barrier_semaphore()
-    for rel in PLANE:
+    for rel in TEAM:
         pl.semaphore_signal(barrier, inc=1, device_id=near(rel), device_id_type=MESH)
-    for dz in (1, 2, 3):
-        pl.semaphore_signal(barrier, inc=1, device_id=along(dz), device_id_type=MESH)
+    for rel in FAR:
+        pl.semaphore_signal(barrier, inc=1, device_id=far(rel), device_id_type=MESH)
 
     @pl.when(moves)
     def _():
         pl.semaphore_signal(barrier, inc=1, device_id=partner, device_id_type=MESH)
 
+    loads = [tx.local(w, g.f_qkv.at[i]) for i, w in enumerate((g.wq, g.wk, g.wv))]
+    loads_o = tx.local(g.wo, g.f_o)
+    loads_in = tx.local(g.win, g.f_in)
+    loads_out = tx.local(g.wout, g.f_out)
+    share_lane = lax.broadcasted_iota(jnp.int32, (8, W), 1) // share
+    low = g.vec[...].astype(BF).astype(F32)
+    spread = jnp.concatenate([low] * (W // share), axis=1)
+    g.vg1[p] = jnp.where(share_lane == 2 * y + c, spread, 0.0)
+    g.bslot[e] = jnp.broadcast_to(g.bias[...].astype(BF).astype(F32), (8, H4))
+    for copy in loads:
+        copy.wait()
     for q in range(8):
-        for i, w in enumerate((g.wq, g.wk, g.wv)):
-            g.pq[q, :, i * W : (i + 1) * W] = w[:, q * W : (q + 1) * W].astype(BF)
-        for k in range(4):
-            at = (8 * k + q) * H4
-            g.pi[q, :, k * H4 : (k + 1) * H4] = g.win[:, at : at + H4].astype(BF)
-    g.w_out[z] = g.wout[...].astype(BF)
-    g.w_o[z, p] = g.wo[...].astype(BF)
-    g.wqkv[z, p] = g.pq[p]
-    g.w_in[z, p] = g.pi[p]
-    g.vg1[p] = g.vec[...]
-    g.bslot[z] = g.bias[...]
-
+        for i in range(3):
+            g.pq[q, :, i * W : (i + 1) * W] = g.f_qkv[i, :, q * W : (q + 1) * W].astype(BF)
+    g.wqkv[zh, zx, y, c] = g.pq[p]
+    loads_o.wait()
+    g.w_o[zh, zx, y, c] = g.f_o[...].astype(BF)
     @pl.when(moves)
     def _():
         pl.semaphore_wait(barrier, 11)
@@ -235,8 +333,11 @@
     def _():
         pl.semaphore_wait(barrier, 10)
 
+    swaps = []
+
     def swap(src, dst_there, dst_here):
         copy = tx.make(src, dst_there, partner)
+        here = pltpu.make_async_copy(src, dst_here, rsem.at[tx.count - 1])
 
         @pl.when(moves)
         def _():
@@ -244,107 +345,99 @@
 
         @pl.when(stays)
         def _():
-            dst_here[...] = src[...]
-
+            here.start()
+
+        swaps.append(copy)
         return copy
 
-    def swap_wait(copy):
-        @pl.when(moves)
-        def _():
+    def far_start(ref):
+        at = ref(zh, y)
+        return [tx.send(at, at, far(rel)) for rel in FAR[:2]]
+
+    def far_forward(ref, copies):
+        copies[0].wait_recv()
+        at = ref(1 - zh, y)
+        copies.append(tx.send(at, at, far((0, 1))))
+
+    def far_finish(copies):
+        for copy in copies[1:]:
             copy.wait_recv()
 
-    def gather_start(ref):
-        at = ref(p)
-        return [tx.send(at, at, near(rel)) for rel in CLASS + [SIB]]
-
-    def gather_finish(ref, copies):
-        forwards = [copies[3]]
-        for rel, copy in zip(CLASS, copies):
-            copy.wait_recv()
-            at = ref(slot(rel))
-            forwards.append(tx.send(at, at, near(SIB)))
-        for copy in forwards:
-            copy.wait_recv()
-
-    def scatter_pair(buf, first, order):
-        rel = QUADS[order]
-        return tx.send(buf(slot((rel[0], rel[1], 1))), first.at[order], near(SIB))
-
-    def scatter_add(buf, first, third, order, copy):
-        rel = QUADS[order]
-        copy.wait_recv()
-        own = buf(slot(rel))
-        own[...] = (own[...].astype(F32) + first[order].astype(F32)).astype(BF)
-        if order < 3:
-            return tx.send(own, third.at[order], near(rel))
-        return None
-
-    def scatter_total(buf, third, copies):
+    def team_send(src, dst):
+        return [tx.send(src(slot(rel)), dst, near(rel)) for rel in TEAM]
+
+    def wait_all(copies):
         for copy in copies:
             copy.wait_recv()
-        total = buf(p)[...].astype(F32)
-        for k in range(3):
-            total = total + third[k].astype(F32)
-        return total
-
-    swap_x = swap(g.x, g.xt, g.xt)
+
+    early = 32
     swap_m = swap(g.mem, g.xm, g.xm)
-    vec_copies = [tx.send(g.vg1.at[p], g.vg1.at[p], near(rel)) for rel in PLANE]
-    qkv_copies = [
-        tx.send(g.pq.at[slot(rel)], g.wqkv.at[z, p], near(rel)) for rel in PLANE
-    ]
-    for copy in vec_copies:
-        copy.wait_recv()
-    for k in range(2):
-        total = g.vg1[4 * k]
-        for i in range(1, 4):
-            total = total + g.vg1[4 * k + i]
-        g.vg2[z, k] = total
-    vec_copies = [tx.send(g.vg2.at[z], g.vg2.at[z], along(dz)) for dz in (1, 2, 3)]
-    bias_copies = [tx.send(g.bslot.at[z], g.bslot.at[z], along(dz)) for dz in (1, 2, 3)]
-    for copy in qkv_copies:
-        copy.wait_recv()
-    qkv_copies = [tx.send(g.wqkv.at[z], g.wqkv.at[z], along(dz)) for dz in (1, 2, 3)]
+    swap_a = swap(g.x.at[:early], g.xt.at[:early], g.xt.at[:early])
+    swap_b = swap(g.x.at[early:], g.xt.at[early:], g.xt.at[early:])
+    vec_copies = [tx.send(g.vg1.at[p], g.vg1.at[p], near(rel)) for rel in TEAM]
+    qkv_copies = team_send(lambda q: g.pq.at[q], g.wqkv.at[zh, zx, y, c])
+    wait_all(vec_copies)
+    for k in range(4):
+        g.vg2[e, k] = g.vg1[2 * k] + g.vg1[2 * k + 1]
+    vec_copies = [tx.send(g.vg2.at[e], g.vg2.at[e], far(rel)) for rel in FAR]
+    vec_copies += [tx.send(g.bslot.at[e], g.bslot.at[e], far(rel)) for rel in FAR]
+    wait_all(qkv_copies)
+    qkv_at = lambda i, j: g.wqkv.at[i, :, j]
+    qkv_copies = far_start(qkv_at)
+    wo_at = lambda i, j: g.w_o.at[i, zx, j, c]
+    wo_copies = far_start(wo_at)
     swap_c = swap(g.cot, g.cot_all.at[partner_slot], g.cot_all.at[p])
-    wo_copies = [tx.send(g.w_o.at[z, p], g.w_o.at[z, p], along(dz)) for dz in (1, 2, 3)]
-    for copy in vec_copies + bias_copies:
-        copy.wait_recv()
+    loads_in.wait()
+    for q in range(8):
+        for k in range(4):
+            at = (16 * (k // 2) + 4 * (q // 2) + 2 * (k % 2) + q % 2) * H4
+            g.pi[q, :, k * H4 : (k + 1) * H4] = g.f_in[:, at : at + H4].astype(BF)
+    g.w_in[zh, zx, y, c] = g.pi[p]
+    loads_out.wait()
+    g.w_out[zh, y] = g.f_out[...].astype(BF)
+    wait_all(vec_copies)
     for k in range(8):
-        g.prm[:, k * W : (k + 1) * W] = g.vg2[k // 2, k % 2]
+        group = g.vg2[2 * (k // 4), k % 4] + g.vg2[2 * (k // 4) + 1, k % 4]
+        g.pg[k] = group
+        g.prm[:, k * W : (k + 1) * W] = group
     prm = g.prm
-
-    swap_wait(swap_m)
-    swap_wait(swap_x)
-    for src, at, count in ((g.xm, 0, M), (g.xt, M, T)):
-
-        def norm_rows(i, _, src=src, at=at):
-            rows = pl.ds(pl.multiple_of(i * 32, 32), 32)
+    half_rows = R // 2
+    n_gather = TeamGather(
+        tx, near, slot, lambda q, h: g.n_all.at[q, pl.ds(h * half_rows, half_rows)]
+    )
+
+    def norm_rows(src, first, count, at):
+        def step(i, _):
+            rows = pl.ds(pl.multiple_of(first + i * 32, 32), 32)
             hat, _unused = norm_parts(src[rows, :].astype(F32))
             out = (hat * prm[0:1] + prm[1:2]).astype(BF)
             g.n_all[p, pl.ds(pl.multiple_of(at + i * 32, 32), 32), :] = out
             return 0
 
-        lax.fori_loop(0, count // 32, norm_rows, 0)
-    n_at = lambda q: g.n_all.at[q]
-    n_copies = gather_start(n_at)
-    win_copies = [tx.send(g.pi.at[slot(rel)], g.w_in.at[z, p], near(rel)) for rel in PLANE]
-    gather_finish(n_at, n_copies)
-    for copy in qkv_copies:
-        copy.wait_recv()
-    wout_copies = [tx.send(g.w_out.at[z], g.w_out.at[z], along(dz)) for dz in (1, 2, 3)]
-    for copy in win_copies:
-        copy.wait_recv()
-    win_copies = [tx.send(g.w_in.at[z], g.w_in.at[z], along(dz)) for dz in (1, 2, 3)]
-    for copy in wo_copies:
-        copy.wait_recv()
-    wo_at = lambda q: g.w_o.at[:, q]
-    wo_copies = gather_start(wo_at)
-    swap_wait(swap_c)
-    cot_at = lambda q: g.cot_all.at[q]
-    cot_copies = gather_start(cot_at)
-
-    wqkv = flat(g.wqkv[...].reshape(32, D32, 3 * W))
-    own_vec = g.vg2[p // 2, p % 2]
+        lax.fori_loop(0, count // 32, step, 0)
+
+    swap_m.wait_recv()
+    norm_rows(g.xm, 0, M, 0)
+    swap_a.wait_recv()
+    norm_rows(g.xt, 0, early, M)
+    n_gather.start(0)
+    swap_b.wait_recv()
+    norm_rows(g.xt, early, T - early, M + early)
+    n_gather.start(1)
+    win_copies = team_send(lambda q: g.pi.at[q], g.w_in.at[zh, zx, y, c])
+    far_forward(qkv_at, qkv_copies)
+    n_gather.forward(0)
+    n_gather.forward(1)
+    far_forward(wo_at, wo_copies)
+    wait_all(win_copies)
+    win_at = lambda i, j: g.w_in.at[i, :, j]
+    win_copies = far_start(win_at)
+    wout_at = lambda i, j: g.w_out.at[i, j]
+    wout_copies = far_start(wout_at)
+    n_gather.finish()
+    far_finish(qkv_copies)
+    wqkv = flat(g.wqkv[...].reshape(32, B, 3 * W))
+    own_vec = g.pg[p]
     qkv_bias = jnp.concatenate(
         [own_vec[2:3], jnp.zeros((1, W), F32), own_vec[3:4]], axis=1
     )
@@ -356,12 +449,20 @@
         return 0
 
     lax.fori_loop(0, 4, project, 0)
-
+    far_finish(wo_copies)
+    wo_gather = TeamGather(
+        tx, near, slot, lambda q, h: g.w_o.at[h, q // 2, :, q % 2]
+    )
+    swap_c.wait_recv()
+    half_tok = T // 2
+    cot_gather = TeamGather(
+        tx, near, slot, lambda q, h: g.cot_all.at[q, pl.ds(h * half_tok, half_tok)]
+    )
+    for gather in (wo_gather, cot_gather):
+        gather.start(0)
+        gather.start(1)
     place = [
-        g.order[2 * (qy + qc * (3 - 2 * qy)) + qx]
-        for qx in (0, 1)
-        for qy in (0, 1)
-        for qc in (0, 1)
+        g.order[4 * qc + 2 * qz + qx] for qz in (0, 1) for qx in (0, 1) for qc in (0, 1)
     ]
 
     def pick(blocks, wanted):
@@ -399,21 +500,20 @@
     for j in range(8):
         g.kk[j * M : (j + 1) * M, :] = g.qkv[j, :M, W : 2 * W]
         g.vv[j * M : (j + 1) * M, :] = g.qkv[j, :M, 2 * W :]
-
-    B = 2 * T
-    lane = lax.broadcasted_iota(jnp.int32, (B, W), 1)
+    N = 2 * T
+    lane = lax.broadcasted_iota(jnp.int32, (N, W), 1)
     head_lanes = [lane < W // 2, lane >= W // 2]
-    below = lax.broadcasted_iota(jnp.int32, (B, B), 1) <= lax.broadcasted_iota(
-        jnp.int32, (B, B), 0
+    below = lax.broadcasted_iota(jnp.int32, (N, N), 1) <= lax.broadcasted_iota(
+        jnp.int32, (N, N), 0
     )
 
     def only(value, h):
         return jnp.where(head_lanes[h], value, jnp.zeros_like(value))
 
-    for i in range(S // B):
-        rows = slice(i * B, (i + 1) * B)
-        past = MK + i * B
-        end = past + B
+    def attend(i):
+        rows = slice(i * N, (i + 1) * N)
+        past = MK + i * N
+        end = past + N
         q_rows = g.qs[rows, :]
         parts = []
         for h in range(2):
@@ -435,20 +535,30 @@
             parts.append(dot(w0, g.vv[:past, :]) + dot(w1, g.vv[past:end, :]))
         g.ctx[rows, :] = jnp.where(head_lanes[0], parts[0], parts[1])
 
+    attend(0)
+    attend(1)
+    attend(2)
+    wo_gather.forward(0)
+    wo_gather.forward(1)
+    attend(3)
     def store_ctx(q, at, rows):
         g.ctx_send[q, pl.ds(at, 16), :] = rows.astype(BF)
 
     from_sorted(lambda j, at: g.ctx[pl.ds(j * T + at, 16), :], store_ctx)
-    ctx_copies = [tx.send(g.ctx_send.at[slot(rel)], g.ctx_own.at[p], near(rel)) for rel in PLANE]
+    ctx_copies = team_send(lambda q: g.ctx_send.at[q], g.ctx_own.at[p])
     g.ctx_own[p] = g.ctx_send[p]
-    gather_finish(wo_at, wo_copies)
-    gather_finish(cot_at, cot_copies)
-    for copy in ctx_copies:
-        copy.wait_recv()
+    cot_gather.forward(0)
+    cot_gather.forward(1)
+    far_forward(win_at, win_copies)
+    wo_gather.finish()
+    wait_all(ctx_copies)
     for q in range(8):
         g.ctx2d[:, q * W : (q + 1) * W] = g.ctx_own[q]
-    w_o = lambda: flat(g.w_o[...].reshape(32, D32, D))
+    w_o = lambda: flat(g.w_o[...].reshape(32, B, D))
     g.mid[...] = dot(g.ctx2d[...], w_o()) + g.xt[...].astype(F32) + prm[4:5]
+    n2_gather = TeamGather(
+        tx, near, slot, lambda q, h: g.n2_all.at[q, pl.ds(h * half_tok, half_tok)]
+    )
 
     def norm_mid(i, _):
         rows = pl.ds(pl.multiple_of(i * 32, 32), 32)
@@ -456,22 +566,28 @@
         g.n2_all[p, rows, :] = (hat * prm[5:6] + prm[6:7]).astype(BF)
         return 0
 
-    lax.fori_loop(0, T // 32, norm_mid, 0)
-    n2_at = lambda q: g.n2_all.at[q]
-    n2_copies = gather_start(n2_at)
-    gather_finish(n2_at, n2_copies)
-    for copy in wout_copies + win_copies:
-        copy.wait_recv()
-
+    for half in (0, 1):
+        lax.fori_loop(half * (half_tok // 32), (half + 1) * (half_tok // 32), norm_mid, 0)
+        n2_gather.start(half)
+    far_forward(wout_at, wout_copies)
+    n2_gather.forward(0)
+    n2_gather.forward(1)
+    cot_gather.finish()
+    n2_gather.finish()
+    far_finish(win_copies)
+    far_finish(wout_copies)
+    tok_halves = [pl.ds(h * half_tok, half_tok) for h in (0, 1)]
     hidden_bias = jnp.concatenate([g.bslot[k, 0:1, :] for k in range(4)], axis=1)
-    pb_a = lambda q: g.pb_a.at[q]
-    pb_b = lambda q: g.pb_b.at[q]
-    sib_a, sib_b, class_a, class_b = [], [], [], []
+    out_sum = TeamScatter(
+        tx, near, slot, lambda q: g.pb_a.at[q], g.r1_a, g.rx_a, g.rz_a, tok_halves
+    )
+    n2_sum = TeamScatter(
+        tx, near, slot, lambda q: g.pb_b.at[q], g.r1_b, g.rx_b, g.rz_b, tok_halves
+    )
     for order in range(4):
-        rel = QUADS[order]
-        pair = 4 * ((x + rel[0]) % 2) + 2 * ((y + rel[1]) % 2)
-        w_in = flat(g.w_in[...].reshape(32, D32, H))
-        w_out = flat(g.w_out[...])
+        pair = 2 * (slot(QUADS[order]) // 2)
+        w_in = flat(g.w_in[...].reshape(32, B, H))
+        w_out = g.w_out[...].reshape(H, D)
         inner = dot(flat(g.n2_all[pl.ds(pair, 2)]), w_in) + hidden_bias
         act, slope = gelu_parts(inner)
         act = act.astype(BF)
@@ -482,42 +598,32 @@
         for k in range(4):
             g.act[k, at, :] = act[:, k * H4 : (k + 1) * H4]
         g.pb_b[pl.ds(pair, 2)] = dot_nt(inner_grad, w_in).astype(BF).reshape(2, T, D)
-        sib_b.append(scatter_pair(pb_b, g.r1_b, order))
+        n2_sum.push(order)
         g.pb_a[pl.ds(pair, 2)] = dot(act, w_out).astype(BF).reshape(2, T, D)
+        out_sum.push(order)
         if order:
-            class_b.append(scatter_add(pb_b, g.r1_b, g.r3_b, order - 1, sib_b[order - 1]))
-    scatter_add(pb_b, g.r1_b, g.r3_b, 3, sib_b[3])
-    for order in range(4):
-        sib_a.append(scatter_pair(pb_a, g.r1_a, order))
-    for order in range(4):
-        class_a.append(scatter_add(pb_a, g.r1_a, g.r3_a, order, sib_a[order]))
-
-    gout_copies, gin_copies, gb_copies = [], [], []
+            n2_sum.add(order - 1)
+    n2_sum.add(3)
     cot = lambda: flat(g.cot_all[...])
+    for j in (1 - y, y):
+        for k in range(2):
+            g.gout_s[k, j] = dot_tn(g.act[2 * k + j], cot()).astype(BF)
+    gout_copy = tx.send(g.gout_s.at[:, 1 - y], g.gout_a, far((0, 1)))
+    n2_sum.turn()
+    out_sum.add(0)
+    for k in range(4):
+        grad = dot_tn(flat(g.n2_all[:, :, k * Q : (k + 1) * Q]), g.inner[...])
+        cut = slice(2 * (k % 2), 2 * (k % 2) + 2)
+        g.gin_s[k // 2, cut] = grad.astype(BF).reshape(2, 2, 2, B, H)
+    gin_copy = tx.send(g.gin_s.at[:, :, 1 - y], g.gin_a, far((0, 1)))
     inner_sum = col_sum(g.inner[...])
     for k in range(4):
         g.bp[k] = jnp.broadcast_to(inner_sum[:, k * H4 : (k + 1) * H4], (8, H4))
-    for dz in (1, 2, 3, 0):
-        to = (z + dz) % 4
-        grad = dot_tn(g.act[to], cot())
-        if dz:
-            g.gout_s[to] = grad.astype(BF)
-            gout_copies.append(tx.send(g.gout_s.at[to], g.gout_r.at[dz - 1], along(dz)))
-            gb_copies.append(tx.send(g.bp.at[to], g.br.at[dz - 1], along(dz)))
-        else:
-            g.gout_own[...] = grad
-    for dz in (1, 2, 3, 0):
-        to = (z + dz) % 4
-        cols = pl.ds(pl.multiple_of(to * Q, Q), Q)
-        grad = dot_tn(flat(g.n2_all[:, :, cols]), g.inner[...])
-        if dz:
-            g.gin_s[to] = grad.astype(BF).reshape(8, D32, H)
-            gin_copies.append(tx.send(g.gin_s.at[to], g.gin_r.at[dz - 1], along(dz)))
-        else:
-            g.gin_own[...] = grad
-
-    g.mg[...] = scatter_total(pb_b, g.r3_b, class_b[:3])
-
+    gb_copies = []
+    for i, rel in enumerate(FAR):
+        to = 2 * ((zh + rel[0]) % 2) + (y + rel[1]) % 2
+        gb_copies.append(tx.send(g.bp.at[to], g.br.at[i], far(rel)))
+    g.mg[...] = n2_sum.total(p)
     def norm_two_back(i, sums):
         rows = pl.ds(pl.multiple_of(i * 32, 32), 32)
         up = g.mg[rows, :]
@@ -545,18 +651,34 @@
     cg = dot_nt(attg, w_o()).astype(BF)
     for q in range(8):
         g.cg_send[q] = cg[:, q * W : (q + 1) * W]
-    cg_copies = [tx.send(g.cg_send.at[slot(rel)], g.cg_all.at[p], near(rel)) for rel in PLANE]
+    cg_copies = team_send(lambda q: g.cg_send.at[q], g.cg_all.at[p])
     g.cg_all[p] = g.cg_send[p]
-
-    go_at = lambda q: g.go_buf.at[:, q]
+    for order in (1, 2, 3):
+        out_sum.add(order)
     for k in range(4):
         grad = dot_tn(g.ctx2d[:, k * Q : (k + 1) * Q], attg)
-        g.go_buf[k] = grad.astype(BF).reshape(8, D32, D)
-    sib_o = [scatter_pair(go_at, g.go_r1, order) for order in range(4)]
-    class_o = [scatter_add(go_at, g.go_r1, g.go_r3, order, sib_o[order]) for order in range(4)]
-
-    for copy in cg_copies:
+        cut = slice(2 * (k % 2), 2 * (k % 2) + 2)
+        g.pb_o[k // 2, cut] = grad.astype(BF).reshape(2, 2, 2, B, D)
+    o_sum = TeamScatter(
+        tx, near, slot, lambda q: g.pb_o.at[:, q // 2, :, q % 2], g.r1_o, g.rx_o, g.rz_o, [0, 1]
+    )
+    for order in range(4):
+        o_sum.push(order)
+
+    def far_turn(copy, own, got, out, last):
         copy.wait_recv()
+        out[...] = (own(1 - zh)[...].astype(F32) + got[1 - zh].astype(F32)).astype(BF)
+        return tx.send(out, last, far((1, 0)))
+
+    def far_total(copy, own, got, last):
+        copy.wait_recv()
+        return own(zh)[...].astype(F32) + got[zh].astype(F32) + last[...].astype(F32)
+
+    gout_own = lambda i: g.gout_s.at[i, y]
+    gin_own = lambda i: g.gin_s.at[i, :, y]
+    gqkv_own = lambda i: g.gqkv_s.at[i, :, y]
+    go_own = lambda i: g.go_s.at[i, y]
+    wait_all(cg_copies)
 
     def store_cg(j, at, rows):
         g.cg_sorted[pl.ds(j * T + at, 16), :] = rows.astype(BF)
@@ -564,9 +686,10 @@
     to_sorted(lambda q, at: g.cg_all[q, pl.ds(at, 16), :], store_cg)
     g.dk[...] = jnp.zeros_like(g.dk)
     g.dv[...] = jnp.zeros_like(g.dv)
-    for i in range(S // B):
-        rows = slice(i * B, (i + 1) * B)
-        end = MK + (i + 1) * B
+
+    def attend_back(i):
+        rows = slice(i * N, (i + 1) * N)
+        end = MK + (i + 1) * N
         cg_rows = g.cg_sorted[rows, :]
         q_rows = g.qs[rows, :]
         product = cg_rows.astype(F32) * g.ctx[rows, :]
@@ -582,6 +705,12 @@
             g.dv[:end, :] += dot_tn(w, ch)
         g.dq[rows, :] = jnp.where(head_lanes[0], parts[0], parts[1]) * 0.125
 
+    attend_back(0)
+    attend_back(1)
+    gout_copy = far_turn(gout_copy, gout_own, g.gout_a, g.gout_b, g.gout_c)
+    attend_back(2)
+    out_sum.turn()
+    attend_back(3)
     def load_grads(j, at):
         keys = pl.ds(MK + j * T + at, 16)
         return jnp.concatenate(
@@ -597,55 +726,40 @@
         g.dqkv[q, :M, :W] = jnp.zeros((M, W), BF)
         g.dqkv[q, :M, W : 2 * W] = g.dk[mt, :].astype(BF)
         g.dqkv[q, :M, 2 * W :] = g.dv[mt, :].astype(BF)
-
-    lo = scatter_total(pb_a, g.r3_a, class_a[:3]) + g.mid[...] + prm[7:8]
-    g.lo_s[...] = lo.astype(BF)
-    swap_lo = swap(g.lo_s, g.lo, g.lo)
-    go_total = scatter_total(go_at, g.go_r3, class_o[:3])
-    g.go_sum[...] = go_total.astype(BF)
-    go_copies = [
-        tx.send(g.go_sum.at[(z + dz) % 4], g.go_z.at[dz - 1], along(dz)) for dz in (1, 2, 3)
-    ]
-
-    sib_n, class_n = [], []
+    n_sum = TeamScatter(
+        tx, near, slot, lambda q: g.pb_n.at[q], g.r1_n, g.rx_n, g.rz_n, tok_halves
+    )
     for order in range(4):
-        rel = QUADS[order]
-        pair = 4 * ((x + rel[0]) % 2) + 2 * ((y + rel[1]) % 2)
+        pair = 2 * (slot(QUADS[order]) // 2)
         rows = flat(g.dqkv[pl.ds(pair, 2), M:, :])
-        w = flat(g.wqkv[...].reshape(32, D32, 3 * W))
+        w = flat(g.wqkv[...].reshape(32, B, 3 * W))
         g.pb_n[pl.ds(pair, 2)] = dot_nt(rows, w).astype(BF).reshape(2, T, D)
-        sib_n.append(scatter_pair(lambda q: g.pb_n.at[q], g.r1_n, order))
+        n_sum.push(order)
         if order:
-            class_n.append(
-                scatter_add(lambda q: g.pb_n.at[q], g.r1_n, g.r3_n, order - 1, sib_n[order - 1])
-            )
-    scatter_add(lambda q: g.pb_n.at[q], g.r1_n, g.r3_n, 3, sib_n[3])
-
+            n_sum.add(order - 1)
+    n_sum.add(3)
+    gin_copy = far_turn(gin_copy, gin_own, g.gin_a, g.gin_b, g.gin_c)
     g.vp[...] = jnp.zeros_like(g.vp)
     qkv_sum = jnp.zeros((1, 3 * W), F32)
     for q in range(8):
         qkv_sum = qkv_sum + col_sum(g.dqkv[q])
     qkv_sum8 = jnp.broadcast_to(qkv_sum, (8, 3 * W))
     ones = jnp.ones((8, 3 * W), F32)
-    gqkv_copies = []
-    for dz in (1, 2, 3, 0):
-        to = (z + dz) % 4
-        cols = pl.ds(pl.multiple_of(to * Q, Q), Q)
-        grad = dot_tn(flat(g.n_all[:, :, cols]), flat(g.dqkv[...]))
-        if dz:
-            g.gqkv_s[to] = grad.astype(BF).reshape(8, D32, 3 * W)
-            gqkv_copies.append(tx.send(g.gqkv_s.at[to], g.gqkv_r.at[dz - 1], along(dz)))
-        else:
-            g.gqkv_own[...] = grad
-        w = flat(g.wqkv[to]).astype(F32)
+    for k in range(4):
+        grad = dot_tn(flat(g.n_all[:, :, k * Q : (k + 1) * Q]), flat(g.dqkv[...]))
+        cut = slice(2 * (k % 2), 2 * (k % 2) + 2)
+        g.gqkv_s[k // 2, cut] = grad.astype(BF).reshape(2, 2, 2, B, 3 * W)
+        w = flat(g.wqkv[k // 2, cut].reshape(8, B, 3 * W)).astype(F32)
         gains = dot_nt(ones, grad * w, EXACT)
         shifts = dot_nt(qkv_sum8, w, EXACT)
-        for k in range(2):
-            at = slice(k * W, (k + 1) * W)
+        for i in range(2):
+            at = slice(i * W, (i + 1) * W)
             shift = shifts[0:1, at]
-            vec = g.vg2[to, k]
-            g.vp[2 * to + k, 0:1, :] = (gains[0:1, at] - vec[1:2] * shift) / vec[0:1]
-            g.vp[2 * to + k, 1:2, :] = shift
+            vec = g.pg[2 * k + i]
+            g.vp[2 * k + i, 0:1, :] = (gains[0:1, at] - vec[1:2] * shift) / vec[0:1]
+            g.vp[2 * k + i, 1:2, :] = shift
+    gqkv_copy = tx.send(g.gqkv_s.at[:, :, 1 - y], g.gqkv_a, far((0, 1)))
+    n_sum.turn()
     g.vp[p, 2:3, :] = qkv_sum[:, :W]
     g.vp[p, 3:4, :] = qkv_sum[:, 2 * W :]
     for k in range(8):
@@ -654,22 +768,28 @@
         g.vp[k, 5:6, :] = gain_two[:, at]
         g.vp[k, 6:7, :] = shift_two[:, at]
         g.vp[k, 7:8, :] = bias_out[:, at]
-    vec_copies = [
-        tx.send(g.vp.at[pl.ds(2 * ((z + dz) % 4), 2)], g.vr.at[dz - 1], along(dz))
-        for dz in (1, 2, 3)
-    ]
-
-    for copy in gout_copies + gb_copies + gin_copies + go_copies:
-        copy.wait_recv()
-    g.gout[...] = g.gout_own[...] + sum(g.gout_r[k].astype(F32) for k in range(3))
-    g.gbin[...] = g.bp[z] + g.br[0] + g.br[1] + g.br[2]
-    total = g.gin_own[...] + sum(flat(g.gin_r[k]).astype(F32) for k in range(3))
-    g.gin_a[...] = total.astype(BF).reshape(8, D32, H)
-    gin_copies = [tx.send(g.gin_a.at[slot(rel)], g.gin_b.at[p], near(rel)) for rel in PLANE]
-    g.gin_b[p] = g.gin_a[p]
-    g.go[...] = g.go_sum[z].astype(F32) + sum(g.go_z[k].astype(F32) for k in range(3))
-
-    g.mid[...] = scatter_total(lambda q: g.pb_n.at[q], g.r3_n, class_n[:3])
+    vec_copies = []
+    for i, rel in enumerate(FAR):
+        to = pl.ds(4 * ((zh + rel[0]) % 2), 4)
+        vec_copies.append(tx.send(g.vp.at[to], g.vr.at[i], far(rel)))
+    for order in range(4):
+        o_sum.add(order)
+    lo = out_sum.total(p) + g.mid[...] + prm[7:8]
+    g.lo_s[...] = lo.astype(BF)
+    swap_lo = swap(g.lo_s, g.lo, g.lo)
+    gqkv_copy = far_turn(gqkv_copy, gqkv_own, g.gqkv_a, g.gqkv_b, g.gqkv_c)
+    o_sum.turn()
+    g.gout[...] = far_total(gout_copy, gout_own, g.gout_a, g.gout_c)
+    g.gin_d[...] = flat_team(far_total(gin_copy, gin_own, g.gin_a, g.gin_c))
+    gin_copies = team_send(lambda q: g.gin_d.at[q], g.gin_e.at[p])
+    g.gin_e[p] = g.gin_d[p]
+    wait_all(gb_copies)
+    g.gbin[...] = g.bp[e] + g.br[0] + g.br[1] + g.br[2]
+    wait_all(vec_copies)
+    g.vs[...] = g.vp[pl.ds(4 * zh, 4)] + g.vr[0] + g.vr[1] + g.vr[2]
+    vec_copies = team_send(lambda q: g.vs.at[q // 2], g.va.at[p])
+    g.va[p] = g.vs[zx]
+    g.mid[...] = n_sum.total(p)
 
     def norm_one_back(i, _):
         rows = pl.ds(pl.multiple_of(i * 32, 32), 32)
@@ -683,41 +803,39 @@
 
     lax.fori_loop(0, T // 32, norm_one_back, 0)
     swap_ig = swap(g.ig_s, g.ig, g.ig)
-
-    for copy in gqkv_copies + vec_copies:
-        copy.wait_recv()
-    total = g.gqkv_own[...] + sum(flat(g.gqkv_r[k]).astype(F32) for k in range(3))
-    g.gqkv_a[...] = total.astype(BF).reshape(8, D32, 3 * W)
-    gqkv_copies = [tx.send(g.gqkv_a.at[slot(rel)], g.gqkv_b.at[p], near(rel)) for rel in PLANE]
-    g.gqkv_b[p] = g.gqkv_a[p]
-    g.vs[...] = g.vp[pl.ds(2 * z, 2)] + g.vr[0] + g.vr[1] + g.vr[2]
-    vec_copies = [tx.send(g.vs.at[(x + rel[0]) % 2], g.va.at[p], near(rel)) for rel in PLANE]
-    g.va[p] = g.vs[x]
-
-    for copy in gin_copies:
-        copy.wait_recv()
+    g.gqkv_d[...] = flat_team(far_total(gqkv_copy, gqkv_own, g.gqkv_a, g.gqkv_c))
+    gqkv_copies = team_send(lambda q: g.gqkv_d.at[q], g.gqkv_e.at[p])
+    g.gqkv_e[p] = g.gqkv_d[p]
+    g.go_s[...] = o_sum.total(p).astype(BF)
+    go_copy = tx.send(g.go_s.at[:, 1 - y], g.go_a, far((0, 1)))
+    wait_all(gin_copies)
     for q in range(8):
         for k in range(4):
-            at = (8 * k + q) * H4
-            g.gin[:, at : at + H4] = g.gin_b[q, :, k * H4 : (k + 1) * H4].astype(F32)
-    for copy in gqkv_copies + vec_copies:
-        copy.wait_recv()
-    for q in range(8):
-        for i, out in enumerate((g.gq, g.gk, g.gv)):
-            out[:, q * W : (q + 1) * W] = g.gqkv_b[q, :, i * W : (i + 1) * W].astype(F32)
+            at = (16 * (k // 2) + 4 * (q // 2) + 2 * (k % 2) + q % 2) * H4
+            g.gin[:, at : at + H4] = g.gin_e[q, :, k * H4 : (k + 1) * H4].astype(F32)
+    go_copy = far_turn(go_copy, go_own, g.go_a, g.go_b, g.go_c)
+    wait_all(vec_copies)
     total = g.va[0]
     for q in range(1, 8):
         total = total + g.va[q]
     g.gvec[...] = total
-
-    for copy in (swap_lo, swap_ig):
-        swap_wait(copy)
+    wait_all(gqkv_copies)
+    for q in range(8):
+        for i, out in enumerate((g.gq, g.gk, g.gv)):
+            out[:, q * W : (q + 1) * W] = g.gqkv_e[q, :, i * W : (i + 1) * W].astype(F32)
+    g.go[...] = far_total(go_copy, go_own, g.go_a, g.go_c)
+    swap_lo.wait_recv()
+    swap_ig.wait_recv()
     tx.drain()
 
     @pl.when(moves)
     def _():
-        for copy in (swap_x, swap_m, swap_c, swap_lo, swap_ig):
+        for copy in swaps:
             copy.wait_send()
+
+
+def flat_team(value):
+    return value.astype(BF).reshape((8,) + value.shape[2:])
 
 
 def run_layer(layer_input, memory, cotangent, block_order, w_query, w_key, w_value, w_output, w_in, w_out, vectors, b_in):
@@ -726,16 +844,12 @@
     FF = w_in.shape[1]
     W = D // 8
     share = vectors.shape[1]
-    low = vectors.astype(BF).astype(F32)
-    lanes = lax.broadcasted_iota(jnp.int32, (8, W), 1) // share
-    mine = lanes == lax.axis_index("dp")
-    vec = jnp.where(mine, jnp.tile(low, (1, W // share)), 0.0)
-    bias = jnp.broadcast_to(b_in.astype(BF).astype(F32)[None], (8, b_in.shape[0]))
     shapes = scratch_list(T, M, D, FF)
     vmem = pl.BlockSpec(memory_space=pltpu.VMEM)
     smem = pl.BlockSpec(memory_space=pltpu.SMEM)
+    hbm = pl.BlockSpec(memory_space=pl.ANY)
     outs = pl.pallas_call(
-        functools.partial(layer_kernel, T, M, D, FF),
+        functools.partial(layer_kernel, T, M, D, FF, share),
         out_shape=(
             jax.ShapeDtypeStruct((T, D), BF),
             jax.ShapeDtypeStruct((T, D), BF),
@@ -748,14 +862,14 @@
             jax.ShapeDtypeStruct((8, W), F32),
             jax.ShapeDtypeStruct((8, b_in.shape[0]), F32),
         ),
-        in_specs=[vmem, vmem, vmem, smem] + [vmem] * 8,
+        in_specs=[hbm, hbm, hbm, smem] + [hbm] * 6 + [vmem] * 2,
         out_specs=[vmem] * 10,
         scratch_shapes=[pltpu.VMEM(shape, kind) for shape, kind in shapes.values()]
         + [pltpu.SemaphoreType.DMA((SEMS,)), pltpu.SemaphoreType.DMA((SEMS,))],
         compiler_params=pltpu.CompilerParams(
             collective_id=0, has_side_effects=True, vmem_limit_bytes=63 * 2**20
         ),
-    )(layer_input[0], memory[0], cotangent[0], block_order, w_query, w_key, w_value, w_output, w_in, w_out, vec, bias)
+    )(layer_input[0], memory[0], cotangent[0], block_order, w_query, w_key, w_value, w_output, w_in, w_out, vectors, b_in[None])
     lo, ig, gq, gk, gv, go, gin, gout, gvec, gbin = outs
     gvec = lax.dynamic_slice(gvec, (0, lax.axis_index("dp") * share), (8, share))
     return (lo[None], ig.astype(F32)[None], gq, gk, gv, go, gin, gout, gvec, gbin[0])

time: 211 us -> 186 us (0.88)
  Pallas kernels: 198 us -> 175 us
    pallas_call x1, Pallas kernels: 198 us -> 175 us  [run_layer(): pl.pallas_call(functools.partial(layer_kernel, T, M, D, FF, share), out_s...]
    unnamed x27 -> x23, local copies, waits for them, and re-layouts: 6.68 us -> 5.95 us
where the time goes in v2:
time: 186 us
  Pallas kernels  175 us (94%)
  local copies, waits for them, and re-layouts  7.8 us (4%)
    pallas_call x1, Pallas kernels, run_layer(): pl.pallas_call(functools.partial(layer_kernel, T, M, D, FF, share), out_s...  175 us
    unnamed x23, local copies, waits for them, and re-layouts  5.95 us

profile of v2, /device:TPU:0, one launch (start us, length us, event | category | flops | bytes accessed | tf_op | source)
XLA Modules:
  0.0 185.8 jit_solution(16771351334124325856)
XLA Ops:
  0.7 175.5 %shard_map.195 = (bf16[128,1024]{1,0:T(8,128)(2,1)}, bf16[128,1024]{1,0:T(8,128)(2,1)}, f32[32,1024]{1,0:T(8,128)}, f32[32,1024]{1,0:T(8,128)}, f32[32,1024]{1,0...) custom-call(bf16[128,1024]{1,0:T(8,128)(2,1)} %bitcast.11, ...), custom_call_target="tpu_custom_call" | custom-call | tf_op jit(solution)/shard_map/pallas_call | solution.py:851
  176.1 0.0 copy-start.7
  176.1 1.2 slice_bitcast_fusion
  177.3 0.0 copy-done.7
  177.3 0.7 constant_dynamic-slice_fusion
  178.0 0.0 copy-start.2
  178.0 1.8 bitcast_convert_fusion
  179.8 0.0 copy-done.2
  179.8 0.0 copy-start.6
  179.8 0.0 copy-start.5
  179.8 0.0 copy-start.4
  179.8 0.7 copy.29
  180.6 0.3 copy-done.6
  180.8 0.0 copy-start.1
  180.8 0.7 copy.30
  181.5 0.0 copy-done.5
  181.5 0.7 copy.31
  182.2 0.0 copy-done.4
  182.2 0.0 copy-start.3
  182.2 0.7 copy.32
  182.8 0.3 copy-done.3
  183.1 0.7 copy.33
  183.8 0.0 copy-done.1
  183.8 0.0 copy-start
  183.8 0.8 copy.34
  184.6 0.4 copy-done
  185.0 0.8 copy.35
Async XLA Ops:
  176.1 1.2 copy-start.7
  178.0 1.8 copy-start.2
  179.8 1.0 copy-start.6
  179.8 1.7 copy-start.5
  179.8 2.3 %copy-start.4 = (f32[32,1024]{1,0:T(8,128)S(1)}, f32[32,1024]{1,0:T(8,128)}, u32[]{:S(2)}) copy-start(f32[32,1024]{1,0:T(8,128)} %get-tuple-element.44) | copy-start | bytes 393220
  180.8 2.9 %copy-start.1 = (f32[32,4096]{1,0:T(8,128)S(1)}, f32[32,4096]{1,0:T(8,128)}, u32[]{:S(2)}) copy-start(f32[32,4096]{1,0:T(8,128)} %get-tuple-element.46) | copy-start | bytes 1572868
  182.2 1.0 copy-start.3
  183.8 1.2 copy-start

commit v3 on v2

--- a/solution.py
+++ b/solution.py
@@ -74,8 +74,7 @@
         f_in=((B, FF), F32),
         f_out=((H4, D), F32),
         n_all=((8, R, D), BF),
-        xm=((M, D), BF),
-        xt=((T, D), BF),
+        raw=((8, R, D), BF),
         cot_all=((8, T, D), BF),
         n2_all=((8, T, D), BF),
         pq=((8, B, 3 * W), BF),
@@ -183,10 +182,14 @@
         copy.start()
         return copy
 
+    def plan(self, src, dst, target):
+        copy = self.make(src, dst, target)
+        self.pending.append(copy)
+        return copy
+
     def send(self, src, dst, target):
-        copy = self.make(src, dst, target)
+        copy = self.plan(src, dst, target)
         copy.start()
-        self.pending.append(copy)
         return copy
 
     def drain(self):
@@ -196,33 +199,64 @@
 
 class TeamGather:
     def __init__(self, tx, near, slot, ref):
-        self.tx, self.near, self.slot, self.ref = tx, near, slot, ref
-        self.sib, self.zn, self.xn, self.diag = [], {}, {}, {}
-
-    def pass_on(self, rel, half, to):
-        at = self.ref(self.slot(rel), half)
-        return self.tx.send(at, at, self.near(to))
+        def plan(rel, to):
+            ats = [ref(slot(rel), half) for half in (0, 1)]
+            return [tx.plan(at, at, near(to)) for at in ats]
+
+        self.zn, self.xn = plan((0, 0, 0), ZN), plan((0, 0, 0), XN)
+        self.diag = plan(ZN, XN)
+        self.sib = {rel: plan(rel, SIB) for rel in QUADS}
 
     def start(self, half):
-        own = (0, 0, 0)
-        self.zn[half] = self.pass_on(own, half, ZN)
-        self.xn[half] = self.pass_on(own, half, XN)
-        self.sib.append(self.pass_on(own, half, SIB))
-
-    def forward(self, half):
-        self.zn[half].wait_recv()
-        self.diag[half] = self.pass_on(ZN, half, XN)
-        self.sib.append(self.pass_on(ZN, half, SIB))
-
-    def finish(self):
+        self.zn[half].start()
+        self.xn[half].start()
+        self.sib[(0, 0, 0)][half].start()
+
+    def forward(self):
+        for half in (0, 1):
+            self.zn[half].wait_recv()
+            self.diag[half].start()
+            self.sib[ZN][half].start()
+
+    def pass_xn(self):
         for half in (0, 1):
             self.xn[half].wait_recv()
-            self.sib.append(self.pass_on(XN, half, SIB))
+            self.sib[XN][half].start()
+
+    def pass_diag(self):
         for half in (0, 1):
             self.diag[half].wait_recv()
-            self.sib.append(self.pass_on((1, 1, 0), half, SIB))
-        for copy in self.sib:
+            self.sib[(1, 1, 0)][half].start()
+
+    def wait_sib(self, rel):
+        for copy in self.sib[rel]:
             copy.wait_recv()
+
+    def finish(self):
+        self.pass_xn()
+        self.pass_diag()
+        for rel in QUADS:
+            self.wait_sib(rel)
+
+
+class FarGather:
+    def __init__(self, tx, far, zh, y, ref):
+        own, passed = ref(zh, y), ref(1 - zh, y)
+        self.over_z = tx.plan(own, own, far((1, 0)))
+        self.over_y = tx.plan(own, own, far((0, 1)))
+        self.passed = tx.plan(passed, passed, far((0, 1)))
+
+    def start(self):
+        self.over_z.start()
+        self.over_y.start()
+
+    def forward(self):
+        self.over_z.wait_recv()
+        self.passed.start()
+
+    def finish(self):
+        self.over_y.wait_recv()
+        self.passed.wait_recv()
 
 
 class TeamScatter:
@@ -265,6 +299,29 @@
         )
 
 
+class FarSum:
+    def __init__(self, tx, far, zh, y, own, first, mid, last):
+        self.tx, self.far, self.zh, self.y, self.own = tx, far, zh, y, own
+        self.first, self.mid, self.last, self.copies = first, mid, last, []
+
+    def start(self, half):
+        src = self.own(half, 1 - self.y)
+        self.copies.append(self.tx.send(src, self.first.at[half], self.far((0, 1))))
+
+    def both(self, half):
+        return self.own(half, self.y)[...].astype(F32) + self.first[half].astype(F32)
+
+    def turn(self):
+        self.copies[0].wait_recv()
+        self.mid[...] = self.both(1 - self.zh).astype(BF)
+        self.ended = self.tx.send(self.mid, self.last, self.far((1, 0)))
+
+    def total(self):
+        self.copies[1].wait_recv()
+        self.ended.wait_recv()
+        return self.both(self.zh) + self.last[...].astype(F32)
+
+
 def layer_kernel(T, M, D, FF, share, *refs):
     names = IN_NAMES + OUT_NAMES + list(scratch_list(T, M, D, FF))
     ssem, rsem = refs[len(names) :]
@@ -297,6 +354,8 @@
     partner_slot = 2 * zx + zh
     stays = c == zh
     moves = jnp.logical_not(stays)
+    outer = zl == zh
+    inner = jnp.logical_not(outer)
 
     barrier = pltpu.get_barrier_semaphore()
     for rel in TEAM:
@@ -317,76 +376,14 @@
     spread = jnp.concatenate([low] * (W // share), axis=1)
     g.vg1[p] = jnp.where(share_lane == 2 * y + c, spread, 0.0)
     g.bslot[e] = jnp.broadcast_to(g.bias[...].astype(BF).astype(F32), (8, H4))
+    loads_o.wait()
+    g.w_o[zh, zx, y, c] = g.f_o[...].astype(BF)
     for copy in loads:
         copy.wait()
     for q in range(8):
         for i in range(3):
             g.pq[q, :, i * W : (i + 1) * W] = g.f_qkv[i, :, q * W : (q + 1) * W].astype(BF)
     g.wqkv[zh, zx, y, c] = g.pq[p]
-    loads_o.wait()
-    g.w_o[zh, zx, y, c] = g.f_o[...].astype(BF)
-    @pl.when(moves)
-    def _():
-        pl.semaphore_wait(barrier, 11)
-
-    @pl.when(stays)
-    def _():
-        pl.semaphore_wait(barrier, 10)
-
-    swaps = []
-
-    def swap(src, dst_there, dst_here):
-        copy = tx.make(src, dst_there, partner)
-        here = pltpu.make_async_copy(src, dst_here, rsem.at[tx.count - 1])
-
-        @pl.when(moves)
-        def _():
-            copy.start()
-
-        @pl.when(stays)
-        def _():
-            here.start()
-
-        swaps.append(copy)
-        return copy
-
-    def far_start(ref):
-        at = ref(zh, y)
-        return [tx.send(at, at, far(rel)) for rel in FAR[:2]]
-
-    def far_forward(ref, copies):
-        copies[0].wait_recv()
-        at = ref(1 - zh, y)
-        copies.append(tx.send(at, at, far((0, 1))))
-
-    def far_finish(copies):
-        for copy in copies[1:]:
-            copy.wait_recv()
-
-    def team_send(src, dst):
-        return [tx.send(src(slot(rel)), dst, near(rel)) for rel in TEAM]
-
-    def wait_all(copies):
-        for copy in copies:
-            copy.wait_recv()
-
-    early = 32
-    swap_m = swap(g.mem, g.xm, g.xm)
-    swap_a = swap(g.x.at[:early], g.xt.at[:early], g.xt.at[:early])
-    swap_b = swap(g.x.at[early:], g.xt.at[early:], g.xt.at[early:])
-    vec_copies = [tx.send(g.vg1.at[p], g.vg1.at[p], near(rel)) for rel in TEAM]
-    qkv_copies = team_send(lambda q: g.pq.at[q], g.wqkv.at[zh, zx, y, c])
-    wait_all(vec_copies)
-    for k in range(4):
-        g.vg2[e, k] = g.vg1[2 * k] + g.vg1[2 * k + 1]
-    vec_copies = [tx.send(g.vg2.at[e], g.vg2.at[e], far(rel)) for rel in FAR]
-    vec_copies += [tx.send(g.bslot.at[e], g.bslot.at[e], far(rel)) for rel in FAR]
-    wait_all(qkv_copies)
-    qkv_at = lambda i, j: g.wqkv.at[i, :, j]
-    qkv_copies = far_start(qkv_at)
-    wo_at = lambda i, j: g.w_o.at[i, zx, j, c]
-    wo_copies = far_start(wo_at)
-    swap_c = swap(g.cot, g.cot_all.at[partner_slot], g.cot_all.at[p])
     loads_in.wait()
     for q in range(8):
         for k in range(4):
@@ -395,72 +392,191 @@
     g.w_in[zh, zx, y, c] = g.pi[p]
     loads_out.wait()
     g.w_out[zh, y] = g.f_out[...].astype(BF)
+    @pl.when(moves)
+    def _():
+        pl.semaphore_wait(barrier, 11)
+
+    @pl.when(stays)
+    def _():
+        pl.semaphore_wait(barrier, 10)
+
+    swaps = []
+
+    class Swap:
+        def __init__(self, src, dst_there, dst_here):
+            self.copy = tx.make(src, dst_there, partner)
+            self.here = pltpu.make_async_copy(src, dst_here, rsem.at[tx.count - 1])
+            swaps.append(self.copy)
+
+        def start(self):
+            pl.when(moves)(self.copy.start)
+            pl.when(stays)(self.here.start)
+
+        def wait_recv(self):
+            self.copy.wait_recv()
+
+    def swap(src, dst_there, dst_here):
+        copy = Swap(src, dst_there, dst_here)
+        copy.start()
+        return copy
+
+    def team_send(src, dst):
+        return [tx.send(src(slot(rel)), dst, near(rel)) for rel in TEAM]
+
+    def wait_all(copies):
+        for copy in copies:
+            copy.wait_recv()
+
+    vec_copies = [tx.send(g.vg1.at[p], g.vg1.at[p], near(rel)) for rel in TEAM]
+    qkv_copies = team_send(lambda q: g.pq.at[q], g.wqkv.at[zh, zx, y, c])
+    wo_far = FarGather(tx, far, zh, y, lambda i, j: g.w_o.at[i, zx, j, c])
+    wo_far.start()
+    half_rows, half_tok = R // 2, T // 2
+    early = half_rows - M
+    raw_here, raw_there = g.raw.at[p], g.raw.at[partner_slot]
+    cuts = [
+        (g.mem, pl.ds(0, M)),
+        (g.x.at[pl.ds(0, early)], pl.ds(M, early)),
+        (g.x.at[pl.ds(early, T - early)], pl.ds(half_rows, half_rows)),
+    ]
+    swap_m, swap_a, swap_b = [
+        swap(src, raw_there.at[to], raw_here.at[to]) for src, to in cuts
+    ]
+    swap_c = Swap(g.cot, g.cot_all.at[partner_slot], g.cot_all.at[p])
+    n_gather = TeamGather(
+        tx, near, slot, lambda q, h: g.raw.at[q, pl.ds(h * half_rows, half_rows)]
+    )
+    cot_gather = TeamGather(
+        tx, near, slot, lambda q, h: g.cot_all.at[q, pl.ds(h * half_tok, half_tok)]
+    )
+    wo_gather = TeamGather(
+        tx, near, slot, lambda q, h: g.w_o.at[h, q // 2, :, q % 2]
+    )
+    qkv_far = FarGather(tx, far, zh, y, lambda i, j: g.wqkv.at[i, :, j])
+    win_far = FarGather(tx, far, zh, y, lambda i, j: g.w_in.at[i, :, j])
+    wout_far = FarGather(tx, far, zh, y, lambda i, j: g.w_out.at[i, j])
+
+    def start_rows():
+        swap_m.wait_recv()
+        swap_a.wait_recv()
+        n_gather.start(0)
+        swap_b.wait_recv()
+        n_gather.start(1)
+
+    def start_cot():
+        swap_c.wait_recv()
+        cot_gather.start(0)
+        cot_gather.start(1)
+
+    @pl.when(stays)
+    def _():
+        swap_c.here.start()
+        start_rows()
+        start_cot()
+
+    wait_all(vec_copies)
+    for k in range(4):
+        g.vg2[e, k] = g.vg1[2 * k] + g.vg1[2 * k + 1]
+    vec_copies = [tx.send(g.vg2.at[e], g.vg2.at[e], far(rel)) for rel in FAR]
+    vec_copies += [tx.send(g.bslot.at[e], g.bslot.at[e], far(rel)) for rel in FAR]
+    wait_all(qkv_copies)
+    qkv_far.start()
+    wo_far.forward()
+
+    @pl.when(stays)
+    def _():
+        n_gather.forward()
+        cot_gather.forward()
+
+    @pl.when(moves)
+    def _():
+        start_rows()
+
+    wo_far.finish()
+    wo_gather.start(0)
+    wo_gather.start(1)
+
     wait_all(vec_copies)
     for k in range(8):
         group = g.vg2[2 * (k // 4), k % 4] + g.vg2[2 * (k // 4) + 1, k % 4]
         g.pg[k] = group
         g.prm[:, k * W : (k + 1) * W] = group
     prm = g.prm
-    half_rows = R // 2
-    n_gather = TeamGather(
-        tx, near, slot, lambda q, h: g.n_all.at[q, pl.ds(h * half_rows, half_rows)]
-    )
-
-    def norm_rows(src, first, count, at):
+
+    def norm_slot(rel, core):
+        at = 2 * (slot(rel) // 2) + core
+
         def step(i, _):
-            rows = pl.ds(pl.multiple_of(first + i * 32, 32), 32)
-            hat, _unused = norm_parts(src[rows, :].astype(F32))
-            out = (hat * prm[0:1] + prm[1:2]).astype(BF)
-            g.n_all[p, pl.ds(pl.multiple_of(at + i * 32, 32), 32), :] = out
+            rows = pl.ds(pl.multiple_of(i * 32, 32), 32)
+            hat, _unused = norm_parts(g.raw[at, rows, :].astype(F32))
+            g.n_all[at, rows, :] = (hat * prm[0:1] + prm[1:2]).astype(BF)
             return 0
 
-        lax.fori_loop(0, count // 32, step, 0)
-
-    swap_m.wait_recv()
-    norm_rows(g.xm, 0, M, 0)
-    swap_a.wait_recv()
-    norm_rows(g.xt, 0, early, M)
-    n_gather.start(0)
-    swap_b.wait_recv()
-    norm_rows(g.xt, early, T - early, M + early)
-    n_gather.start(1)
+        lax.fori_loop(0, R // 32, step, 0)
+
+    def early_rows(rel, step):
+        @pl.when(stays)
+        def _():
+            step()
+
+        @pl.when(moves)
+        def _():
+            n_gather.wait_sib(rel)
+
+        norm_slot(rel, zh)
+
+    def late_rows(rel, step):
+        @pl.when(moves)
+        def _():
+            step()
+
+        @pl.when(stays)
+        def _():
+            n_gather.wait_sib(rel)
+
+        norm_slot(rel, 1 - zh)
+
+    def nothing():
+        pass
+
+    early_rows((0, 0, 0), nothing)
+    early_rows(ZN, nothing)
+    early_rows(XN, n_gather.pass_xn)
+    early_rows((1, 1, 0), n_gather.pass_diag)
+
+    @pl.when(moves)
+    def _():
+        n_gather.forward()
+
+    qkv_far.forward()
+    late_rows((0, 0, 0), nothing)
+    late_rows(ZN, nothing)
+
+    wout_far.start()
+
+    @pl.when(moves)
+    def _():
+        swap_c.copy.start()
+
+    late_rows(XN, n_gather.pass_xn)
+    wo_gather.forward()
     win_copies = team_send(lambda q: g.pi.at[q], g.w_in.at[zh, zx, y, c])
-    far_forward(qkv_at, qkv_copies)
-    n_gather.forward(0)
-    n_gather.forward(1)
-    far_forward(wo_at, wo_copies)
-    wait_all(win_copies)
-    win_at = lambda i, j: g.w_in.at[i, :, j]
-    win_copies = far_start(win_at)
-    wout_at = lambda i, j: g.w_out.at[i, j]
-    wout_copies = far_start(wout_at)
-    n_gather.finish()
-    far_finish(qkv_copies)
-    wqkv = flat(g.wqkv[...].reshape(32, B, 3 * W))
+    qkv_far.finish()
+    wqkv = lambda: flat(g.wqkv[...].reshape(32, B, 3 * W))
     own_vec = g.pg[p]
     qkv_bias = jnp.concatenate(
         [own_vec[2:3], jnp.zeros((1, W), F32), own_vec[3:4]], axis=1
     )
 
-    def project(i, _):
-        rows = flat(g.n_all[pl.ds(2 * i, 2)])
-        out = dot(rows, wqkv) + qkv_bias
-        g.qkv[pl.ds(2 * i, 2)] = out.astype(BF).reshape(2, R, 3 * W)
-        return 0
-
-    lax.fori_loop(0, 4, project, 0)
-    far_finish(wo_copies)
-    wo_gather = TeamGather(
-        tx, near, slot, lambda q, h: g.w_o.at[h, q // 2, :, q % 2]
-    )
-    swap_c.wait_recv()
-    half_tok = T // 2
-    cot_gather = TeamGather(
-        tx, near, slot, lambda q, h: g.cot_all.at[q, pl.ds(h * half_tok, half_tok)]
-    )
-    for gather in (wo_gather, cot_gather):
-        gather.start(0)
-        gather.start(1)
+    def project(rel):
+        pair = pl.ds(2 * (slot(rel) // 2), 2)
+        out = dot(flat(g.n_all[pair]), wqkv()) + qkv_bias
+        g.qkv[pair] = out.astype(BF).reshape(2, R, 3 * W)
+
+    for rel in (SIB, ZN, XN):
+        project(rel)
+    late_rows((1, 1, 0), n_gather.pass_diag)
+    project((1, 1, 0))
     place = [
         g.order[4 * qc + 2 * qz + qx] for qz in (0, 1) for qx in (0, 1) for qc in (0, 1)
     ]
@@ -535,11 +651,21 @@
             parts.append(dot(w0, g.vv[:past, :]) + dot(w1, g.vv[past:end, :]))
         g.ctx[rows, :] = jnp.where(head_lanes[0], parts[0], parts[1])
 
+    wait_all(win_copies)
+
+    @pl.when(inner)
+    def _():
+        win_far.start()
+
     attend(0)
     attend(1)
+
+    @pl.when(moves)
+    def _():
+        start_cot()
+
+    wout_far.forward()
     attend(2)
-    wo_gather.forward(0)
-    wo_gather.forward(1)
     attend(3)
     def store_ctx(q, at, rows):
         g.ctx_send[q, pl.ds(at, 16), :] = rows.astype(BF)
@@ -547,15 +673,25 @@
     from_sorted(lambda j, at: g.ctx[pl.ds(j * T + at, 16), :], store_ctx)
     ctx_copies = team_send(lambda q: g.ctx_send.at[q], g.ctx_own.at[p])
     g.ctx_own[p] = g.ctx_send[p]
-    cot_gather.forward(0)
-    cot_gather.forward(1)
-    far_forward(win_at, win_copies)
+    @pl.when(outer)
+    def _():
+        win_far.start()
+
     wo_gather.finish()
+
+    @pl.when(moves)
+    def _():
+        cot_gather.forward()
+
+    @pl.when(outer)
+    def _():
+        win_far.forward()
+
     wait_all(ctx_copies)
     for q in range(8):
         g.ctx2d[:, q * W : (q + 1) * W] = g.ctx_own[q]
     w_o = lambda: flat(g.w_o[...].reshape(32, B, D))
-    g.mid[...] = dot(g.ctx2d[...], w_o()) + g.xt[...].astype(F32) + prm[4:5]
+    g.mid[...] = dot(g.ctx2d[...], w_o()) + g.raw[p, M:, :].astype(F32) + prm[4:5]
     n2_gather = TeamGather(
         tx, near, slot, lambda q, h: g.n2_all.at[q, pl.ds(h * half_tok, half_tok)]
     )
@@ -569,13 +705,19 @@
     for half in (0, 1):
         lax.fori_loop(half * (half_tok // 32), (half + 1) * (half_tok // 32), norm_mid, 0)
         n2_gather.start(half)
-    far_forward(wout_at, wout_copies)
-    n2_gather.forward(0)
-    n2_gather.forward(1)
+    n2_gather.forward()
+
+    @pl.when(inner)
+    def _():
+        win_far.forward()
+
+    n2_gather.pass_xn()
     cot_gather.finish()
-    n2_gather.finish()
-    far_finish(win_copies)
-    far_finish(wout_copies)
+    n2_gather.pass_diag()
+    for rel in QUADS:
+        n2_gather.wait_sib(rel)
+    win_far.finish()
+    wout_far.finish()
     tok_halves = [pl.ds(h * half_tok, half_tok) for h in (0, 1)]
     hidden_bias = jnp.concatenate([g.bslot[k, 0:1, :] for k in range(4)], axis=1)
     out_sum = TeamScatter(
@@ -604,18 +746,27 @@
         if order:
             n2_sum.add(order - 1)
     n2_sum.add(3)
+    out_sum.add(0)
+    out_sum.add(1)
     cot = lambda: flat(g.cot_all[...])
     for j in (1 - y, y):
         for k in range(2):
             g.gout_s[k, j] = dot_tn(g.act[2 * k + j], cot()).astype(BF)
-    gout_copy = tx.send(g.gout_s.at[:, 1 - y], g.gout_a, far((0, 1)))
+    gout_own = lambda i, j: g.gout_s.at[i, j]
+    gout_sum = FarSum(tx, far, zh, y, gout_own, g.gout_a, g.gout_b, g.gout_c)
+    gout_sum.start(1 - zh)
     n2_sum.turn()
-    out_sum.add(0)
+    out_sum.add(2)
+    out_sum.add(3)
     for k in range(4):
         grad = dot_tn(flat(g.n2_all[:, :, k * Q : (k + 1) * Q]), g.inner[...])
         cut = slice(2 * (k % 2), 2 * (k % 2) + 2)
         g.gin_s[k // 2, cut] = grad.astype(BF).reshape(2, 2, 2, B, H)
-    gin_copy = tx.send(g.gin_s.at[:, :, 1 - y], g.gin_a, far((0, 1)))
+    gin_own = lambda i, j: g.gin_s.at[i, :, j]
+    gin_sum = FarSum(tx, far, zh, y, gin_own, g.gin_a, g.gin_b, g.gin_c)
+    gin_sum.start(1 - zh)
+    gout_sum.start(zh)
+    gin_sum.start(zh)
     inner_sum = col_sum(g.inner[...])
     for k in range(4):
         g.bp[k] = jnp.broadcast_to(inner_sum[:, k * H4 : (k + 1) * H4], (8, H4))
@@ -623,6 +774,7 @@
     for i, rel in enumerate(FAR):
         to = 2 * ((zh + rel[0]) % 2) + (y + rel[1]) % 2
         gb_copies.append(tx.send(g.bp.at[to], g.br.at[i], far(rel)))
+    gout_sum.turn()
     g.mg[...] = n2_sum.total(p)
     def norm_two_back(i, sums):
         rows = pl.ds(pl.multiple_of(i * 32, 32), 32)
@@ -653,8 +805,8 @@
         g.cg_send[q] = cg[:, q * W : (q + 1) * W]
     cg_copies = team_send(lambda q: g.cg_send.at[q], g.cg_all.at[p])
     g.cg_all[p] = g.cg_send[p]
-    for order in (1, 2, 3):
-        out_sum.add(order)
+    out_sum.turn()
+    gin_sum.turn()
     for k in range(4):
         grad = dot_tn(g.ctx2d[:, k * Q : (k + 1) * Q], attg)
         cut = slice(2 * (k % 2), 2 * (k % 2) + 2)
@@ -665,19 +817,6 @@
     for order in range(4):
         o_sum.push(order)
 
-    def far_turn(copy, own, got, out, last):
-        copy.wait_recv()
-        out[...] = (own(1 - zh)[...].astype(F32) + got[1 - zh].astype(F32)).astype(BF)
-        return tx.send(out, last, far((1, 0)))
-
-    def far_total(copy, own, got, last):
-        copy.wait_recv()
-        return own(zh)[...].astype(F32) + got[zh].astype(F32) + last[...].astype(F32)
-
-    gout_own = lambda i: g.gout_s.at[i, y]
-    gin_own = lambda i: g.gin_s.at[i, :, y]
-    gqkv_own = lambda i: g.gqkv_s.at[i, :, y]
-    go_own = lambda i: g.go_s.at[i, y]
     wait_all(cg_copies)
 
     def store_cg(j, at, rows):
@@ -707,9 +846,9 @@
 
     attend_back(0)
     attend_back(1)
-    gout_copy = far_turn(gout_copy, gout_own, g.gout_a, g.gout_b, g.gout_c)
+    for order in range(4):
+        o_sum.add(order)
     attend_back(2)
-    out_sum.turn()
     attend_back(3)
     def load_grads(j, at):
         keys = pl.ds(MK + j * T + at, 16)
@@ -732,13 +871,11 @@
     for order in range(4):
         pair = 2 * (slot(QUADS[order]) // 2)
         rows = flat(g.dqkv[pl.ds(pair, 2), M:, :])
-        w = flat(g.wqkv[...].reshape(32, B, 3 * W))
-        g.pb_n[pl.ds(pair, 2)] = dot_nt(rows, w).astype(BF).reshape(2, T, D)
+        g.pb_n[pl.ds(pair, 2)] = dot_nt(rows, wqkv()).astype(BF).reshape(2, T, D)
         n_sum.push(order)
         if order:
             n_sum.add(order - 1)
     n_sum.add(3)
-    gin_copy = far_turn(gin_copy, gin_own, g.gin_a, g.gin_b, g.gin_c)
     g.vp[...] = jnp.zeros_like(g.vp)
     qkv_sum = jnp.zeros((1, 3 * W), F32)
     for q in range(8):
@@ -758,7 +895,10 @@
             vec = g.pg[2 * k + i]
             g.vp[2 * k + i, 0:1, :] = (gains[0:1, at] - vec[1:2] * shift) / vec[0:1]
             g.vp[2 * k + i, 1:2, :] = shift
-    gqkv_copy = tx.send(g.gqkv_s.at[:, :, 1 - y], g.gqkv_a, far((0, 1)))
+    gqkv_own = lambda i, j: g.gqkv_s.at[i, :, j]
+    gqkv_sum = FarSum(tx, far, zh, y, gqkv_own, g.gqkv_a, g.gqkv_b, g.gqkv_c)
+    gqkv_sum.start(1 - zh)
+    gqkv_sum.start(zh)
     n_sum.turn()
     g.vp[p, 2:3, :] = qkv_sum[:, :W]
     g.vp[p, 3:4, :] = qkv_sum[:, 2 * W :]
@@ -772,19 +912,17 @@
     for i, rel in enumerate(FAR):
         to = pl.ds(4 * ((zh + rel[0]) % 2), 4)
         vec_copies.append(tx.send(g.vp.at[to], g.vr.at[i], far(rel)))
-    for order in range(4):
-        o_sum.add(order)
     lo = out_sum.total(p) + g.mid[...] + prm[7:8]
     g.lo_s[...] = lo.astype(BF)
     swap_lo = swap(g.lo_s, g.lo, g.lo)
-    gqkv_copy = far_turn(gqkv_copy, gqkv_own, g.gqkv_a, g.gqkv_b, g.gqkv_c)
+    gqkv_sum.turn()
     o_sum.turn()
-    g.gout[...] = far_total(gout_copy, gout_own, g.gout_a, g.gout_c)
-    g.gin_d[...] = flat_team(far_total(gin_copy, gin_own, g.gin_a, g.gin_c))
+    g.gout[...] = gout_sum.total()
+    g.gin_d[...] = flat_team(gin_sum.total())
     gin_copies = team_send(lambda q: g.gin_d.at[q], g.gin_e.at[p])
     g.gin_e[p] = g.gin_d[p]
     wait_all(gb_copies)
-    g.gbin[...] = g.bp[e] + g.br[0] + g.br[1] + g.br[2]
+    g.gbin[...] = (g.bp[e] + g.br[0] + g.br[1] + g.br[2])[:1]
     wait_all(vec_copies)
     g.vs[...] = g.vp[pl.ds(4 * zh, 4)] + g.vr[0] + g.vr[1] + g.vr[2]
     vec_copies = team_send(lambda q: g.vs.at[q // 2], g.va.at[p])
@@ -793,7 +931,9 @@
 
     def norm_one_back(i, _):
         rows = pl.ds(pl.multiple_of(i * 32, 32), 32)
-        hat, scale = norm_parts(g.xt[rows, :].astype(F32))
+        hat, scale = norm_parts(
+            g.raw[p, pl.ds(pl.multiple_of(M + i * 32, 32), 32), :].astype(F32)
+        )
         pull = g.mid[rows, :] * prm[0:1]
         mean = jnp.mean(pull, axis=-1, keepdims=True)
         along_hat = jnp.mean(pull * hat, axis=-1, keepdims=True)
@@ -803,17 +943,20 @@
 
     lax.fori_loop(0, T // 32, norm_one_back, 0)
     swap_ig = swap(g.ig_s, g.ig, g.ig)
-    g.gqkv_d[...] = flat_team(far_total(gqkv_copy, gqkv_own, g.gqkv_a, g.gqkv_c))
+    g.gqkv_d[...] = flat_team(gqkv_sum.total())
     gqkv_copies = team_send(lambda q: g.gqkv_d.at[q], g.gqkv_e.at[p])
     g.gqkv_e[p] = g.gqkv_d[p]
     g.go_s[...] = o_sum.total(p).astype(BF)
-    go_copy = tx.send(g.go_s.at[:, 1 - y], g.go_a, far((0, 1)))
+    go_own = lambda i, j: g.go_s.at[i, j]
+    go_sum = FarSum(tx, far, zh, y, go_own, g.go_a, g.go_b, g.go_c)
+    go_sum.start(1 - zh)
+    go_sum.start(zh)
     wait_all(gin_copies)
     for q in range(8):
         for k in range(4):
             at = (16 * (k // 2) + 4 * (q // 2) + 2 * (k % 2) + q % 2) * H4
             g.gin[:, at : at + H4] = g.gin_e[q, :, k * H4 : (k + 1) * H4].astype(F32)
-    go_copy = far_turn(go_copy, go_own, g.go_a, g.go_b, g.go_c)
+    go_sum.turn()
     wait_all(vec_copies)
     total = g.va[0]
     for q in range(1, 8):
@@ -823,7 +966,7 @@
     for q in range(8):
         for i, out in enumerate((g.gq, g.gk, g.gv)):
             out[:, q * W : (q + 1) * W] = g.gqkv_e[q, :, i * W : (i + 1) * W].astype(F32)
-    g.go[...] = far_total(go_copy, go_own, g.go_a, g.go_c)
+    g.go[...] = go_sum.total()
     swap_lo.wait_recv()
     swap_ig.wait_recv()
     tx.drain()
@@ -836,6 +979,32 @@
 
 def flat_team(value):
     return value.astype(BF).reshape((8,) + value.shape[2:])
+
+
+def finish_kernel(share, *refs):
+    ins, outs, held = refs[:10], refs[10:20], refs[20:30]
+    wide, picked, sems = refs[30:]
+    loads = [pltpu.make_async_copy(ins[i], held[i], sems.at[i]) for i in range(10)]
+    for copy in loads:
+        copy.start()
+    stores = []
+    for i in (0, 2, 3, 4, 5, 6, 7, 9, 1, 8):
+        loads[i].wait()
+        src = held[i]
+        if i == 1:
+            wide[...] = src[...].astype(F32)
+            src = wide
+        if i == 8:
+            mine = lax.axis_index("dp")
+            part = src[:, :share]
+            for k in range(1, src.shape[1] // share):
+                part = jnp.where(mine == k, src[:, k * share : (k + 1) * share], part)
+            picked[...] = part
+            src = picked
+        stores.append(pltpu.make_async_copy(src, outs[i], sems.at[10 + i]))
+        stores[-1].start()
+    for copy in stores:
+        copy.wait()
 
 
 def run_layer(layer_input, memory, cotangent, block_order, w_query, w_key, w_value, w_output, w_in, w_out, vectors, b_in):
@@ -860,7 +1029,7 @@
             jax.ShapeDtypeStruct(w_in.shape, F32),
             jax.ShapeDtypeStruct(w_out.shape, F32),
             jax.ShapeDtypeStruct((8, W), F32),
-            jax.ShapeDtypeStruct((8, b_in.shape[0]), F32),
+            jax.ShapeDtypeStruct((1, b_in.shape[0]), F32),
         ),
         in_specs=[hbm, hbm, hbm, smem] + [hbm] * 6 + [vmem] * 2,
         out_specs=[vmem] * 10,
@@ -870,9 +1039,23 @@
             collective_id=0, has_side_effects=True, vmem_limit_bytes=63 * 2**20
         ),
     )(layer_input[0], memory[0], cotangent[0], block_order, w_query, w_key, w_value, w_output, w_in, w_out, vectors, b_in[None])
-    lo, ig, gq, gk, gv, go, gin, gout, gvec, gbin = outs
-    gvec = lax.dynamic_slice(gvec, (0, lax.axis_index("dp") * share), (8, share))
-    return (lo[None], ig.astype(F32)[None], gq, gk, gv, go, gin, gout, gvec, gbin[0])
+    final = [jax.ShapeDtypeStruct(outs[0].shape, BF), jax.ShapeDtypeStruct(outs[1].shape, F32)]
+    final += [jax.ShapeDtypeStruct(out.shape, F32) for out in outs[2:8]]
+    final += [jax.ShapeDtypeStruct((8, share), F32), jax.ShapeDtypeStruct((1, b_in.shape[0]), F32)]
+    lo, ig, gq, gk, gv, go, gin, gout, gvec, gbin = pl.pallas_call(
+        functools.partial(finish_kernel, share),
+        out_shape=final,
+        in_specs=[hbm] * 10,
+        out_specs=[hbm] * 10,
+        scratch_shapes=[pltpu.VMEM(out.shape, out.dtype) for out in outs]
+        + [
+            pltpu.VMEM((T, D), F32),
+            pltpu.VMEM((8, share), F32),
+            pltpu.SemaphoreType.DMA((20,)),
+        ],
+        compiler_params=pltpu.CompilerParams(vmem_limit_bytes=60 * 2**20),
+    )(*outs)
+    return (lo[None], ig[None], gq, gk, gv, go, gin, gout, gvec, gbin[0])
 
 
 masked_value = -1e30

time: 186 us -> 177 us (0.952)
  local copies, waits for them, and re-layouts: 7.8 us -> 0 us
    unnamed x23 -> x0, local copies, waits for them, and re-layouts: 5.95 us -> none
    pallas_call x0 -> x1, Pallas kernels: none -> 2.69 us  [run_layer(): pl.pallas_call(functools.partial(finish_kernel, share), out_shape=final,...]
    pallas_call x1, Pallas kernels: 175 us -> 173 us  [run_layer(): pl.pallas_call(functools.partial(layer_kernel, T, M, D, FF, share), out_s...]
where the time goes in v3:
time: 177 us; the launch traced here: 176 us
  Pallas kernels  176 us (99%)
    pallas_call x1, Pallas kernels, run_layer(): pl.pallas_call(functools.partial(layer_kernel, T, M, D, FF, share), out_s...  173 us

profile of v3, /device:TPU:0, one launch (start us, length us, event | category | flops | bytes accessed | tf_op | source)
XLA Modules:
  0.0 176.4 jit_solution(17763699541020174871)
XLA Ops:
  0.6 172.9 %shard_map.195 = (bf16[128,1024]{1,0:T(8,128)(2,1)}, bf16[128,1024]{1,0:T(8,128)(2,1)}, f32[32,1024]{1,0:T(8,128)}, f32[32,1024]{1,0:T(8,128)}, f32[32,1024]{1,0...) custom-call(bf16[128,1024]{1,0:T(8,128)(2,1)} %bitcast.7, ...), custom_call_target="tpu_custom_call" | custom-call | tf_op jit(solution)/shard_map/pallas_call | solution.py:1020
  173.5 2.7 %shard_map.196 = (bf16[128,1024]{1,0:T(8,128)(2,1)}, f32[128,1024]{1,0:T(8,128)}, f32[32,1024]{1,0:T(8,128)}, f32[32,1024]{1,0:T(8,128)}, f32[32,1024]{1,0:T(8,1...) custom-call(bf16[128,1024]{1,0:T(8,128)(2,1)} %get-tuple-element.30., ...), custom_call_target="tpu_custom_call" | custom-call | tf_op jit(solution)/shard_map/pallas_call | solution.py:1045

commit v4 on v3

--- a/solution.py
+++ b/solution.py
@@ -118,11 +118,11 @@
         cg_all=((8, T, W), BF),
         pb_o=(grid + (D,), BF),
         r1_o=((4, 2, 2, B, D), BF),
-        rx_o=((2, 2, 2, B, D), BF),
-        rz_o=((2, 2, B, D), BF),
-        go_s=((2, 2, B, D), BF),
-        go_a=((2, B, D), BF),
-        go_b=((B, D), BF),
+        rx_o=((2, 2, B, D), BF),
+        rz_o=((2, B, D), BF),
+        go_y=((2, 4, B, D), BF),
+        go_m=((4, 2, B, D), BF),
+        go_s=((2, B, D), BF),
         go_c=((B, D), BF),
         cg_sorted=((S, W), BF),
         dq=((S, W), F32),
@@ -270,16 +270,23 @@
         src = self.buf(self.slot((rel[0], rel[1], 1)))
         self.sib[order] = self.tx.send(src, self.first.at[order], self.near(SIB))
 
-    def add(self, order):
+    def sum(self, order, half):
+        own = self.buf(self.slot(QUADS[order]))
+        part, more = own.at[half], self.first.at[order].at[half]
+        part[...] = (part[...].astype(F32) + more[...].astype(F32)).astype(BF)
+
+    def hand(self, order, half):
+        part = self.buf(self.slot(QUADS[order])).at[half]
+        to = self.cross.at[order].at[half]
+        copy = self.tx.send(part, to, self.near(XN))
+        (self.ended if order else self.turned).append(copy)
+
+    def add(self, order, hand=True):
         self.sib[order].wait_recv()
-        own = self.buf(self.slot(QUADS[order]))
         for half in self.halves:
-            part, more = own.at[half], self.first.at[order].at[half]
-            part[...] = (part[...].astype(F32) + more[...].astype(F32)).astype(BF)
-            if order == 0:
-                self.turned.append(self.tx.send(part, self.cross.at[0].at[half], self.near(XN)))
-            if order == 1:
-                self.ended.append(self.tx.send(part, self.cross.at[1].at[half], self.near(XN)))
+            self.sum(order, half)
+            if hand and order < 2:
+                self.hand(order, half)
 
     def turn(self):
         own = self.buf(self.slot(ZN))
@@ -547,20 +554,15 @@
     @pl.when(moves)
     def _():
         n_gather.forward()
+        swap_c.copy.start()
 
     qkv_far.forward()
     late_rows((0, 0, 0), nothing)
     late_rows(ZN, nothing)
-
-    wout_far.start()
-
-    @pl.when(moves)
-    def _():
-        swap_c.copy.start()
-
+    win_copies = team_send(lambda q: g.pi.at[q], g.w_in.at[zh, zx, y, c])
     late_rows(XN, n_gather.pass_xn)
     wo_gather.forward()
-    win_copies = team_send(lambda q: g.pi.at[q], g.w_in.at[zh, zx, y, c])
+    wout_far.start()
     qkv_far.finish()
     wqkv = lambda: flat(g.wqkv[...].reshape(32, B, 3 * W))
     own_vec = g.pg[p]
@@ -664,7 +666,6 @@
     def _():
         start_cot()
 
-    wout_far.forward()
     attend(2)
     attend(3)
     def store_ctx(q, at, rows):
@@ -677,16 +678,13 @@
     def _():
         win_far.start()
 
-    wo_gather.finish()
+    wout_far.forward()
 
     @pl.when(moves)
     def _():
         cot_gather.forward()
 
-    @pl.when(outer)
-    def _():
-        win_far.forward()
-
+    wo_gather.finish()
     wait_all(ctx_copies)
     for q in range(8):
         g.ctx2d[:, q * W : (q + 1) * W] = g.ctx_own[q]
@@ -706,11 +704,7 @@
         lax.fori_loop(half * (half_tok // 32), (half + 1) * (half_tok // 32), norm_mid, 0)
         n2_gather.start(half)
     n2_gather.forward()
-
-    @pl.when(inner)
-    def _():
-        win_far.forward()
-
+    win_far.forward()
     n2_gather.pass_xn()
     cot_gather.finish()
     n2_gather.pass_diag()
@@ -747,7 +741,6 @@
             n2_sum.add(order - 1)
     n2_sum.add(3)
     out_sum.add(0)
-    out_sum.add(1)
     cot = lambda: flat(g.cot_all[...])
     for j in (1 - y, y):
         for k in range(2):
@@ -766,7 +759,6 @@
     gin_sum = FarSum(tx, far, zh, y, gin_own, g.gin_a, g.gin_b, g.gin_c)
     gin_sum.start(1 - zh)
     gout_sum.start(zh)
-    gin_sum.start(zh)
     inner_sum = col_sum(g.inner[...])
     for k in range(4):
         g.bp[k] = jnp.broadcast_to(inner_sum[:, k * H4 : (k + 1) * H4], (8, H4))
@@ -805,17 +797,18 @@
         g.cg_send[q] = cg[:, q * W : (q + 1) * W]
     cg_copies = team_send(lambda q: g.cg_send.at[q], g.cg_all.at[p])
     g.cg_all[p] = g.cg_send[p]
-    out_sum.turn()
-    gin_sum.turn()
+    out_sum.add(1)
     for k in range(4):
         grad = dot_tn(g.ctx2d[:, k * Q : (k + 1) * Q], attg)
         cut = slice(2 * (k % 2), 2 * (k % 2) + 2)
         g.pb_o[k // 2, cut] = grad.astype(BF).reshape(2, 2, 2, B, D)
     o_sum = TeamScatter(
-        tx, near, slot, lambda q: g.pb_o.at[:, q // 2, :, q % 2], g.r1_o, g.rx_o, g.rz_o, [0, 1]
+        tx, near, slot, lambda q: g.pb_o.at[:, q // 2, :, q % 2], g.r1_o, None, None, [0, 1]
     )
     for order in range(4):
         o_sum.push(order)
+    out_sum.turn()
+    gin_sum.turn()
 
     wait_all(cg_copies)
 
@@ -845,9 +838,10 @@
         g.dq[rows, :] = jnp.where(head_lanes[0], parts[0], parts[1]) * 0.125
 
     attend_back(0)
+    for order in range(4):
+        o_sum.add(order, hand=False)
+    go_copy = tx.send(g.pb_o.at[:, :, 1 - y, c], g.go_y, far((0, 1)))
     attend_back(1)
-    for order in range(4):
-        o_sum.add(order)
     attend_back(2)
     attend_back(3)
     def load_grads(j, at):
@@ -876,30 +870,38 @@
         if order:
             n_sum.add(order - 1)
     n_sum.add(3)
+    lo = out_sum.total(p) + g.mid[...] + prm[7:8]
+    g.lo_s[...] = lo.astype(BF)
+    swap_lo = swap(g.lo_s, g.lo, g.lo)
     g.vp[...] = jnp.zeros_like(g.vp)
     qkv_sum = jnp.zeros((1, 3 * W), F32)
     for q in range(8):
         qkv_sum = qkv_sum + col_sum(g.dqkv[q])
     qkv_sum8 = jnp.broadcast_to(qkv_sum, (8, 3 * W))
     ones = jnp.ones((8, 3 * W), F32)
+    gains = []
     for k in range(4):
         grad = dot_tn(flat(g.n_all[:, :, k * Q : (k + 1) * Q]), flat(g.dqkv[...]))
         cut = slice(2 * (k % 2), 2 * (k % 2) + 2)
         g.gqkv_s[k // 2, cut] = grad.astype(BF).reshape(2, 2, 2, B, 3 * W)
         w = flat(g.wqkv[k // 2, cut].reshape(8, B, 3 * W)).astype(F32)
-        gains = dot_nt(ones, grad * w, EXACT)
+        gains.append(dot_nt(ones, grad * w, EXACT)[0:1])
+    gqkv_own = lambda i, j: g.gqkv_s.at[i, :, j]
+    gqkv_sum = FarSum(tx, far, zh, y, gqkv_own, g.gqkv_a, g.gqkv_b, g.gqkv_c)
+    gqkv_sum.start(1 - zh)
+    gin_sum.start(zh)
+    gqkv_sum.start(zh)
+    n_sum.turn()
+    for k in range(4):
+        cut = slice(2 * (k % 2), 2 * (k % 2) + 2)
+        w = flat(g.wqkv[k // 2, cut].reshape(8, B, 3 * W)).astype(F32)
         shifts = dot_nt(qkv_sum8, w, EXACT)
         for i in range(2):
             at = slice(i * W, (i + 1) * W)
             shift = shifts[0:1, at]
             vec = g.pg[2 * k + i]
-            g.vp[2 * k + i, 0:1, :] = (gains[0:1, at] - vec[1:2] * shift) / vec[0:1]
+            g.vp[2 * k + i, 0:1, :] = (gains[k][:, at] - vec[1:2] * shift) / vec[0:1]
             g.vp[2 * k + i, 1:2, :] = shift
-    gqkv_own = lambda i, j: g.gqkv_s.at[i, :, j]
-    gqkv_sum = FarSum(tx, far, zh, y, gqkv_own, g.gqkv_a, g.gqkv_b, g.gqkv_c)
-    gqkv_sum.start(1 - zh)
-    gqkv_sum.start(zh)
-    n_sum.turn()
     g.vp[p, 2:3, :] = qkv_sum[:, :W]
     g.vp[p, 3:4, :] = qkv_sum[:, 2 * W :]
     for k in range(8):
@@ -912,11 +914,17 @@
     for i, rel in enumerate(FAR):
         to = pl.ds(4 * ((zh + rel[0]) % 2), 4)
         vec_copies.append(tx.send(g.vp.at[to], g.vr.at[i], far(rel)))
-    lo = out_sum.total(p) + g.mid[...] + prm[7:8]
-    g.lo_s[...] = lo.astype(BF)
-    swap_lo = swap(g.lo_s, g.lo, g.lo)
+    go_copy.wait_recv()
+    for k in range(4):
+        total = g.pb_o[:, k, y, c].astype(F32) + g.go_y[:, k].astype(F32)
+        g.go_m[k] = total.astype(BF)
+    go_team = TeamScatter(
+        tx, near, slot, lambda q: g.go_m.at[q // 2], None, g.rx_o, g.rz_o, [0, 1]
+    )
+    for order in (0, 1):
+        for half in (0, 1):
+            go_team.hand(order, half)
     gqkv_sum.turn()
-    o_sum.turn()
     g.gout[...] = gout_sum.total()
     g.gin_d[...] = flat_team(gin_sum.total())
     gin_copies = team_send(lambda q: g.gin_d.at[q], g.gin_e.at[p])
@@ -943,20 +951,17 @@
 
     lax.fori_loop(0, T // 32, norm_one_back, 0)
     swap_ig = swap(g.ig_s, g.ig, g.ig)
+    go_team.turn()
     g.gqkv_d[...] = flat_team(gqkv_sum.total())
     gqkv_copies = team_send(lambda q: g.gqkv_d.at[q], g.gqkv_e.at[p])
     g.gqkv_e[p] = g.gqkv_d[p]
-    g.go_s[...] = o_sum.total(p).astype(BF)
-    go_own = lambda i, j: g.go_s.at[i, j]
-    go_sum = FarSum(tx, far, zh, y, go_own, g.go_a, g.go_b, g.go_c)
-    go_sum.start(1 - zh)
-    go_sum.start(zh)
+    g.go_s[...] = go_team.total(p).astype(BF)
+    go_copy = tx.send(g.go_s.at[1 - zh], g.go_c, far((1, 0)))
     wait_all(gin_copies)
     for q in range(8):
         for k in range(4):
             at = (16 * (k // 2) + 4 * (q // 2) + 2 * (k % 2) + q % 2) * H4
             g.gin[:, at : at + H4] = g.gin_e[q, :, k * H4 : (k + 1) * H4].astype(F32)
-    go_sum.turn()
     wait_all(vec_copies)
     total = g.va[0]
     for q in range(1, 8):
@@ -966,7 +971,8 @@
     for q in range(8):
         for i, out in enumerate((g.gq, g.gk, g.gv)):
             out[:, q * W : (q + 1) * W] = g.gqkv_e[q, :, i * W : (i + 1) * W].astype(F32)
-    g.go[...] = go_sum.total()
+    go_copy.wait_recv()
+    g.go[...] = g.go_s[zh].astype(F32) + g.go_c[...].astype(F32)
     swap_lo.wait_recv()
     swap_ig.wait_recv()
     tx.drain()

time: 177 us -> 167 us (0.944)
  Pallas kernels: 176 us -> 166 us
    pallas_call x1, Pallas kernels: 173 us -> 163 us  [run_layer(): pl.pallas_call(functools.partial(layer_kernel, T, M, D, FF, share), out_s...]
where the time goes in v4:
time: 167 us
  Pallas kernels  166 us (99%)
    pallas_call x1, Pallas kernels, run_layer(): pl.pallas_call(functools.partial(layer_kernel, T, M, D, FF, share), out_s...  163 us

profile of v4, /device:TPU:0, one launch (start us, length us, event | category | flops | bytes accessed | tf_op | source)
XLA Modules:
  0.0 167.0 jit_solution(1052273354180090154)
XLA Ops:
  0.6 163.4 %shard_map.195 = (bf16[128,1024]{1,0:T(8,128)(2,1)}, bf16[128,1024]{1,0:T(8,128)(2,1)}, f32[32,1024]{1,0:T(8,128)}, f32[32,1024]{1,0:T(8,128)}, f32[32,1024]{1,0...) custom-call(bf16[128,1024]{1,0:T(8,128)(2,1)} %bitcast.7, ...), custom_call_target="tpu_custom_call" | custom-call | tf_op jit(solution)/shard_map/pallas_call | solution.py:1026
  164.1 2.7 %shard_map.196 = (bf16[128,1024]{1,0:T(8,128)(2,1)}, f32[128,1024]{1,0:T(8,128)}, f32[32,1024]{1,0:T(8,128)}, f32[32,1024]{1,0:T(8,128)}, f32[32,1024]{1,0:T(8,1...) custom-call(bf16[128,1024]{1,0:T(8,128)(2,1)} %get-tuple-element.30., ...), custom_call_target="tpu_custom_call" | custom-call | tf_op jit(solution)/shard_map/pallas_call | solution.py:1051

commit v5 on v4

--- a/solution.py
+++ b/solution.py
@@ -296,6 +296,16 @@
             part[...] = (part[...].astype(F32) + more[...].astype(F32)).astype(BF)
             self.ended.append(self.tx.send(part, self.last.at[half], self.near(ZN)))
 
+    def total_half(self, own, at):
+        half = self.halves[at]
+        self.ended[at].wait_recv()
+        self.ended[2 + at].wait_recv()
+        return (
+            self.buf(own).at[half][...].astype(F32)
+            + self.cross.at[1].at[half][...].astype(F32)
+            + self.last.at[half][...].astype(F32)
+        )
+
     def total(self, own):
         for copy in self.ended:
             copy.wait_recv()
@@ -735,11 +745,16 @@
             g.act[k, at, :] = act[:, k * H4 : (k + 1) * H4]
         g.pb_b[pl.ds(pair, 2)] = dot_nt(inner_grad, w_in).astype(BF).reshape(2, T, D)
         n2_sum.push(order)
-        g.pb_a[pl.ds(pair, 2)] = dot(act, w_out).astype(BF).reshape(2, T, D)
-        out_sum.push(order)
         if order:
             n2_sum.add(order - 1)
     n2_sum.add(3)
+    for order in range(4):
+        pair = 2 * (slot(QUADS[order]) // 2)
+        at = pl.ds(pl.multiple_of(pair * T, 2 * T), 2 * T)
+        act = jnp.concatenate([g.act[k, at, :] for k in range(4)], axis=1)
+        out = dot(act, g.w_out[...].reshape(H, D))
+        g.pb_a[pl.ds(pair, 2)] = out.astype(BF).reshape(2, T, D)
+        out_sum.push(order)
     out_sum.add(0)
     cot = lambda: flat(g.cot_all[...])
     for j in (1 - y, y):
@@ -766,8 +781,6 @@
     for i, rel in enumerate(FAR):
         to = 2 * ((zh + rel[0]) % 2) + (y + rel[1]) % 2
         gb_copies.append(tx.send(g.bp.at[to], g.br.at[i], far(rel)))
-    gout_sum.turn()
-    g.mg[...] = n2_sum.total(p)
     def norm_two_back(i, sums):
         rows = pl.ds(pl.multiple_of(i * 32, 32), 32)
         up = g.mg[rows, :]
@@ -788,9 +801,12 @@
         )
 
     zero_row = jnp.zeros((1, D), F32)
-    gain_two, shift_two, bias_o, bias_out = lax.fori_loop(
-        0, T // 32, norm_two_back, (zero_row, zero_row, zero_row, zero_row)
-    )
+    sums = (zero_row, zero_row, zero_row, zero_row)
+    steps = half_tok // 32
+    for half in (0, 1):
+        g.mg[tok_halves[half], :] = n2_sum.total_half(p, half)
+        sums = lax.fori_loop(half * steps, (half + 1) * steps, norm_two_back, sums)
+    gain_two, shift_two, bias_o, bias_out = sums
     attg = g.attg[...]
     cg = dot_nt(attg, w_o()).astype(BF)
     for q in range(8):
@@ -807,8 +823,8 @@
     )
     for order in range(4):
         o_sum.push(order)
+    gout_sum.turn()
     out_sum.turn()
-    gin_sum.turn()
 
     wait_all(cg_copies)
 
@@ -842,6 +858,7 @@
         o_sum.add(order, hand=False)
     go_copy = tx.send(g.pb_o.at[:, :, 1 - y, c], g.go_y, far((0, 1)))
     attend_back(1)
+    gin_sum.turn()
     attend_back(2)
     attend_back(3)
     def load_grads(j, at):
@@ -870,9 +887,6 @@
         if order:
             n_sum.add(order - 1)
     n_sum.add(3)
-    lo = out_sum.total(p) + g.mid[...] + prm[7:8]
-    g.lo_s[...] = lo.astype(BF)
-    swap_lo = swap(g.lo_s, g.lo, g.lo)
     g.vp[...] = jnp.zeros_like(g.vp)
     qkv_sum = jnp.zeros((1, 3 * W), F32)
     for q in range(8):
@@ -925,6 +939,9 @@
         for half in (0, 1):
             go_team.hand(order, half)
     gqkv_sum.turn()
+    lo = out_sum.total(p) + g.mid[...] + prm[7:8]
+    g.lo_s[...] = lo.astype(BF)
+    swap_lo = swap(g.lo_s, g.lo, g.lo)
     g.gout[...] = gout_sum.total()
     g.gin_d[...] = flat_team(gin_sum.total())
     gin_copies = team_send(lambda q: g.gin_d.at[q], g.gin_e.at[p])
@@ -935,8 +952,6 @@
     g.vs[...] = g.vp[pl.ds(4 * zh, 4)] + g.vr[0] + g.vr[1] + g.vr[2]
     vec_copies = team_send(lambda q: g.vs.at[q // 2], g.va.at[p])
     g.va[p] = g.vs[zx]
-    g.mid[...] = n_sum.total(p)
-
     def norm_one_back(i, _):
         rows = pl.ds(pl.multiple_of(i * 32, 32), 32)
         hat, scale = norm_parts(
@@ -949,8 +964,12 @@
         g.ig_s[rows, :] = out.astype(BF)
         return 0
 
-    lax.fori_loop(0, T // 32, norm_one_back, 0)
-    swap_ig = swap(g.ig_s, g.ig, g.ig)
+    swap_ig = []
+    for half in (0, 1):
+        at = tok_halves[half]
+        g.mid[at, :] = n_sum.total_half(p, half)
+        lax.fori_loop(half * steps, (half + 1) * steps, norm_one_back, 0)
+        swap_ig.append(swap(g.ig_s.at[at], g.ig.at[at], g.ig.at[at]))
     go_team.turn()
     g.gqkv_d[...] = flat_team(gqkv_sum.total())
     gqkv_copies = team_send(lambda q: g.gqkv_d.at[q], g.gqkv_e.at[p])
@@ -974,7 +993,8 @@
     go_copy.wait_recv()
     g.go[...] = g.go_s[zh].astype(F32) + g.go_c[...].astype(F32)
     swap_lo.wait_recv()
-    swap_ig.wait_recv()
+    for copy in swap_ig:
+        copy.wait_recv()
     tx.drain()
 
     @pl.when(moves)

time: 167 us -> 162 us (0.970)
  Pallas kernels: 166 us -> 161 us
    pallas_call x1, Pallas kernels: 163 us -> 158 us  [run_layer(): pl.pallas_call(functools.partial(layer_kernel, T, M, D, FF, share), out_s...]
where the time goes in v5:
time: 162 us
  Pallas kernels  161 us (99%)
    pallas_call x1, Pallas kernels, run_layer(): pl.pallas_call(functools.partial(layer_kernel, T, M, D, FF, share), out_s...  158 us

profile of v5, /device:TPU:0, one launch (start us, length us, event | category | flops | bytes accessed | tf_op | source)
XLA Modules:
  0.0 161.6 jit_solution(17083944177454512731)
XLA Ops:
  0.6 158.0 %shard_map.195 = (bf16[128,1024]{1,0:T(8,128)(2,1)}, bf16[128,1024]{1,0:T(8,128)(2,1)}, f32[32,1024]{1,0:T(8,128)}, f32[32,1024]{1,0:T(8,128)}, f32[32,1024]{1,0...) custom-call(bf16[128,1024]{1,0:T(8,128)(2,1)} %bitcast.7, ...), custom_call_target="tpu_custom_call" | custom-call | tf_op jit(solution)/shard_map/pallas_call | solution.py:1046
  158.7 2.7 %shard_map.196 = (bf16[128,1024]{1,0:T(8,128)(2,1)}, f32[128,1024]{1,0:T(8,128)}, f32[32,1024]{1,0:T(8,128)}, f32[32,1024]{1,0:T(8,128)}, f32[32,1024]{1,0:T(8,1...) custom-call(bf16[128,1024]{1,0:T(8,128)(2,1)} %get-tuple-element.30., ...), custom_call_target="tpu_custom_call" | custom-call | tf_op jit(solution)/shard_map/pallas_call | solution.py:1071
